TPU v7x, 32 devices: a whole 2x2x4 slice. The times are simulated.
32 devices in a mesh: grp: 2 (over y), tm: 4 (over z), space: 4 (over x, core).
Axes of the slice: x: 2, y: 2, z: 4, core: 2. Of those that a mesh axis runs over, the one named last changes fastest.
Arguments:
- solutions: bfloat16 [128, 4, 2, 3, 256, 128], P(('grp', 'tm'), None, None, None, 'space'), parts along dimension 0, may hold values from -6 to 6
- eigvecs: bfloat16 [4, 2, 3, 256, 128], P('tm', None, None, 'space'), may hold values from -0.15625 to 0.15625
- sink_time: int32 [128, 1], P(('grp', 'tm')), parts along dimension 0, may hold values from 0 to 3; in each aligned block of 16 rows (0 to 15, 16 to 31, ...) at most 8 rows name the same one
Outputs:
- perambulator: bfloat16 [128, 4, 2, 128, 128], P(('grp', 'tm'), None, None, 'space'), parts along dimension 0
There are 2 independent parts, one for each index of `grp`. A program takes and returns all parts, laid end to end along the dimension named above; an argument that names none is the same for every part. Nothing has to cross between parts.
Inputs may be any that keep to these rules, and one draw needn't show every extreme that they name: `sink_time`: among the rows of one device (aligned blocks of 16 rows) no timeslice is named by more than 8 rows, a bound that some block reaches of them.
All inputs are finite; a program needn't handle non-finite values.
Results may differ from a plain program's by a relative error of at most 0.012.
Values may be sent and summed in bfloat16 or wider, within the bound.
No kernel may reach another device: no remote copies, remote signals or barrier semaphores. Data moves between devices by JAX's collectives and lax.ppermute only.
A program may use at most 128 MiB of HBM per device.

v0:
```python
import jax
import jax.numpy as jnp
from jax import lax
from jax.sharding import PartitionSpec as P


def combine(vector):
    joined = jnp.stack([vector, jnp.stack([-vector[1], vector[0]])])
    return joined.reshape(2, -1, vector.shape[-1])


def shards(solutions, eigvecs, sink_time):
    blocks = solutions.shape[0]
    spin_count = solutions.shape[1]
    columns = solutions.shape[-1]
    time_count = lax.axis_size("tm")
    per_peer = max(2, (2 * blocks + time_count - 1) // time_count)
    target_time = sink_time[:, 0]
    one_hot = (target_time[:, None] == jnp.arange(time_count, dtype=jnp.int32)[None, :]).astype(
        jnp.int32
    )
    earlier = jnp.cumsum(one_hot, axis=0) - one_hot
    position = jnp.sum(earlier * one_hot, axis=1)
    slot_index = target_time * per_peer + position
    outgoing = (
        jnp.zeros((time_count * per_peer,) + solutions.shape[1:], solutions.dtype)
        .at[slot_index]
        .set(solutions)
    )
    outgoing = outgoing.reshape((time_count, per_peer) + solutions.shape[1:])
    incoming = lax.all_to_all(outgoing, "tm", split_axis=0, concat_axis=0, tiled=True)
    right_matrix = incoming.reshape(time_count * per_peer, spin_count, -1, columns)
    left_matrix = combine(eigvecs[0])
    partial_terms = jnp.einsum(
        "oke,bskj->bsoej", left_matrix, right_matrix, preferred_element_type=jnp.float32
    )
    summed = lax.psum_scatter(
        partial_terms.astype(jnp.bfloat16), "space", scatter_dimension=3, tiled=True
    )
    summed = summed.reshape((time_count, per_peer) + summed.shape[1:])
    returned = lax.all_to_all(summed, "tm", split_axis=0, concat_axis=0, tiled=True)
    returned = returned.reshape((time_count * per_peer,) + returned.shape[2:])
    return returned[slot_index]


def solution(mesh):
    in_specs = (
        P(("grp", "tm"), None, None, None, "space", None),
        P("tm", None, None, "space", None),
        P(("grp", "tm"), None),
    )
    out_specs = P(("grp", "tm"), None, None, "space", None)
    return jax.shard_map(shards, mesh=mesh, in_specs=in_specs, out_specs=out_specs, check_vma=False)
```

profile of v0, /device:TPU:0, one launch (start us, length us, event | category | flops | bytes accessed | tf_op | source)
XLA Modules:
  0.0 480.4 jit_solution(17348396388431306449)
XLA Ops:
  6.5 0.7 fusion.2
  7.3 0.8 select_reduce_fusion
  8.1 0.7 fusion.3
  8.8 7.7 %broadcast_in_dim.2 = bf16[32,4,2,3,64,128]{5,4,3,2,1,0:T(8,128)(2,1)} broadcast(bf16[]{:T(256)} %constant.4.clone.1), dimensions={} | broadcast | bytes 12582914 | tf_op jit(solution)/shard_map/broadcast_in_dim | solution.py:26
  16.5 19.1 %scatter_fusion = bf16[32,4,2,3,64,128]{5,4,3,2,1,0:T(8,128)(2,1)} fusion(bf16[32,4,2,3,64,128]{5,4,3,2,1,0:T(8,128)(2,1)} %broadcast_in_dim.2, s32[16]{0:T(128)S(1)} %fusion.3, bf16[16,4,2,3,64,128]{5,4,3,2,1,0:T(8,128)(2,1)} %param.3), kind=kCustom, calls=%fused_computation.1 | custom fusion | bytes 18874432 | tf_op jit(solution)/shard_map/scatter | solution.py:28
  35.6 0.0 copy-start
  35.6 6.5 %all-to-all-start = ((bf16[4,8,4,2,3,64,128]{6,5,4,3,2,1,0:T(8,128)(2,1)}), bf16[4,8,4,2,3,64,128]{6,5,4,3,2,1,0:T(8,128)(2,1)}, u32[]{:S(2)}, u32[]{:S(2)}) async-start(bf16[4,8,4,2,3,64,128]{6,5,4,3,2,1,0:T(8,128)(2,1)} %bitcast.29), calls=%async_computation | async-start | bytes 25165824 | tf_op jit(solution)/shard_map/all_to_all | solution.py:31
  42.1 0.0 reduce-scatter.2.cloned.1.call-start
  42.1 0.0 copy-done
  42.2 274.6 %all-to-all-done = bf16[4,8,4,2,3,64,128]{6,5,4,3,2,1,0:T(8,128)(2,1)} async-done(((bf16[4,8,4,2,3,64,128]{6,5,4,3,2,1,0:T(8,128)(2,1)}), bf16[4,8,4,2,3,64,128]{6,5,4,3,2,1,0:T(8,128)(2,1)}, u32[]{:S(2)}, u32[]{:S(2)}) %all-to-all-start) | async-done | bytes 12582944 | tf_op jit(solution)/shard_map/all_to_all | solution.py:31
  316.8 12.3 %convert_bitcast_fusion = bf16[32,4,2,128,128]{3,4,2,1,0:T(8,128)(2,1)} fusion(bf16[32,4,384,128,1]{3,2,4,1,0:T(8,128)(2,1)} %bitcast.16, bf16[1,384,128]{2,1,0:T(8,128)(2,1)S(1)} %bitcast.33, bf16[1,384,128]{2,1,0:T(8,128)(2,1)S(1)} %bitcast.32), kind=kOutput, calls=%fused_computation.2 | convolution fusion | flops 3225812992 | bytes 21168128 | tf_op jit(solution)/shard_map/oke,bskj->bsoej/dot_general | solution.py:34
  329.1 14.6 %copy.7 = bf16[32,4,2,128,128]{4,0,2,1,3:T(8,128)(2,1)} copy(bf16[32,4,2,128,128]{3,4,2,1,0:T(8,128)(2,1)} %convert_bitcast_fusion) | data formatting | bytes 16777216 | tf_op jit(solution)/shard_map/convert_element_type | solution.py:38
  343.8 0.0 reduce-scatter.2.cloned.1.call-update
  343.8 71.0 %reduce-scatter.2.cloned.1.call-done = bf16[32,4,2,32,128]{4,0,2,1,3:T(8,128)(2,1)} async-done(((bf16[32,4,2,128,128]{4,0,2,1,3:T(8,128)(2,1)}), bf16[32,4,2,32,128]{4,0,2,1,3:T(8,128)(2,1)}) %reduce-scatter.2.cloned.1.call-update) | async-done | bytes 2097168 | tf_op jit(solution)/shard_map/reduce_scatter | solution.py:37
  414.8 4.3 copy.8
  419.1 4.6 all-to-all-start.1
  423.7 48.2 %all-to-all-done.1 = bf16[4,8,4,2,32,128]{5,4,3,2,1,0:T(8,128)(2,1)S(1)} async-done(((bf16[4,8,4,2,32,128]{5,4,3,2,1,0:T(8,128)(2,1)}), bf16[4,8,4,2,32,128]{5,4,3,2,1,0:T(8,128)(2,1)S(1)}, u32[]{:S(2)}, u32[]{:S(2)}) %all-to-all-start.1) | async-done | bytes 2097184 | tf_op jit(solution)/shard_map/all_to_all | solution.py:41
  471.9 1.6 gather_fusion
  (4 shorter events, 0.1 us)
Async XLA Ops:
  35.6 6.5 %copy-start = (bf16[1,2,3,64,128]{4,3,2,1,0:T(8,128)(2,1)S(1)}, bf16[1,2,3,64,128]{4,3,2,1,0:T(8,128)(2,1)}, u32[]{:S(2)}) copy-start(bf16[1,2,3,64,128]{4,3,2,1,0:T(8,128)(2,1)} %param.4) | copy-start | bytes 294916
  35.6 281.2 %all-to-all-start = ((bf16[4,8,4,2,3,64,128]{6,5,4,3,2,1,0:T(8,128)(2,1)}), bf16[4,8,4,2,3,64,128]{6,5,4,3,2,1,0:T(8,128)(2,1)}, u32[]{:S(2)}, u32[]{:S(2)}) async-start(bf16[4,8,4,2,3,64,128]{6,5,4,3,2,1,0:T(8,128)(2,1)} %bitcast.29), calls=%async_computation | async-start | bytes 25165824 | tf_op jit(solution)/shard_map/all_to_all | solution.py:31
  42.1 372.7 %reduce-scatter.2.cloned.1.call-start = ((), (), s32[]{:S(2)}) async-start(), calls=%async_computation.3 | async-start | bytes 10485760 | tf_op jit(solution)/shard_map/reduce_scatter | solution.py:37
  419.1 52.8 %all-to-all-start.1 = ((bf16[4,8,4,2,32,128]{5,4,3,2,1,0:T(8,128)(2,1)}), bf16[4,8,4,2,32,128]{5,4,3,2,1,0:T(8,128)(2,1)S(1)}, u32[]{:S(2)}, u32[]{:S(2)}) async-start(bf16[4,8,4,2,32,128]{5,4,3,2,1,0:T(8,128)(2,1)} %copy.8), calls=%async_computation.2 | async-start | bytes 4194304 | tf_op jit(solution)/shard_map/all_to_all | solution.py:41
Sparse Core Ops, SparseCore 0:
  343.9 70.8 reduce-scatter.1
where the time goes:
time: 481 us; the launch traced here: 480 us
  waiting for transfers between devices  394 us (82%)
  local copies, waits for them, and re-layouts  47.4 us (10%)
  between operations  13.4 us (3%)
  matrix products  12.3 us (3%)
  starting transfers between devices  11.1 us (2%)
    all_to_all x1, waiting for transfers between devices, shards(): lax.all_to_all(outgoing, 'tm', split_axis=0, concat_axis=0, tiled=True)  275 us
    reduce_scatter x1, waiting for transfers between devices, shards(): lax.psum_scatter(partial_terms.astype(jnp.bfloat16), 'space', scatter_dim...  71 us
    all_to_all x1, waiting for transfers between devices, shards(): lax.all_to_all(summed, 'tm', split_axis=0, concat_axis=0, tiled=True)  48.2 us
    scatter x1, local copies, waits for them, and re-layouts, shards(): outgoing = jnp.zeros((time_count * per_peer,) + solutions.shape[1:], solu...  19.1 us
    convert_element_type x1, local copies, waits for them, and re-layouts, shards(): partial_terms.astype(jnp.bfloat16)  14.6 us
    dot_general x1, matrix products, shards(): jnp.einsum('oke,bskj->bsoej', left_matrix, right_matrix, preferred_elemen...  12.3 us
  transfers between devices with their start and end apart: 3, of which 3 were waited for; matrix products, arithmetic and copies ran while one was open for 0% of the time, Pallas kernels for 0%

commit v1 on v0

v1 whole, which is shorter than its diff:
```python
import functools

import jax
import jax.numpy as jnp
from jax import lax
from jax.experimental import pallas as pl
from jax.experimental.pallas import tpu as pltpu
from jax.sharding import PartitionSpec as P

SMEM = pl.BlockSpec(memory_space=pltpu.SMEM)
VMEM = pl.BlockSpec(memory_space=pltpu.VMEM)
ANY = pl.BlockSpec(memory_space=pl.ANY)
HBM = pl.BlockSpec(memory_space=pltpu.HBM)
LITTLE = pl.CostEstimate(flops=1, bytes_accessed=1, transcendentals=0)
MUCH = pl.CostEstimate(flops=20_000_000_000, bytes_accessed=80_000_000, transcendentals=0)
PARAMS = pltpu.CompilerParams(vmem_limit_bytes=16 * 1024 * 1024)


def near(array):
    return pltpu.with_memory_space_constraint(array, pltpu.VMEM)


def far(array):
    return pltpu.with_memory_space_constraint(array, pltpu.HBM)


def in_pairs(count):
    return count & (count - 1) == 0


def peer(index, step, count):
    return index ^ step if in_pairs(count) else (index + step) % count


def apart(here, there, count):
    return here ^ there if in_pairs(count) else lax.rem(there - here + count, count)


def swap(array, axis, step, count):
    return lax.ppermute(array, axis, [(i, peer(i, step, count)) for i in range(count)])


def call(kernel, ins, outs, operands, cost=LITTLE, **more):
    specs, shapes = zip(*outs)
    return pl.pallas_call(
        kernel,
        in_specs=ins,
        out_specs=specs,
        out_shape=shapes,
        cost_estimate=cost,
        compiler_params=PARAMS,
        **more,
    )(*operands)


def load(steps, first, times_ref, place_ref, data_ref, order_ref, slot_ref, held_ref, sem):
    blocks = times_ref.shape[0]
    count = len(steps)
    here = place_ref[0]

    def slot_of(i):
        step = apart(times_ref[i], here, count)
        slot = jnp.int32(0)
        for at, value in enumerate(steps):
            slot = jnp.where(step == value, at, slot)
        return slot

    def count_early(i, total):
        return total + (slot_of(i) < first).astype(jnp.int32)

    early = lax.fori_loop(0, blocks, count_early, jnp.int32(0))

    def copy(block, where):
        return pltpu.make_async_copy(data_ref.at[block], held_ref.at[where], sem.at[where])

    def place(i, at):
        low, high = at
        slot = slot_of(i)
        is_early = slot < first
        where = jnp.where(is_early, low, high)
        order_ref[where] = i
        slot_ref[where] = slot
        copy(i, where).start()
        one = is_early.astype(jnp.int32)
        return low + one, high + 1 - one

    lax.fori_loop(0, blocks, place, (jnp.int32(0), early))
    for where in range(blocks):
        copy(order_ref[where], where).wait()


def join(*refs):
    for at, ref in enumerate(refs[:-1]):
        refs[-1][at] = ref[...]


def project_sites(chips, width, size, vectors, place_ref, slot_ref, *refs):
    vector_refs, held_ref = refs[:vectors], refs[vectors]
    outs, left_ref = refs[vectors + 1 : -1], refs[-1]
    spins, columns = held_ref.shape[1], held_ref.shape[-1]
    rows = 2 * width
    chip, core = place_ref[1], place_ref[2]
    for slot, ref in enumerate(vector_refs):
        real, imag = ref[0], ref[1]
        for part, pair in enumerate(((real, imag), (-imag, real))):
            turned = jnp.concatenate(pair, axis=0).T
            for to_chip in range(chips):
                for to_core in range(2):
                    stays = (core == to_core).astype(jnp.int32)
                    at = ((stays * chips + apart(chip, to_chip, chips)) * 2 + part) * width
                    start = (to_chip * 2 + to_core) * width
                    left_ref[slot, pl.ds(pl.multiple_of(at, width), width), :] = turned[
                        start : start + width
                    ]
    for piece in range(len(outs) // 2):
        give_ref, keep_ref = outs[2 * piece : 2 * piece + 2]
        for i in range(size):
            left = left_ref[slot_ref[piece * size + i]]
            for spin in range(0, spins, 2):
                right = jnp.concatenate(
                    [
                        held_ref[piece * size + i, s].reshape(-1, columns)
                        for s in range(spin, spin + 2)
                    ],
                    axis=1,
                )
                result = jnp.dot(left, right, preferred_element_type=jnp.float32)
                result = result.astype(give_ref.dtype)
                for s in range(2):
                    side = result[:, s * columns : (s + 1) * columns]
                    for ref, part in ((give_ref, side[: chips * rows]), (keep_ref, side[chips * rows :])):
                        ref[:, i, spin + s] = part.reshape(chips, rows, columns)


def project_chip(chips, width, start, size, vectors, place_ref, order_ref, slot_ref, *refs):
    if vectors:
        vector_refs, others_ref = refs[:vectors], refs[vectors]
        held_ref, other_ref = refs[vectors + 1 : vectors + 3]
        outs = refs[vectors + 3 : -2]
        left_ref = outs[chips]
    else:
        left_ref, held_ref, other_ref = refs[:3]
        outs = refs[3:-2]
    came_ref, sem = refs[-2:]
    spins, columns = held_ref.shape[1], held_ref.shape[-1]
    rows = 2 * width

    def copy(i):
        return pltpu.make_async_copy(
            other_ref.at[order_ref[start + i]], came_ref.at[i], sem.at[i]
        )

    for i in range(size):
        copy(i).start()
    chip, core = place_ref[1], place_ref[2]
    for slot in range(vectors):
        real, imag = (
            jnp.concatenate([vector_refs[slot][part], others_ref[slot, part]], axis=0)
            for part in range(2)
        )
        for part, pair in enumerate(((real, imag), (-imag, real))):
            turned = jnp.concatenate(pair, axis=0).T
            for to_chip in range(chips):
                at = (apart(chip, to_chip, chips) * 2 + part) * width
                low = to_chip * 2 * width
                left_ref[slot, pl.ds(pl.multiple_of(at, width), width), :] = jnp.where(
                    core == 0,
                    turned[low : low + width],
                    turned[low + width : low + 2 * width],
                )
    for i in range(size):
        left = left_ref[slot_ref[start + i]]
        copy(i).wait()
        for spin in range(0, spins, 2):
            right = jnp.concatenate(
                [
                    jnp.concatenate(
                        [
                            ref[at, s, part]
                            for part in range(2)
                            for ref, at in ((held_ref, start + i), (came_ref, i))
                        ],
                        axis=0,
                    )
                    for s in range(spin, spin + 2)
                ],
                axis=1,
            )
            result = jnp.dot(left, right, preferred_element_type=jnp.float32)
            result = result.astype(outs[0].dtype)
            for s in range(2):
                for step in range(chips):
                    outs[step][i, spin + s] = result[
                        step * rows : (step + 1) * rows, s * columns : (s + 1) * columns
                    ]


def finish(start, size, terms, order_ref, *refs):
    out_ref, stage_ref, sem = refs[-3:]

    def copy(i):
        return pltpu.make_async_copy(stage_ref.at[i], out_ref.at[order_ref[start + i]], sem.at[i])

    for i in range(size):
        total = None
        for ref in refs[:terms]:
            term = ref[i] if len(ref.shape) == 4 else ref[0, i]
            term = term.astype(jnp.float32)
            total = term if total is None else total + term
        stage_ref[i] = total.reshape(stage_ref.shape[1:]).astype(stage_ref.dtype)
        copy(i).start()
    for i in range(size):
        copy(i).wait()


def shards(solutions, eigvecs, sink_time):
    blocks, spins, _, colours, sites, columns = solutions.shape
    times = lax.axis_size("tm")
    members = lax.axis_size("space")
    chips = members // 2
    width = eigvecs.shape[-1] // members
    rows = 2 * width
    depth = 2 * colours * sites
    kind = solutions.dtype
    at = lax.axis_index("space")
    place = jnp.stack([lax.axis_index("tm"), at // 2, at % 2]).astype(jnp.int32)
    cores = [(i, i ^ 1) for i in range(members)]

    most = max(2, (2 * blocks + times - 1) // times)
    half = blocks // 2
    late = half // most
    first = times - late
    steps = [0] + list(range(1, times, 2)) + list(range(2, times, 2))

    own = eigvecs[0].reshape(2, colours * sites, -1)
    data = solutions.reshape(blocks, spins, 2, colours * sites, columns)
    other_data = lax.ppermute(data, "space", cores)
    vectors = [own]
    for slot, step in enumerate(steps[1:], 1):
        if slot >= first and in_pairs(times) and steps.index(step ^ 1) < first:
            vectors.append(swap(vectors[steps.index(step ^ 1)], "tm", 1, times))
        else:
            vectors.append(swap(own, "tm", step, times))

    numbers = jax.ShapeDtypeStruct((blocks,), jnp.int32)
    order, slots, held = call(
        functools.partial(load, steps, first),
        [SMEM, SMEM, HBM],
        [(SMEM, numbers), (SMEM, numbers), (VMEM, pltpu.VMEM(data.shape, kind))],
        [sink_time[:, 0], place, far(data)],
        scratch_shapes=[pltpu.SemaphoreType.DMA((blocks,))],
    )
    held = near(held)

    size = half // 2
    piece = pltpu.VMEM((chips, size, spins, rows, columns), kind)
    pieces = call(
        functools.partial(project_sites, chips, width, size, first),
        [SMEM, SMEM] + [VMEM] * (first + 1),
        [(VMEM, piece)] * 4,
        [place, slots, *[near(v) for v in vectors[:first]], held],
        scratch_shapes=[pltpu.VMEM((first, 4 * chips * width, depth), kind)],
    )
    terms = []
    for give, keep in (pieces[:2], pieces[2:]):
        got = lax.ppermute(give, "space", cores)
        sums = [keep, got]
        for step in range(1, chips):
            sent = (keep[step].astype(jnp.float32) + got[step].astype(jnp.float32)).astype(kind)
            sums.append(send(sent, step, members))
        terms.append(sums)

    vectors = [near(v) for v in vectors]
    (joined,) = call(
        join, [VMEM] * times, [(VMEM, pltpu.VMEM((times, *own.shape), kind))], vectors
    )
    others = near(lax.ppermute(joined, "space", cores))

    piece = pltpu.VMEM((size, spins, rows, columns), kind)
    lefts = (VMEM, pltpu.VMEM((times, chips * rows, 2 * depth), kind))
    left = None
    for start in (half, half + size):
        results = call(
            functools.partial(
                project_chip, chips, width, start, size, times if left is None else 0
            ),
            [SMEM] * 3 + [VMEM] * (times + 2 if left is None else 2) + [HBM],
            [(VMEM, piece)] * chips + ([lefts] if left is None else []),
            [place, order, slots, *([*vectors, others] if left is None else [left]), held, far(other_data)],
            scratch_shapes=[
                pltpu.VMEM((size, *data.shape[1:]), kind),
                pltpu.SemaphoreType.DMA((size,)),
            ],
        )
        if left is None:
            left = near(results[chips])
        terms.append(
            [results[0]] + [send(results[step], step, members) for step in range(1, chips)]
        )

    result = None
    for at, sums in enumerate(terms):
        operands = [order, *[near(a) for a in sums]]
        ins = [SMEM] + [VMEM] * len(sums)
        aliases = {}
        if result is not None:
            aliases = {len(operands): 0}
            operands.append(result)
            ins.append(HBM)
        (result,) = call(
            functools.partial(finish, at * size, size, len(sums)),
            ins,
            [(HBM, jax.ShapeDtypeStruct((blocks, spins, 2, width, columns), kind))],
            operands,
            MUCH,
            scratch_shapes=[
                pltpu.VMEM((size, spins, 2, width, columns), kind),
                pltpu.SemaphoreType.DMA((size,)),
            ],
            input_output_aliases=aliases,
        )
    return result


def send(array, step, members):
    route = [(i, peer(i // 2, step, members // 2) * 2 + i % 2) for i in range(members)]
    return lax.ppermute(array, "space", route)


def solution(mesh):
    in_specs = (
        P(("grp", "tm"), None, None, None, "space", None),
        P("tm", None, None, "space", None),
        P(("grp", "tm"), None),
    )
    out_specs = P(("grp", "tm"), None, None, "space", None)
    return jax.shard_map(shards, mesh=mesh, in_specs=in_specs, out_specs=out_specs, check_vma=False)
```

time: 481 us -> 42.6 us (0.09)
  waiting for transfers between devices: 394 us -> 12.1 us
  local copies, waits for them, and re-layouts: 47.4 us -> 0.66 us
  Pallas kernels: 0 us -> 17.2 us
  between operations: 13.4 us -> 0.13 us
  matrix products: 12.3 us -> 0 us
    all_to_all x2 -> x0, waiting for transfers between devices: 323 us -> none  [the longest x1 275 us: shards(): lax.all_to_all(outgoing, 'tm', split_axis=0, concat_axis=0, tiled=True)]
    reduce_scatter x1 -> x0, waiting for transfers between devices: 71 us -> none  [shards(): lax.psum_scatter(partial_terms.astype(jnp.bfloat16), 'space', scatter_dim...]
    scatter x1 -> x0, local copies, waits for them, and re-layouts: 19.1 us -> none  [shards(): outgoing = jnp.zeros((time_count * per_peer,) + solutions.shape[1:], solu...]
    pallas_call x0 -> x9, Pallas kernels: none -> 17.2 us  [call(): pl.pallas_call(kernel, in_specs=ins, out_specs=specs, out_shape=shapes, c...]
    convert_element_type x1 -> x0, local copies, waits for them, and re-layouts: 14.6 us -> none  [shards(): partial_terms.astype(jnp.bfloat16)]
    dot_general x1 -> x0, matrix products: 12.3 us -> none  [shards(): jnp.einsum('oke,bskj->bsoej', left_matrix, right_matrix, preferred_elemen...]
    ppermute x0 -> x11, waiting for transfers between devices: none -> 12.1 us  [the longest x4 9.06 us: send(): return lax.ppermute(array, 'space', route)]
    ppermute x0 -> x11, starting transfers between devices: none -> 12.1 us  [the longest x3 5.72 us: swap(): lax.ppermute(array, axis, [(i, peer(i, step, count)) for i in range(count)])]
  transfers between devices with their start and end apart: 3 -> 11, of which waited for: 3 -> 6; matrix products, arithmetic and copies ran while one was open for 0% -> 1% of each run, Pallas kernels for 0% -> 37%
where the time goes in v1:
time: 42.6 us; the launch traced here: 42.4 us
  Pallas kernels  17.2 us (40%)
  starting transfers between devices  12.1 us (28%)
  waiting for transfers between devices  12.1 us (28%)
  local copies, waits for them, and re-layouts  0.66 us (2%)
    pallas_call x9, Pallas kernels, call(): pl.pallas_call(kernel, in_specs=ins, out_specs=specs, out_shape=shapes, c...  17.2 us
    ppermute x4, waiting for transfers between devices, send(): return lax.ppermute(array, 'space', route)  9.06 us
    ppermute x3, starting transfers between devices, swap(): lax.ppermute(array, axis, [(i, peer(i, step, count)) for i in range(count)])  5.72 us
    ppermute x4, starting transfers between devices, send(): return lax.ppermute(array, 'space', route)  5.27 us
    ppermute x3, waiting for transfers between devices, swap(): lax.ppermute(array, axis, [(i, peer(i, step, count)) for i in range(count)])  2.26 us
  transfers between devices with their start and end apart: 11, of which 6 were waited for; matrix products, arithmetic and copies ran while one was open for 1% of the time, Pallas kernels for 37%

profile of v1, /device:TPU:0, one launch (start us, length us, event | category | flops | bytes accessed | tf_op | source)
XLA Modules:
  0.0 42.4 jit_solution(4506838038237576062)
XLA Ops:
  0.0 0.5 %collective-permute-start.4 = (bf16[16,4,2,192,128]{4,3,2,1,0:T(8,128)(2,1)}, bf16[16,4,2,192,128]{4,3,2,1,0:T(8,128)(2,1)}, u32[]{:S(2)}, u32[]{:S(2)}) collective-permute-start(bf16[16,4,2,192,128]{4,3,2,1,0:T(8,128)(2,1)} %bitcast.16), channel_id=1, source_target_pairs={{0,1},{1,0},{2,3},{3,2},{4,5},{5,4},{6,7},{7,6},{8,9},{9,8},{10,11... | collective-permute-start | bytes 18874376 | tf_op jit(solution)/shard_map/ppermute | solution.py:237
  0.5 2.6 %collective-permute-start = (bf16[2,192,128]{2,1,0:T(8,128)(2,1)}, bf16[2,192,128]{2,1,0:T(8,128)(2,1)S(1)}, u32[]{:S(2)}, u32[]{:S(2)}) collective-permute-start(bf16[2,192,128]{2,1,0:T(8,128)(2,1)} %bitcast.10), channel_id=1, source_target_pairs={{0,4},{4,0},{8,12},{12,8},{1,5},{5,1},{9,13},{13,9},{2,6},{6,2},{1... | collective-permute-start | bytes 294920 | tf_op jit(solution)/shard_map/ppermute | solution.py:40
  3.1 2.5 %collective-permute-start.1 = (bf16[2,192,128]{2,1,0:T(8,128)(2,1)}, bf16[2,192,128]{2,1,0:T(8,128)(2,1)S(1)}, u32[]{:S(2)}, u32[]{:S(2)}) collective-permute-start(bf16[2,192,128]{2,1,0:T(8,128)(2,1)} %bitcast.11), channel_id=1, source_target_pairs={{0,12},{4,8},{8,4},{12,0},{1,13},{5,9},{9,5},{13,1},{2,14},{6,10},... | collective-permute-start | bytes 294920 | tf_op jit(solution)/shard_map/ppermute | solution.py:40
  5.6 0.1 pad_add_fusion.place_ref
  5.6 0.7 %copy-done.1 = s32[16,1]{0,1:T(1,128)S(1)} copy-done((s32[16,1]{0,1:T(1,128)S(1)}, s32[16,1]{0,1:T(1,128)}, u32[]{:S(2)}) %copy-start.1) | copy-done | bytes 88
  6.3 4.3 %shard_map.37 = (s32[16]{0:T(128)S(1)}, s32[16]{0:T(128)S(1)}, bf16[16,4,2,192,128]{4,3,2,1,0:T(8,128)(2,1)S(1)}) custom-call(s32[16]{0:T(128)S(1)} %bitcast.15, s32[3]{0:T(128)S(1)} %pad_add_fusion.place_ref, bf16[16,4,2,192,128]{4,3,2,1,0:T(8,128)(2,1)} %bitcast.17), custom_call_target="tpu_custom_call" | custom-call | flops 1 | bytes 1 | tf_op jit(solution)/shard_map/pallas_call | solution.py:45
  10.6 0.0 collective-permute-done.refs_1_
  10.6 0.5 %collective-permute-done.1.refs_2_ = bf16[2,192,128]{2,1,0:T(8,128)(2,1)S(1)} collective-permute-done((bf16[2,192,128]{2,1,0:T(8,128)(2,1)}, bf16[2,192,128]{2,1,0:T(8,128)(2,1)S(1)}, u32[]{:S(2)}, u32[]{:S(2)}) %collective-permute-start.1) | collective-permute-done | bytes 98336 | tf_op jit(solution)/shard_map/ppermute | solution.py:40
  11.1 2.0 %shard_map.41 = (bf16[2,4,4,64,128]{4,3,2,1,0:T(8,128)(2,1)S(1)}, bf16[2,4,4,64,128]{4,3,2,1,0:T(8,128)(2,1)S(1)}, bf16[2,4,4,64,128]{4,3,2,1,0:T(8,128)(2,1)S(1)}, bf16[2,4,4,64,128]{4,3,2,1,0:T(8,128)(2,1)S(1)}) custom-call(s32[3]{0:T(128)S(1)} %pad_add_fusion.place_ref, s32[16]{0:T(128)S(1)} %get-tuple-element.18.slot_ref, ...), custom_call_target="tpu_custom_call" | custom-call | flops 1 | bytes 1 | tf_op jit(solution)/shard_map/pallas_call | solution.py:45
  13.1 0.1 collective-permute-start.9
  13.2 0.5 %collective-permute-start.7 = (bf16[2,4,4,64,128]{4,3,2,1,0:T(8,128)(2,1)S(1)}, bf16[2,4,4,64,128]{4,3,2,1,0:T(8,128)(2,1)S(1)}, u32[]{:S(2)}, u32[]{:S(2)}) collective-permute-start(bf16[2,4,4,64,128]{4,3,2,1,0:T(8,128)(2,1)S(1)} %get-tuple-element.26), channel_id=1, source_target_pairs={{0,1},{1,0},{2,3},{3,2},{4,5},{5,4},{6,7},{7,6},{8,9},{9,8},{10,11... | collective-permute-start | bytes 1572872 | tf_op jit(solution)/shard_map/ppermute | solution.py:266
  13.7 0.6 %collective-permute-start.2 = (bf16[2,192,128]{2,1,0:T(8,128)(2,1)S(1)}, bf16[2,192,128]{2,1,0:T(8,128)(2,1)S(1)}, u32[]{:S(2)}, u32[]{:S(2)}) collective-permute-start(bf16[2,192,128]{2,1,0:T(8,128)(2,1)S(1)} %collective-permute-done.1.refs_2_), channel_id=1, source_target_pairs={{0,4},{4,0},{8,12},{12,8},{1,5},{5,1},{9,13},{13,9},{2,6},{6,2},{1... | collective-permute-start | bytes 294920 | tf_op jit(solution)/shard_map/ppermute | solution.py:40
  14.3 0.8 %collective-permute-done.9.refs_1_ = bf16[2,4,4,64,128]{4,3,2,1,0:T(8,128)(2,1)S(1)} collective-permute-done((bf16[2,4,4,64,128]{4,3,2,1,0:T(8,128)(2,1)S(1)}, bf16[2,4,4,64,128]{4,3,2,1,0:T(8,128)(2,1)S(1)}, u32[]{:S(2)}, u32[]{:S(2)}) %collective-permute-start.9) | collective-permute-done | bytes 524320 | tf_op jit(solution)/shard_map/ppermute | solution.py:266
  15.1 0.1 fusion.1
  15.2 1.6 %collective-permute-start.10 = (bf16[4,4,64,128]{3,2,1,0:T(8,128)(2,1)S(1)}, bf16[4,4,64,128]{3,2,1,0:T(8,128)(2,1)S(1)}, u32[]{:S(2)}, u32[]{:S(2)}) collective-permute-start(bf16[4,4,64,128]{3,2,1,0:T(8,128)(2,1)S(1)} %fusion.1), channel_id=1, source_target_pairs={{0,2},{1,3},{2,0},{3,1},{4,6},{5,7},{6,4},{7,5},{8,10},{9,11},{10,... | collective-permute-start | bytes 786440 | tf_op jit(solution)/shard_map/ppermute | solution.py:327
  16.7 1.7 %collective-permute-done.2.refs_3_ = bf16[2,192,128]{2,1,0:T(8,128)(2,1)S(1)} collective-permute-done((bf16[2,192,128]{2,1,0:T(8,128)(2,1)S(1)}, bf16[2,192,128]{2,1,0:T(8,128)(2,1)S(1)}, u32[]{:S(2)}, u32[]{:S(2)}) %collective-permute-start.2) | collective-permute-done | bytes 98336 | tf_op jit(solution)/shard_map/ppermute | solution.py:40
  18.5 0.1 collective-permute-start.3
  18.6 0.0 collective-permute-done.7.refs_1_
  18.6 0.1 fusion
  18.7 1.6 %collective-permute-start.8 = (bf16[4,4,64,128]{3,2,1,0:T(8,128)(2,1)S(1)}, bf16[4,4,64,128]{3,2,1,0:T(8,128)(2,1)S(1)}, u32[]{:S(2)}, u32[]{:S(2)}) collective-permute-start(bf16[4,4,64,128]{3,2,1,0:T(8,128)(2,1)S(1)} %fusion), channel_id=1, source_target_pairs={{0,2},{1,3},{2,0},{3,1},{4,6},{5,7},{6,4},{7,5},{8,10},{9,11},{10,... | collective-permute-start | bytes 786440 | tf_op jit(solution)/shard_map/ppermute | solution.py:327
  20.2 4.2 %collective-permute-done.10.refs_2_ = bf16[4,4,64,128]{3,2,1,0:T(8,128)(2,1)S(1)} collective-permute-done((bf16[4,4,64,128]{3,2,1,0:T(8,128)(2,1)S(1)}, bf16[4,4,64,128]{3,2,1,0:T(8,128)(2,1)S(1)}, u32[]{:S(2)}, u32[]{:S(2)}) %collective-permute-start.10) | collective-permute-done | bytes 262176 | tf_op jit(solution)/shard_map/ppermute | solution.py:327
  24.4 1.3 %shard_map.42.refs_3_ = bf16[16,4,2,32,128]{4,3,2,1,0:T(8,128)(2,1)} custom-call(s32[16]{0:T(128)S(1)} %get-tuple-element.17.order_ref, bf16[2,4,4,64,128]{4,3,2,1,0:T(8,128)(2,1)S(1)} %get-tuple-element.27.refs_0_, bf16[2,4,4,64,128]{4,3,2,1,0:T(8,128)(2,1)S(1)} %collective-permute-done.9.refs_1_, bf16[4,4,64,128]{3,2,1,0:T(8,128)(2,1)S(1)} %collective-permute-done.10.refs_2_), custom_call_target="tpu_custom_call" | custom-call | flops 20000000000 | bytes 80000000 | tf_op jit(solution)/shard_map/pallas_call | solution.py:45
  25.7 0.0 collective-permute-done.4.refs_6_.refs_2_
  25.7 3.0 %shard_map.39 = (bf16[4,4,64,128]{3,2,1,0:T(8,128)(2,1)S(1)}, bf16[4,4,64,128]{3,2,1,0:T(8,128)(2,1)S(1)}, bf16[4,128,768]{2,1,0:T(8,128)(2,1)S(1)}) custom-call(s32[3]{0:T(128)S(1)} %pad_add_fusion.place_ref, s32[16]{0:T(128)S(1)} %get-tuple-element.17.order_ref, s32[16]{0:T(128)S(1)} %get-tuple-element.18.slot_ref, bf16[2,192,128]{2,1,0:T(8,128)(2,1)S(1)} %bitcast.14, ...), custom_call_target="tpu_custom_call" | custom-call | flops 1 | bytes 1 | tf_op jit(solution)/shard_map/pallas_call | solution.py:45
  28.7 1.6 %collective-permute-start.6 = (bf16[4,4,64,128]{3,2,1,0:T(8,128)(2,1)S(1)}, bf16[4,4,64,128]{3,2,1,0:T(8,128)(2,1)S(1)}, u32[]{:S(2)}, u32[]{:S(2)}) collective-permute-start(bf16[4,4,64,128]{3,2,1,0:T(8,128)(2,1)S(1)} %get-tuple-element.24), channel_id=1, source_target_pairs={{0,2},{1,3},{2,0},{3,1},{4,6},{5,7},{6,4},{7,5},{8,10},{9,11},{10,... | collective-permute-start | bytes 786440 | tf_op jit(solution)/shard_map/ppermute | solution.py:327
  30.3 1.3 %shard_map.43.refs_2_ = bf16[16,4,2,32,128]{4,3,2,1,0:T(8,128)(2,1)} custom-call(s32[16]{0:T(128)S(1)} %get-tuple-element.17.order_ref, bf16[2,4,4,64,128]{4,3,2,1,0:T(8,128)(2,1)S(1)} %get-tuple-element.25.refs_0_, bf16[2,4,4,64,128]{4,3,2,1,0:T(8,128)(2,1)S(1)} %collective-permute-done.7.refs_1_, ...), custom_call_target="tpu_custom_call", output_to_operand_aliasing={{}: (4, {})} | custom-call | flops 20000000000 | bytes 80000000 | tf_op jit(solution)/shard_map/pallas_call | solution.py:45
  31.6 2.7 %shard_map.40 = (bf16[4,4,64,128]{3,2,1,0:T(8,128)(2,1)S(1)}, bf16[4,4,64,128]{3,2,1,0:T(8,128)(2,1)S(1)}) custom-call(s32[3]{0:T(128)S(1)} %pad_add_fusion.place_ref, s32[16]{0:T(128)S(1)} %get-tuple-element.17.order_ref, s32[16]{0:T(128)S(1)} %get-tuple-element.18.slot_ref, bf16[4,128,768]{2,1,0:T(8,128)(2,1)S(1)} %get-tuple-element.20.refs_0_, ...), custom_call_target="tpu_custom_call" | custom-call | flops 1 | bytes 1 | tf_op jit(solution)/shard_map/pallas_call | solution.py:45
  34.3 0.6 %collective-permute-start.5 = (bf16[4,4,64,128]{3,2,1,0:T(8,128)(2,1)S(1)}, bf16[4,4,64,128]{3,2,1,0:T(8,128)(2,1)S(1)}, u32[]{:S(2)}, u32[]{:S(2)}) collective-permute-start(bf16[4,4,64,128]{3,2,1,0:T(8,128)(2,1)S(1)} %get-tuple-element.22), channel_id=1, source_target_pairs={{0,2},{1,3},{2,0},{3,1},{4,6},{5,7},{6,4},{7,5},{8,10},{9,11},{10,... | collective-permute-start | bytes 786440 | tf_op jit(solution)/shard_map/ppermute | solution.py:327
  34.9 0.8 %collective-permute-done.6.refs_1_ = bf16[4,4,64,128]{3,2,1,0:T(8,128)(2,1)S(1)} collective-permute-done((bf16[4,4,64,128]{3,2,1,0:T(8,128)(2,1)S(1)}, bf16[4,4,64,128]{3,2,1,0:T(8,128)(2,1)S(1)}, u32[]{:S(2)}, u32[]{:S(2)}) %collective-permute-start.6) | collective-permute-done | bytes 262176 | tf_op jit(solution)/shard_map/ppermute | solution.py:327
  35.7 1.3 %shard_map.44.refs_2_ = bf16[16,4,2,32,128]{4,3,2,1,0:T(8,128)(2,1)} custom-call(s32[16]{0:T(128)S(1)} %get-tuple-element.17.order_ref, bf16[4,4,64,128]{3,2,1,0:T(8,128)(2,1)S(1)} %get-tuple-element.23.refs_0_, bf16[4,4,64,128]{3,2,1,0:T(8,128)(2,1)S(1)} %collective-permute-done.6.refs_1_, ...), custom_call_target="tpu_custom_call", output_to_operand_aliasing={{}: (3, {})} | custom-call | flops 20000000000 | bytes 80000000 | tf_op jit(solution)/shard_map/pallas_call | solution.py:45
  37.0 4.1 %collective-permute-done.5.refs_1_ = bf16[4,4,64,128]{3,2,1,0:T(8,128)(2,1)S(1)} collective-permute-done((bf16[4,4,64,128]{3,2,1,0:T(8,128)(2,1)S(1)}, bf16[4,4,64,128]{3,2,1,0:T(8,128)(2,1)S(1)}, u32[]{:S(2)}, u32[]{:S(2)}) %collective-permute-start.5) | collective-permute-done | bytes 262176 | tf_op jit(solution)/shard_map/ppermute | solution.py:327
  41.1 1.3 %shard_map.45 = bf16[16,4,2,32,128]{4,3,2,1,0:T(8,128)(2,1)} custom-call(s32[16]{0:T(128)S(1)} %get-tuple-element.17.order_ref, bf16[4,4,64,128]{3,2,1,0:T(8,128)(2,1)S(1)} %get-tuple-element.21.refs_0_, bf16[4,4,64,128]{3,2,1,0:T(8,128)(2,1)S(1)} %collective-permute-done.5.refs_1_, ...), custom_call_target="tpu_custom_call", output_to_operand_aliasing={{}: (3, {})} | custom-call | flops 20000000000 | bytes 80000000 | tf_op jit(solution)/shard_map/pallas_call | solution.py:45
  (6 shorter events, 0.0 us)
Async XLA Ops:
  0.0 11.1 %copy-start = (bf16[1,2,3,64,128]{4,3,2,1,0:T(8,128)(2,1)S(1)}, bf16[1,2,3,64,128]{4,3,2,1,0:T(8,128)(2,1)}, u32[]{:S(2)}) copy-start(bf16[1,2,3,64,128]{4,3,2,1,0:T(8,128)(2,1)} %param.4) | copy-start | bytes 294916
  0.0 25.7 %collective-permute-start.4 = (bf16[16,4,2,192,128]{4,3,2,1,0:T(8,128)(2,1)}, bf16[16,4,2,192,128]{4,3,2,1,0:T(8,128)(2,1)}, u32[]{:S(2)}, u32[]{:S(2)}) collective-permute-start(bf16[16,4,2,192,128]{4,3,2,1,0:T(8,128)(2,1)} %bitcast.16), channel_id=1, source_target_pairs={{0,1},{1,0},{2,3},{3,2},{4,5},{5,4},{6,7},{7,6},{8,9},{9,8},{10,11... | collective-permute-start | bytes 18874376 | tf_op jit(solution)/shard_map/ppermute | solution.py:237
  0.5 10.1 %collective-permute-start = (bf16[2,192,128]{2,1,0:T(8,128)(2,1)}, bf16[2,192,128]{2,1,0:T(8,128)(2,1)S(1)}, u32[]{:S(2)}, u32[]{:S(2)}) collective-permute-start(bf16[2,192,128]{2,1,0:T(8,128)(2,1)} %bitcast.10), channel_id=1, source_target_pairs={{0,4},{4,0},{8,12},{12,8},{1,5},{5,1},{9,13},{13,9},{2,6},{6,2},{1... | collective-permute-start | bytes 294920 | tf_op jit(solution)/shard_map/ppermute | solution.py:40
  3.1 8.0 %collective-permute-start.1 = (bf16[2,192,128]{2,1,0:T(8,128)(2,1)}, bf16[2,192,128]{2,1,0:T(8,128)(2,1)S(1)}, u32[]{:S(2)}, u32[]{:S(2)}) collective-permute-start(bf16[2,192,128]{2,1,0:T(8,128)(2,1)} %bitcast.11), channel_id=1, source_target_pairs={{0,12},{4,8},{8,4},{12,0},{1,13},{5,9},{9,5},{13,1},{2,14},{6,10},... | collective-permute-start | bytes 294920 | tf_op jit(solution)/shard_map/ppermute | solution.py:40
  5.6 0.7 %copy-start.1 = (s32[16,1]{0,1:T(1,128)S(1)}, s32[16,1]{0,1:T(1,128)}, u32[]{:S(2)}) copy-start(s32[16,1]{0,1:T(1,128)} %param.5) | copy-start | bytes 196
  13.1 2.0 %collective-permute-start.9 = (bf16[2,4,4,64,128]{4,3,2,1,0:T(8,128)(2,1)S(1)}, bf16[2,4,4,64,128]{4,3,2,1,0:T(8,128)(2,1)S(1)}, u32[]{:S(2)}, u32[]{:S(2)}) collective-permute-start(bf16[2,4,4,64,128]{4,3,2,1,0:T(8,128)(2,1)S(1)} %get-tuple-element.28), channel_id=1, source_target_pairs={{0,1},{1,0},{2,3},{3,2},{4,5},{5,4},{6,7},{7,6},{8,9},{9,8},{10,11... | collective-permute-start | bytes 1572872 | tf_op jit(solution)/shard_map/ppermute | solution.py:266
  13.2 5.4 %collective-permute-start.7 = (bf16[2,4,4,64,128]{4,3,2,1,0:T(8,128)(2,1)S(1)}, bf16[2,4,4,64,128]{4,3,2,1,0:T(8,128)(2,1)S(1)}, u32[]{:S(2)}, u32[]{:S(2)}) collective-permute-start(bf16[2,4,4,64,128]{4,3,2,1,0:T(8,128)(2,1)S(1)} %get-tuple-element.26), channel_id=1, source_target_pairs={{0,1},{1,0},{2,3},{3,2},{4,5},{5,4},{6,7},{7,6},{8,9},{9,8},{10,11... | collective-permute-start | bytes 1572872 | tf_op jit(solution)/shard_map/ppermute | solution.py:266
  13.7 4.8 %collective-permute-start.2 = (bf16[2,192,128]{2,1,0:T(8,128)(2,1)S(1)}, bf16[2,192,128]{2,1,0:T(8,128)(2,1)S(1)}, u32[]{:S(2)}, u32[]{:S(2)}) collective-permute-start(bf16[2,192,128]{2,1,0:T(8,128)(2,1)S(1)} %collective-permute-done.1.refs_2_), channel_id=1, source_target_pairs={{0,4},{4,0},{8,12},{12,8},{1,5},{5,1},{9,13},{13,9},{2,6},{6,2},{1... | collective-permute-start | bytes 294920 | tf_op jit(solution)/shard_map/ppermute | solution.py:40
  15.2 9.2 %collective-permute-start.10 = (bf16[4,4,64,128]{3,2,1,0:T(8,128)(2,1)S(1)}, bf16[4,4,64,128]{3,2,1,0:T(8,128)(2,1)S(1)}, u32[]{:S(2)}, u32[]{:S(2)}) collective-permute-start(bf16[4,4,64,128]{3,2,1,0:T(8,128)(2,1)S(1)} %fusion.1), channel_id=1, source_target_pairs={{0,2},{1,3},{2,0},{3,1},{4,6},{5,7},{6,4},{7,5},{8,10},{9,11},{10,... | collective-permute-start | bytes 786440 | tf_op jit(solution)/shard_map/ppermute | solution.py:327
  18.5 7.2 %collective-permute-start.3 = (bf16[4,2,192,128]{3,2,1,0:T(8,128)(2,1)S(1)}, bf16[4,2,192,128]{3,2,1,0:T(8,128)(2,1)S(1)}, u32[]{:S(2)}, u32[]{:S(2)}) collective-permute-start(bf16[4,2,192,128]{3,2,1,0:T(8,128)(2,1)S(1)} %shard_map.38), channel_id=1, source_target_pairs={{0,1},{1,0},{2,3},{3,2},{4,5},{5,4},{6,7},{7,6},{8,9},{9,8},{10,11... | collective-permute-start | bytes 1179656 | tf_op jit(solution)/shard_map/ppermute | solution.py:277
  18.7 11.6 %collective-permute-start.8 = (bf16[4,4,64,128]{3,2,1,0:T(8,128)(2,1)S(1)}, bf16[4,4,64,128]{3,2,1,0:T(8,128)(2,1)S(1)}, u32[]{:S(2)}, u32[]{:S(2)}) collective-permute-start(bf16[4,4,64,128]{3,2,1,0:T(8,128)(2,1)S(1)} %fusion), channel_id=1, source_target_pairs={{0,2},{1,3},{2,0},{3,1},{4,6},{5,7},{6,4},{7,5},{8,10},{9,11},{10,... | collective-permute-start | bytes 786440 | tf_op jit(solution)/shard_map/ppermute | solution.py:327
  28.7 7.0 %collective-permute-start.6 = (bf16[4,4,64,128]{3,2,1,0:T(8,128)(2,1)S(1)}, bf16[4,4,64,128]{3,2,1,0:T(8,128)(2,1)S(1)}, u32[]{:S(2)}, u32[]{:S(2)}) collective-permute-start(bf16[4,4,64,128]{3,2,1,0:T(8,128)(2,1)S(1)} %get-tuple-element.24), channel_id=1, source_target_pairs={{0,2},{1,3},{2,0},{3,1},{4,6},{5,7},{6,4},{7,5},{8,10},{9,11},{10,... | collective-permute-start | bytes 786440 | tf_op jit(solution)/shard_map/ppermute | solution.py:327
  34.3 6.8 %collective-permute-start.5 = (bf16[4,4,64,128]{3,2,1,0:T(8,128)(2,1)S(1)}, bf16[4,4,64,128]{3,2,1,0:T(8,128)(2,1)S(1)}, u32[]{:S(2)}, u32[]{:S(2)}) collective-permute-start(bf16[4,4,64,128]{3,2,1,0:T(8,128)(2,1)S(1)} %get-tuple-element.22), channel_id=1, source_target_pairs={{0,2},{1,3},{2,0},{3,1},{4,6},{5,7},{6,4},{7,5},{8,10},{9,11},{10,... | collective-permute-start | bytes 786440 | tf_op jit(solution)/shard_map/ppermute | solution.py:327

commit v2 on v1

v2 whole, which is shorter than its diff:
```python
import functools

import jax
import jax.numpy as jnp
from jax import lax
from jax.experimental import pallas as pl
from jax.experimental.pallas import tpu as pltpu
from jax.sharding import PartitionSpec as P

SHARES = (4, 4, 4, 4)
AFTER = (None, None, 1, 2)
SMEM = pl.BlockSpec(memory_space=pltpu.SMEM)
VMEM = pl.BlockSpec(memory_space=pltpu.VMEM)
ANY = pl.BlockSpec(memory_space=pl.ANY)
HBM = pl.BlockSpec(memory_space=pltpu.HBM)
LITTLE = pl.CostEstimate(flops=1, bytes_accessed=1, transcendentals=0)
COSTS = [LITTLE] * 4
MUCH = pl.CostEstimate(flops=20_000_000_000, bytes_accessed=1, transcendentals=0)
PARAMS = pltpu.CompilerParams(vmem_limit_bytes=16 * 1024 * 1024)


def scalars(array):
    return pltpu.with_memory_space_constraint(array, pltpu.SMEM)


def near(array):
    return pltpu.with_memory_space_constraint(array, pltpu.VMEM)


def far(array):
    return pltpu.with_memory_space_constraint(array, pltpu.HBM)


def in_pairs(count):
    return count & (count - 1) == 0


def peer(index, step, count):
    return index ^ step if in_pairs(count) else (index + step) % count


def apart(here, there, count):
    return here ^ there if in_pairs(count) else lax.rem(there - here + count, count)


def swap(array, axis, step, count):
    return lax.ppermute(array, axis, [(i, peer(i, step, count)) for i in range(count)])


def call(kernel, ins, outs, operands, cost=LITTLE, **more):
    specs, shapes = zip(*outs)
    return pl.pallas_call(
        kernel,
        in_specs=ins,
        out_specs=specs,
        out_shape=shapes,
        cost_estimate=cost,
        compiler_params=PARAMS,
        **more,
    )(*operands)


def load(steps, first, times_ref, place_ref, data_ref, order_ref, slot_ref, spot_ref, held_ref, sem):
    blocks = times_ref.shape[0]
    count = len(steps)
    here = place_ref[0]

    def slot_of(i):
        step = apart(times_ref[i], here, count)
        slot = jnp.int32(0)
        for at, value in enumerate(steps):
            slot = jnp.where(step == value, at, slot)
        return slot

    def count_early(i, total):
        return total + (slot_of(i) < first).astype(jnp.int32)

    early = lax.fori_loop(0, blocks, count_early, jnp.int32(0))

    def copy(block, where):
        return pltpu.make_async_copy(data_ref.at[block], held_ref.at[where], sem.at[where])

    def place(i, at):
        low, high = at
        slot = slot_of(i)
        is_early = slot < first
        where = jnp.where(is_early, low, high)
        order_ref[where] = i
        slot_ref[where] = slot
        copy(i, where).start()
        one = is_early.astype(jnp.int32)
        return low + one, high + 1 - one

    lax.fori_loop(0, blocks, place, (jnp.int32(0), early))
    for i in range(3):
        spot_ref[i] = place_ref[i]
    for where in range(blocks):
        copy(order_ref[where], where).wait()


def turn_sites(chips, width, slot, vector_ref, place_ref, left_ref):
    chip, core = place_ref[1], place_ref[2]
    real, imag = vector_ref[0], vector_ref[1]
    for part, pair in enumerate(((real, imag), (-imag, real))):
        turned = jnp.concatenate(pair, axis=0).T
        for to_chip in range(chips):
            for to_core in range(2):
                stays = (core == to_core).astype(jnp.int32)
                at = ((stays * chips + apart(chip, to_chip, chips)) * 2 + part) * width
                start = (to_chip * 2 + to_core) * width
                left_ref[slot, pl.ds(pl.multiple_of(at, width), width), :] = turned[
                    start : start + width
                ]


def project_sites(chips, width, start, slot_ref, left_ref, held_ref, give_ref, keep_ref):
    spins, columns = held_ref.shape[1], held_ref.shape[-1]
    rows = 2 * width
    for i in range(give_ref.shape[1]):
        left = left_ref[slot_ref[start + i]]
        for spin in range(0, spins, 2):
            right = jnp.concatenate(
                [held_ref[start + i, s].reshape(-1, columns) for s in range(spin, spin + 2)],
                axis=1,
            )
            result = jnp.dot(left, right, preferred_element_type=jnp.float32)
            result = result.astype(give_ref.dtype)
            for s in range(2):
                side = result[:, s * columns : (s + 1) * columns]
                for ref, part in ((give_ref, side[: chips * rows]), (keep_ref, side[chips * rows :])):
                    ref[:, i, spin + s] = part.reshape(chips, rows, columns)


def project(chips, width, start, known, fresh, place_ref, slot_ref, *refs):
    vector_refs, held_ref = refs[:fresh], refs[fresh]
    if fresh:
        give_ref, keep_ref, left_ref = refs[-3:]
        for at, ref in enumerate(vector_refs):
            turn_sites(chips, width, known + at, ref, place_ref, left_ref)
    else:
        left_ref = refs[1]
        give_ref, keep_ref = refs[-2:]
    project_sites(chips, width, start, slot_ref, left_ref, held_ref, give_ref, keep_ref)


def finish(start, size, terms, order_ref, *refs):
    out_ref, stage_ref, sem = refs[-3:]

    def copy(i):
        return pltpu.make_async_copy(stage_ref.at[i], out_ref.at[order_ref[start + i]], sem.at[i])

    for i in range(size):
        total = None
        for ref in refs[:terms]:
            term = ref[i] if len(ref.shape) == 4 else ref[0, i]
            term = term.astype(jnp.float32)
            total = term if total is None else total + term
        stage_ref[i] = total.reshape(stage_ref.shape[1:]).astype(stage_ref.dtype)
        copy(i).start()
    for i in range(size):
        copy(i).wait()


def shards(solutions, eigvecs, sink_time):
    blocks, spins, _, colours, sites, columns = solutions.shape
    times = lax.axis_size("tm")
    members = lax.axis_size("space")
    chips = members // 2
    width = eigvecs.shape[-1] // members
    rows = 2 * width
    depth = 2 * colours * sites
    kind = solutions.dtype
    at = lax.axis_index("space")
    place = jnp.stack([lax.axis_index("tm"), at // 2, at % 2]).astype(jnp.int32)
    cores = [(i, i ^ 1) for i in range(members)]

    most = max(2, (2 * blocks + times - 1) // times)
    half = blocks // 2
    late = half // most
    first = times - late
    steps = [0] + list(range(1, times, 2)) + list(range(2, times, 2))

    own = eigvecs[0].reshape(2, colours * sites, -1)
    data = solutions.reshape(blocks, spins, 2, colours * sites, columns)
    vectors = [own]
    for slot, step in enumerate(steps[1:], 1):
        if slot >= first and in_pairs(times) and steps.index(step ^ 1) < first:
            vectors.append(swap(vectors[steps.index(step ^ 1)], "tm", 1, times))
        else:
            vectors.append(swap(own, "tm", step, times))

    numbers = pltpu.SMEM((blocks,), jnp.int32)
    order, slots, spot, held = call(
        functools.partial(load, steps, first),
        [SMEM, SMEM, HBM],
        [(SMEM, numbers), (SMEM, numbers), (SMEM, pltpu.SMEM((3,), jnp.int32)), (VMEM, pltpu.VMEM(data.shape, kind))],
        [sink_time[:, 0], place, far(data)],
        scratch_shapes=[pltpu.SemaphoreType.DMA((blocks,))],
    )
    held = near(held)
    order, slots, place = scalars(order), scalars(slots), scalars(spot)

    sizes = [share * blocks // 16 for share in SHARES]
    vectors = [near(v) for v in vectors]
    lefts = (VMEM, pltpu.VMEM((times, 4 * chips * width, depth), kind))
    left = None
    known = start = 0
    terms = []
    sents = []
    for at, size in enumerate(sizes):
        piece = (VMEM, pltpu.VMEM((chips, size, spins, rows, columns), kind))
        wanted = first if start + size <= half else times
        fresh = wanted - known
        after = sents[AFTER[at] : AFTER[at] + 1] if AFTER[at] is not None else []
        operands = [place, slots, *vectors[known:wanted], held]
        ins = [SMEM] * 2 + [VMEM] * (fresh + 1)
        if left is not None:
            operands.append(near(left))
            ins.append(VMEM)
        results = call(
            functools.partial(project, chips, width, start, known, fresh),
            ins + [ANY] * len(after),
            [piece, piece] + [lefts] * bool(fresh),
            operands + after,
            COSTS[at],
            input_output_aliases={len(operands) - 1: 2} if fresh and left is not None else {},
        )
        give, keep = results[:2]
        if fresh:
            left = results[2]
        got = lax.ppermute(give, "space", cores)
        sums = [keep, got]
        for step in range(1, chips):
            sent = (keep[step].astype(jnp.float32) + got[step].astype(jnp.float32)).astype(kind)
            sums.append(send(sent, step, members))
        sents.append(sent)
        terms.append(sums)
        known = wanted
        start += size

    result = None
    start = 0
    for size, sums in zip(sizes, terms):
        operands = [order, *[near(a) for a in sums]]
        ins = [SMEM] + [VMEM] * len(sums)
        aliases = {}
        if result is not None:
            aliases = {len(operands): 0}
            operands.append(result)
            ins.append(HBM)
        (result,) = call(
            functools.partial(finish, start, size, len(sums)),
            ins,
            [(HBM, jax.ShapeDtypeStruct((blocks, spins, 2, width, columns), kind))],
            operands,
            MUCH,
            scratch_shapes=[
                pltpu.VMEM((size, spins, 2, width, columns), kind),
                pltpu.SemaphoreType.DMA((size,)),
            ],
            input_output_aliases=aliases,
        )
        start += size
    return result


def send(array, step, members):
    route = [(i, peer(i // 2, step, members // 2) * 2 + i % 2) for i in range(members)]
    return lax.ppermute(array, "space", route)


def solution(mesh):
    in_specs = (
        P(("grp", "tm"), None, None, None, "space", None),
        P("tm", None, None, "space", None),
        P(("grp", "tm"), None),
    )
    out_specs = P(("grp", "tm"), None, None, "space", None)
    return jax.shard_map(shards, mesh=mesh, in_specs=in_specs, out_specs=out_specs, check_vma=False)
```

time: 42.6 us -> 39.5 us (0.927)
  Pallas kernels: 17.2 us -> 9.78 us
  waiting for transfers between devices: 12.1 us -> 16.2 us
    pallas_call x9, Pallas kernels: 17.2 us -> 9.78 us  [call(): pl.pallas_call(kernel, in_specs=ins, out_specs=specs, out_shape=shapes, c...]
    ppermute x4, waiting for transfers between devices: 9.06 us -> 11.8 us  [send(): return lax.ppermute(array, 'space', route)]
    ppermute x3, waiting for transfers between devices: 2.26 us -> 3.76 us  [swap(): lax.ppermute(array, axis, [(i, peer(i, step, count)) for i in range(count)])]
    ppermute x2 -> x0, starting transfers between devices: 0.52 us -> none  [the longest x1 0.45 us: shards(): other_data = lax.ppermute(data, 'space', cores)]
  transfers between devices with their start and end apart: 11 -> 11, of which waited for: 6 -> 7; matrix products, arithmetic and copies ran while one was open for 1% -> 1% of each run, Pallas kernels for 37% -> 21%
where the time goes in v2:
time: 39.5 us; the launch traced here: 39.4 us
  waiting for transfers between devices  16.2 us (41%)
  starting transfers between devices  12.2 us (31%)
  Pallas kernels  9.78 us (25%)
  local copies, waits for them, and re-layouts  0.66 us (2%)
    ppermute x4, waiting for transfers between devices, send(): return lax.ppermute(array, 'space', route)  11.8 us
    pallas_call x9, Pallas kernels, call(): pl.pallas_call(kernel, in_specs=ins, out_specs=specs, out_shape=shapes, c...  9.78 us
    ppermute x3, starting transfers between devices, swap(): lax.ppermute(array, axis, [(i, peer(i, step, count)) for i in range(count)])  6.14 us
    ppermute x4, starting transfers between devices, send(): return lax.ppermute(array, 'space', route)  5.28 us
    ppermute x3, waiting for transfers between devices, swap(): lax.ppermute(array, axis, [(i, peer(i, step, count)) for i in range(count)])  3.76 us
  transfers between devices with their start and end apart: 11, of which 7 were waited for; matrix products, arithmetic and copies ran while one was open for 1% of the time, Pallas kernels for 21%

profile of v2, /device:TPU:0, one launch (start us, length us, event | category | flops | bytes accessed | tf_op | source)
XLA Modules:
  0.0 39.4 jit_solution(14474223756173990212)
XLA Ops:
  0.0 3.0 %collective-permute-start.2 = (bf16[2,192,128]{2,1,0:T(8,128)(2,1)}, bf16[2,192,128]{2,1,0:T(8,128)(2,1)S(1)}, u32[]{:S(2)}, u32[]{:S(2)}) collective-permute-start(bf16[2,192,128]{2,1,0:T(8,128)(2,1)} %bitcast.14), channel_id=1, source_target_pairs={{0,4},{4,0},{8,12},{12,8},{1,5},{5,1},{9,13},{13,9},{2,6},{6,2},{1... | collective-permute-start | bytes 294920 | tf_op jit(solution)/shard_map/ppermute | solution.py:47
  3.0 2.5 %collective-permute-start = (bf16[2,192,128]{2,1,0:T(8,128)(2,1)}, bf16[2,192,128]{2,1,0:T(8,128)(2,1)S(1)}, u32[]{:S(2)}, u32[]{:S(2)}) collective-permute-start(bf16[2,192,128]{2,1,0:T(8,128)(2,1)} %bitcast.15), channel_id=1, source_target_pairs={{0,12},{4,8},{8,4},{12,0},{1,13},{5,9},{9,5},{13,1},{2,14},{6,10},... | collective-permute-start | bytes 294920 | tf_op jit(solution)/shard_map/ppermute | solution.py:47
  5.5 0.1 pad_add_fusion.place_ref
  5.6 0.7 %copy-done.1 = s32[16,1]{0,1:T(1,128)S(1)} copy-done((s32[16,1]{0,1:T(1,128)S(1)}, s32[16,1]{0,1:T(1,128)}, u32[]{:S(2)}) %copy-start.1) | copy-done | bytes 88
  6.2 3.7 %shard_map.37 = (s32[16]{0:T(128)S(4)}, s32[16]{0:T(128)S(4)}, s32[3]{0:T(128)S(4)}, bf16[16,4,2,192,128]{4,3,2,1,0:T(8,128)(2,1)S(1)}) custom-call(s32[16]{0:T(128)S(1)} %bitcast.17, s32[3]{0:T(128)S(1)} %pad_add_fusion.place_ref, bf16[16,4,2,192,128]{4,3,2,1,0:T(8,128)(2,1)} %bitcast.18), custom_call_target="tpu_custom_call" | custom-call | flops 1 | bytes 1 | tf_op jit(solution)/shard_map/pallas_call | solution.py:52
  9.9 0.5 %collective-permute-done.refs_2_ = bf16[2,192,128]{2,1,0:T(8,128)(2,1)S(1)} collective-permute-done((bf16[2,192,128]{2,1,0:T(8,128)(2,1)}, bf16[2,192,128]{2,1,0:T(8,128)(2,1)S(1)}, u32[]{:S(2)}, u32[]{:S(2)}) %collective-permute-start) | collective-permute-done | bytes 98336 | tf_op jit(solution)/shard_map/ppermute | solution.py:47
  10.4 0.9 %shard_map.38 = (bf16[2,4,4,64,128]{4,3,2,1,0:T(8,128)(2,1)S(1)}, bf16[2,4,4,64,128]{4,3,2,1,0:T(8,128)(2,1)S(1)}, bf16[4,256,384]{2,1,0:T(8,128)(2,1)S(1)}) custom-call(s32[3]{0:T(128)S(4)} %get-tuple-element.20.place_ref, s32[16]{0:T(128)S(4)} %get-tuple-element.21.slot_ref, bf16[2,192,128]{2,1,0:T(8,128)(2,1)S(1)} %bitcast.16, ...), custom_call_target="tpu_custom_call" | custom-call | flops 1 | bytes 1 | tf_op jit(solution)/shard_map/pallas_call | solution.py:52
  11.3 0.1 collective-permute-start.9
  11.4 0.7 %shard_map.39 = (bf16[2,4,4,64,128]{4,3,2,1,0:T(8,128)(2,1)S(1)}, bf16[2,4,4,64,128]{4,3,2,1,0:T(8,128)(2,1)S(1)}) custom-call(s32[3]{0:T(128)S(4)} %get-tuple-element.20.place_ref, s32[16]{0:T(128)S(4)} %get-tuple-element.21.slot_ref, bf16[16,4,2,192,128]{4,3,2,1,0:T(8,128)(2,1)S(1)} %get-tuple-element.22.refs_3_.refs_0_.refs_1_, ...), custom_call_target="tpu_custom_call" | custom-call | flops 1 | bytes 1 | tf_op jit(solution)/shard_map/pallas_call | solution.py:52
  12.1 0.6 %collective-permute-start.3 = (bf16[2,4,4,64,128]{4,3,2,1,0:T(8,128)(2,1)S(1)}, bf16[2,4,4,64,128]{4,3,2,1,0:T(8,128)(2,1)S(1)}, u32[]{:S(2)}, u32[]{:S(2)}) collective-permute-start(bf16[2,4,4,64,128]{4,3,2,1,0:T(8,128)(2,1)S(1)} %get-tuple-element.25), channel_id=1, source_target_pairs={{0,1},{1,0},{2,3},{3,2},{4,5},{5,4},{6,7},{7,6},{8,9},{9,8},{10,11... | collective-permute-start | bytes 1572872 | tf_op jit(solution)/shard_map/ppermute | solution.py:231
  12.6 0.6 %collective-permute-done.9.refs_1_ = bf16[2,4,4,64,128]{4,3,2,1,0:T(8,128)(2,1)S(1)} collective-permute-done((bf16[2,4,4,64,128]{4,3,2,1,0:T(8,128)(2,1)S(1)}, bf16[2,4,4,64,128]{4,3,2,1,0:T(8,128)(2,1)S(1)}, u32[]{:S(2)}, u32[]{:S(2)}) %collective-permute-start.9) | collective-permute-done | bytes 524320 | tf_op jit(solution)/shard_map/ppermute | solution.py:231
  13.3 0.1 fusion.3
  13.3 1.6 %collective-permute-start.10 = (bf16[4,4,64,128]{3,2,1,0:T(8,128)(2,1)S(1)}, bf16[4,4,64,128]{3,2,1,0:T(8,128)(2,1)S(1)}, u32[]{:S(2)}, u32[]{:S(2)}) collective-permute-start(bf16[4,4,64,128]{3,2,1,0:T(8,128)(2,1)S(1)} %fusion.3), channel_id=1, source_target_pairs={{0,2},{1,3},{2,0},{3,1},{4,6},{5,7},{6,4},{7,5},{8,10},{9,11},{10,... | collective-permute-start | bytes 786440 | tf_op jit(solution)/shard_map/ppermute | solution.py:269
  14.9 0.6 %collective-permute-start.1 = (bf16[2,192,128]{2,1,0:T(8,128)(2,1)S(1)}, bf16[2,192,128]{2,1,0:T(8,128)(2,1)S(1)}, u32[]{:S(2)}, u32[]{:S(2)}) collective-permute-start(bf16[2,192,128]{2,1,0:T(8,128)(2,1)S(1)} %collective-permute-done.refs_2_), channel_id=1, source_target_pairs={{0,4},{4,0},{8,12},{12,8},{1,5},{5,1},{9,13},{13,9},{2,6},{6,2},{1... | collective-permute-start | bytes 294920 | tf_op jit(solution)/shard_map/ppermute | solution.py:47
  15.5 0.1 fusion.refs_3_
  15.6 0.6 %collective-permute-start.8 = (bf16[4,4,64,128]{3,2,1,0:T(8,128)(2,1)S(1)}, bf16[4,4,64,128]{3,2,1,0:T(8,128)(2,1)S(1)}, u32[]{:S(2)}, u32[]{:S(2)}) collective-permute-start(bf16[4,4,64,128]{3,2,1,0:T(8,128)(2,1)S(1)} %fusion.refs_3_), channel_id=1, source_target_pairs={{0,2},{1,3},{2,0},{3,1},{4,6},{5,7},{6,4},{7,5},{8,10},{9,11},{10,... | collective-permute-start | bytes 786440 | tf_op jit(solution)/shard_map/ppermute | solution.py:269
  16.2 3.3 %collective-permute-done.1.refs_0_ = bf16[2,192,128]{2,1,0:T(8,128)(2,1)S(1)} collective-permute-done((bf16[2,192,128]{2,1,0:T(8,128)(2,1)S(1)}, bf16[2,192,128]{2,1,0:T(8,128)(2,1)S(1)}, u32[]{:S(2)}, u32[]{:S(2)}) %collective-permute-start.1) | collective-permute-done | bytes 98336 | tf_op jit(solution)/shard_map/ppermute | solution.py:47
  19.5 0.8 %shard_map.40 = (bf16[2,4,4,64,128]{4,3,2,1,0:T(8,128)(2,1)S(1)}, bf16[2,4,4,64,128]{4,3,2,1,0:T(8,128)(2,1)S(1)}, bf16[4,256,384]{2,1,0:T(8,128)(2,1)S(1)}) custom-call(s32[3]{0:T(128)S(4)} %get-tuple-element.20.place_ref, s32[16]{0:T(128)S(4)} %get-tuple-element.21.slot_ref, ...), custom_call_target="tpu_custom_call", output_to_operand_aliasing={{2}: (4, {})} | custom-call | flops 1 | bytes 1 | tf_op jit(solution)/shard_map/pallas_call | solution.py:52
  20.3 0.1 collective-permute-start.4
  20.4 2.2 %collective-permute-done.10.refs_2_ = bf16[4,4,64,128]{3,2,1,0:T(8,128)(2,1)S(1)} collective-permute-done((bf16[4,4,64,128]{3,2,1,0:T(8,128)(2,1)S(1)}, bf16[4,4,64,128]{3,2,1,0:T(8,128)(2,1)S(1)}, u32[]{:S(2)}, u32[]{:S(2)}) %collective-permute-start.10) | collective-permute-done | bytes 262176 | tf_op jit(solution)/shard_map/ppermute | solution.py:269
  22.6 0.8 %shard_map.42.refs_3_ = bf16[16,4,2,32,128]{4,3,2,1,0:T(8,128)(2,1)} custom-call(s32[16]{0:T(128)S(4)} %get-tuple-element.19.order_ref, bf16[2,4,4,64,128]{4,3,2,1,0:T(8,128)(2,1)S(1)} %get-tuple-element.31.refs_0_, bf16[2,4,4,64,128]{4,3,2,1,0:T(8,128)(2,1)S(1)} %collective-permute-done.9.refs_1_, bf16[4,4,64,128]{3,2,1,0:T(8,128)(2,1)S(1)} %collective-permute-done.10.refs_2_), custom_call_target="tpu_custom_call" | custom-call | flops 20000000000 | bytes 1 | tf_op jit(solution)/shard_map/pallas_call | solution.py:52
  23.3 0.1 fusion.1.refs_2_
  23.4 1.6 %collective-permute-start.7 = (bf16[4,4,64,128]{3,2,1,0:T(8,128)(2,1)S(1)}, bf16[4,4,64,128]{3,2,1,0:T(8,128)(2,1)S(1)}, u32[]{:S(2)}, u32[]{:S(2)}) collective-permute-start(bf16[4,4,64,128]{3,2,1,0:T(8,128)(2,1)S(1)} %fusion.1.refs_2_), channel_id=1, source_target_pairs={{0,2},{1,3},{2,0},{3,1},{4,6},{5,7},{6,4},{7,5},{8,10},{9,11},{10,... | collective-permute-start | bytes 786440 | tf_op jit(solution)/shard_map/ppermute | solution.py:269
  25.0 0.7 %shard_map.41 = (bf16[2,4,4,64,128]{4,3,2,1,0:T(8,128)(2,1)S(1)}, bf16[2,4,4,64,128]{4,3,2,1,0:T(8,128)(2,1)S(1)}) custom-call(s32[3]{0:T(128)S(4)} %get-tuple-element.20.place_ref, s32[16]{0:T(128)S(4)} %get-tuple-element.21.slot_ref, bf16[16,4,2,192,128]{4,3,2,1,0:T(8,128)(2,1)S(1)} %get-tuple-element.22.refs_3_.refs_0_.refs_1_, ...), custom_call_target="tpu_custom_call" | custom-call | flops 1 | bytes 1 | tf_op jit(solution)/shard_map/pallas_call | solution.py:52
  25.8 2.4 %collective-permute-done.8.refs_2_ = bf16[4,4,64,128]{3,2,1,0:T(8,128)(2,1)S(1)} collective-permute-done((bf16[4,4,64,128]{3,2,1,0:T(8,128)(2,1)S(1)}, bf16[4,4,64,128]{3,2,1,0:T(8,128)(2,1)S(1)}, u32[]{:S(2)}, u32[]{:S(2)}) %collective-permute-start.8) | collective-permute-done | bytes 262176 | tf_op jit(solution)/shard_map/ppermute | solution.py:269
  28.2 0.8 %shard_map.43.refs_3_ = bf16[16,4,2,32,128]{4,3,2,1,0:T(8,128)(2,1)} custom-call(s32[16]{0:T(128)S(4)} %get-tuple-element.19.order_ref, bf16[2,4,4,64,128]{4,3,2,1,0:T(8,128)(2,1)S(1)} %get-tuple-element.24.refs_0_, bf16[2,4,4,64,128]{4,3,2,1,0:T(8,128)(2,1)S(1)} %collective-permute-done.3.refs_1_, ...), custom_call_target="tpu_custom_call", output_to_operand_aliasing={{}: (4, {})} | custom-call | flops 20000000000 | bytes 1 | tf_op jit(solution)/shard_map/pallas_call | solution.py:52
  29.0 0.1 fusion.2
  29.0 1.6 %collective-permute-start.6 = (bf16[4,4,64,128]{3,2,1,0:T(8,128)(2,1)S(1)}, bf16[4,4,64,128]{3,2,1,0:T(8,128)(2,1)S(1)}, u32[]{:S(2)}, u32[]{:S(2)}) collective-permute-start(bf16[4,4,64,128]{3,2,1,0:T(8,128)(2,1)S(1)} %fusion.2), channel_id=1, source_target_pairs={{0,2},{1,3},{2,0},{3,1},{4,6},{5,7},{6,4},{7,5},{8,10},{9,11},{10,... | collective-permute-start | bytes 786440 | tf_op jit(solution)/shard_map/ppermute | solution.py:269
  30.6 3.2 %collective-permute-done.7.refs_2_ = bf16[4,4,64,128]{3,2,1,0:T(8,128)(2,1)S(1)} collective-permute-done((bf16[4,4,64,128]{3,2,1,0:T(8,128)(2,1)S(1)}, bf16[4,4,64,128]{3,2,1,0:T(8,128)(2,1)S(1)}, u32[]{:S(2)}, u32[]{:S(2)}) %collective-permute-start.7) | collective-permute-done | bytes 262176 | tf_op jit(solution)/shard_map/ppermute | solution.py:269
  33.8 0.8 %shard_map.44.refs_3_ = bf16[16,4,2,32,128]{4,3,2,1,0:T(8,128)(2,1)} custom-call(s32[16]{0:T(128)S(4)} %get-tuple-element.19.order_ref, bf16[2,4,4,64,128]{4,3,2,1,0:T(8,128)(2,1)S(1)} %get-tuple-element.27.refs_0_, bf16[2,4,4,64,128]{4,3,2,1,0:T(8,128)(2,1)S(1)} %collective-permute-done.4.refs_1_, ...), custom_call_target="tpu_custom_call", output_to_operand_aliasing={{}: (4, {})} | custom-call | flops 20000000000 | bytes 1 | tf_op jit(solution)/shard_map/pallas_call | solution.py:52
  34.6 4.0 %collective-permute-done.6.refs_2_ = bf16[4,4,64,128]{3,2,1,0:T(8,128)(2,1)S(1)} collective-permute-done((bf16[4,4,64,128]{3,2,1,0:T(8,128)(2,1)S(1)}, bf16[4,4,64,128]{3,2,1,0:T(8,128)(2,1)S(1)}, u32[]{:S(2)}, u32[]{:S(2)}) %collective-permute-start.6) | collective-permute-done | bytes 262176 | tf_op jit(solution)/shard_map/ppermute | solution.py:269
  38.6 0.8 %shard_map.45 = bf16[16,4,2,32,128]{4,3,2,1,0:T(8,128)(2,1)} custom-call(s32[16]{0:T(128)S(4)} %get-tuple-element.19.order_ref, bf16[2,4,4,64,128]{4,3,2,1,0:T(8,128)(2,1)S(1)} %get-tuple-element.29.refs_0_, bf16[2,4,4,64,128]{4,3,2,1,0:T(8,128)(2,1)S(1)} %collective-permute-done.5.refs_1_, ...), custom_call_target="tpu_custom_call", output_to_operand_aliasing={{}: (4, {})} | custom-call | flops 20000000000 | bytes 1 | tf_op jit(solution)/shard_map/pallas_call | solution.py:52
  (8 shorter events, 0.1 us)
Async XLA Ops:
  0.0 10.4 %copy-start = (bf16[1,2,3,64,128]{4,3,2,1,0:T(8,128)(2,1)S(1)}, bf16[1,2,3,64,128]{4,3,2,1,0:T(8,128)(2,1)}, u32[]{:S(2)}) copy-start(bf16[1,2,3,64,128]{4,3,2,1,0:T(8,128)(2,1)} %param.4) | copy-start | bytes 294916
  0.0 9.9 %collective-permute-start.2 = (bf16[2,192,128]{2,1,0:T(8,128)(2,1)}, bf16[2,192,128]{2,1,0:T(8,128)(2,1)S(1)}, u32[]{:S(2)}, u32[]{:S(2)}) collective-permute-start(bf16[2,192,128]{2,1,0:T(8,128)(2,1)} %bitcast.14), channel_id=1, source_target_pairs={{0,4},{4,0},{8,12},{12,8},{1,5},{5,1},{9,13},{13,9},{2,6},{6,2},{1... | collective-permute-start | bytes 294920 | tf_op jit(solution)/shard_map/ppermute | solution.py:47
  3.0 7.4 %collective-permute-start = (bf16[2,192,128]{2,1,0:T(8,128)(2,1)}, bf16[2,192,128]{2,1,0:T(8,128)(2,1)S(1)}, u32[]{:S(2)}, u32[]{:S(2)}) collective-permute-start(bf16[2,192,128]{2,1,0:T(8,128)(2,1)} %bitcast.15), channel_id=1, source_target_pairs={{0,12},{4,8},{8,4},{12,0},{1,13},{5,9},{9,5},{13,1},{2,14},{6,10},... | collective-permute-start | bytes 294920 | tf_op jit(solution)/shard_map/ppermute | solution.py:47
  5.6 0.7 %copy-start.1 = (s32[16,1]{0,1:T(1,128)S(1)}, s32[16,1]{0,1:T(1,128)}, u32[]{:S(2)}) copy-start(s32[16,1]{0,1:T(1,128)} %param.5) | copy-start | bytes 196
  11.3 2.0 %collective-permute-start.9 = (bf16[2,4,4,64,128]{4,3,2,1,0:T(8,128)(2,1)S(1)}, bf16[2,4,4,64,128]{4,3,2,1,0:T(8,128)(2,1)S(1)}, u32[]{:S(2)}, u32[]{:S(2)}) collective-permute-start(bf16[2,4,4,64,128]{4,3,2,1,0:T(8,128)(2,1)S(1)} %get-tuple-element.32), channel_id=1, source_target_pairs={{0,1},{1,0},{2,3},{3,2},{4,5},{5,4},{6,7},{7,6},{8,9},{9,8},{10,11... | collective-permute-start | bytes 1572872 | tf_op jit(solution)/shard_map/ppermute | solution.py:231
  12.1 3.5 %collective-permute-start.3 = (bf16[2,4,4,64,128]{4,3,2,1,0:T(8,128)(2,1)S(1)}, bf16[2,4,4,64,128]{4,3,2,1,0:T(8,128)(2,1)S(1)}, u32[]{:S(2)}, u32[]{:S(2)}) collective-permute-start(bf16[2,4,4,64,128]{4,3,2,1,0:T(8,128)(2,1)S(1)} %get-tuple-element.25), channel_id=1, source_target_pairs={{0,1},{1,0},{2,3},{3,2},{4,5},{5,4},{6,7},{7,6},{8,9},{9,8},{10,11... | collective-permute-start | bytes 1572872 | tf_op jit(solution)/shard_map/ppermute | solution.py:231
  13.3 9.2 %collective-permute-start.10 = (bf16[4,4,64,128]{3,2,1,0:T(8,128)(2,1)S(1)}, bf16[4,4,64,128]{3,2,1,0:T(8,128)(2,1)S(1)}, u32[]{:S(2)}, u32[]{:S(2)}) collective-permute-start(bf16[4,4,64,128]{3,2,1,0:T(8,128)(2,1)S(1)} %fusion.3), channel_id=1, source_target_pairs={{0,2},{1,3},{2,0},{3,1},{4,6},{5,7},{6,4},{7,5},{8,10},{9,11},{10,... | collective-permute-start | bytes 786440 | tf_op jit(solution)/shard_map/ppermute | solution.py:269
  14.9 4.6 %collective-permute-start.1 = (bf16[2,192,128]{2,1,0:T(8,128)(2,1)S(1)}, bf16[2,192,128]{2,1,0:T(8,128)(2,1)S(1)}, u32[]{:S(2)}, u32[]{:S(2)}) collective-permute-start(bf16[2,192,128]{2,1,0:T(8,128)(2,1)S(1)} %collective-permute-done.refs_2_), channel_id=1, source_target_pairs={{0,4},{4,0},{8,12},{12,8},{1,5},{5,1},{9,13},{13,9},{2,6},{6,2},{1... | collective-permute-start | bytes 294920 | tf_op jit(solution)/shard_map/ppermute | solution.py:47
  15.6 12.6 %collective-permute-start.8 = (bf16[4,4,64,128]{3,2,1,0:T(8,128)(2,1)S(1)}, bf16[4,4,64,128]{3,2,1,0:T(8,128)(2,1)S(1)}, u32[]{:S(2)}, u32[]{:S(2)}) collective-permute-start(bf16[4,4,64,128]{3,2,1,0:T(8,128)(2,1)S(1)} %fusion.refs_3_), channel_id=1, source_target_pairs={{0,2},{1,3},{2,0},{3,1},{4,6},{5,7},{6,4},{7,5},{8,10},{9,11},{10,... | collective-permute-start | bytes 786440 | tf_op jit(solution)/shard_map/ppermute | solution.py:269
  20.3 3.0 %collective-permute-start.4 = (bf16[2,4,4,64,128]{4,3,2,1,0:T(8,128)(2,1)S(1)}, bf16[2,4,4,64,128]{4,3,2,1,0:T(8,128)(2,1)S(1)}, u32[]{:S(2)}, u32[]{:S(2)}) collective-permute-start(bf16[2,4,4,64,128]{4,3,2,1,0:T(8,128)(2,1)S(1)} %get-tuple-element.28), channel_id=1, source_target_pairs={{0,1},{1,0},{2,3},{3,2},{4,5},{5,4},{6,7},{7,6},{8,9},{9,8},{10,11... | collective-permute-start | bytes 1572872 | tf_op jit(solution)/shard_map/ppermute | solution.py:231
  23.4 10.4 %collective-permute-start.7 = (bf16[4,4,64,128]{3,2,1,0:T(8,128)(2,1)S(1)}, bf16[4,4,64,128]{3,2,1,0:T(8,128)(2,1)S(1)}, u32[]{:S(2)}, u32[]{:S(2)}) collective-permute-start(bf16[4,4,64,128]{3,2,1,0:T(8,128)(2,1)S(1)} %fusion.1.refs_2_), channel_id=1, source_target_pairs={{0,2},{1,3},{2,0},{3,1},{4,6},{5,7},{6,4},{7,5},{8,10},{9,11},{10,... | collective-permute-start | bytes 786440 | tf_op jit(solution)/shard_map/ppermute | solution.py:269
  25.7 3.3 %collective-permute-start.5 = (bf16[2,4,4,64,128]{4,3,2,1,0:T(8,128)(2,1)S(1)}, bf16[2,4,4,64,128]{4,3,2,1,0:T(8,128)(2,1)S(1)}, u32[]{:S(2)}, u32[]{:S(2)}) collective-permute-start(bf16[2,4,4,64,128]{4,3,2,1,0:T(8,128)(2,1)S(1)} %get-tuple-element.30), channel_id=1, source_target_pairs={{0,1},{1,0},{2,3},{3,2},{4,5},{5,4},{6,7},{7,6},{8,9},{9,8},{10,11... | collective-permute-start | bytes 1572872 | tf_op jit(solution)/shard_map/ppermute | solution.py:231
  29.0 9.6 %collective-permute-start.6 = (bf16[4,4,64,128]{3,2,1,0:T(8,128)(2,1)S(1)}, bf16[4,4,64,128]{3,2,1,0:T(8,128)(2,1)S(1)}, u32[]{:S(2)}, u32[]{:S(2)}) collective-permute-start(bf16[4,4,64,128]{3,2,1,0:T(8,128)(2,1)S(1)} %fusion.2), channel_id=1, source_target_pairs={{0,2},{1,3},{2,0},{3,1},{4,6},{5,7},{6,4},{7,5},{8,10},{9,11},{10,... | collective-permute-start | bytes 786440 | tf_op jit(solution)/shard_map/ppermute | solution.py:269

commit v3 on v2

--- a/solution.py
+++ b/solution.py
@@ -7,14 +7,13 @@
 from jax.experimental.pallas import tpu as pltpu
 from jax.sharding import PartitionSpec as P
 
-SHARES = (4, 4, 4, 4)
-AFTER = (None, None, 1, 2)
+SHARES = (4, 4, 8)
+AFTER = (None, None, 1)
 SMEM = pl.BlockSpec(memory_space=pltpu.SMEM)
 VMEM = pl.BlockSpec(memory_space=pltpu.VMEM)
 ANY = pl.BlockSpec(memory_space=pl.ANY)
 HBM = pl.BlockSpec(memory_space=pltpu.HBM)
 LITTLE = pl.CostEstimate(flops=1, bytes_accessed=1, transcendentals=0)
-COSTS = [LITTLE] * 4
 MUCH = pl.CostEstimate(flops=20_000_000_000, bytes_accessed=1, transcendentals=0)
 PARAMS = pltpu.CompilerParams(vmem_limit_bytes=16 * 1024 * 1024)
 
@@ -60,10 +59,10 @@
     )(*operands)
 
 
-def load(steps, first, times_ref, place_ref, data_ref, order_ref, slot_ref, spot_ref, held_ref, sem):
+def load(steps, first, times_ref, data_ref, order_ref, slot_ref, held_ref, sem):
     blocks = times_ref.shape[0]
     count = len(steps)
-    here = place_ref[0]
+    here = lax.axis_index("tm")
 
     def slot_of(i):
         step = apart(times_ref[i], here, count)
@@ -92,14 +91,13 @@
         return low + one, high + 1 - one
 
     lax.fori_loop(0, blocks, place, (jnp.int32(0), early))
-    for i in range(3):
-        spot_ref[i] = place_ref[i]
     for where in range(blocks):
         copy(order_ref[where], where).wait()
 
 
-def turn_sites(chips, width, slot, vector_ref, place_ref, left_ref):
-    chip, core = place_ref[1], place_ref[2]
+def turn_sites(chips, width, slot, vector_ref, left_ref):
+    here = lax.axis_index("space")
+    chip, core = here // 2, here % 2
     real, imag = vector_ref[0], vector_ref[1]
     for part, pair in enumerate(((real, imag), (-imag, real))):
         turned = jnp.concatenate(pair, axis=0).T
@@ -113,10 +111,10 @@
                 ]
 
 
-def project_sites(chips, width, start, slot_ref, left_ref, held_ref, give_ref, keep_ref):
+def project_sites(chips, width, start, slot_ref, left_ref, held_ref, give_refs, keep_ref):
     spins, columns = held_ref.shape[1], held_ref.shape[-1]
     rows = 2 * width
-    for i in range(give_ref.shape[1]):
+    for i in range(keep_ref.shape[1]):
         left = left_ref[slot_ref[start + i]]
         for spin in range(0, spins, 2):
             right = jnp.concatenate(
@@ -124,23 +122,25 @@
                 axis=1,
             )
             result = jnp.dot(left, right, preferred_element_type=jnp.float32)
-            result = result.astype(give_ref.dtype)
+            result = result.astype(keep_ref.dtype)
             for s in range(2):
                 side = result[:, s * columns : (s + 1) * columns]
-                for ref, part in ((give_ref, side[: chips * rows]), (keep_ref, side[chips * rows :])):
-                    ref[:, i, spin + s] = part.reshape(chips, rows, columns)
-
-
-def project(chips, width, start, known, fresh, place_ref, slot_ref, *refs):
+                parts = side.reshape(2, chips, rows, columns)
+                give_refs[0][0, i, spin + s] = parts[0, 0]
+                give_refs[1][:, i, spin + s] = parts[0, 1:]
+                keep_ref[:, i, spin + s] = parts[1]
+
+
+def project(chips, width, start, known, fresh, slot_ref, *refs):
     vector_refs, held_ref = refs[:fresh], refs[fresh]
     if fresh:
-        give_ref, keep_ref, left_ref = refs[-3:]
+        *give_refs, keep_ref, left_ref = refs[-4:]
         for at, ref in enumerate(vector_refs):
-            turn_sites(chips, width, known + at, ref, place_ref, left_ref)
+            turn_sites(chips, width, known + at, ref, left_ref)
     else:
         left_ref = refs[1]
-        give_ref, keep_ref = refs[-2:]
-    project_sites(chips, width, start, slot_ref, left_ref, held_ref, give_ref, keep_ref)
+        *give_refs, keep_ref = refs[-3:]
+    project_sites(chips, width, start, slot_ref, left_ref, held_ref, give_refs, keep_ref)
 
 
 def finish(start, size, terms, order_ref, *refs):
@@ -170,8 +170,6 @@
     rows = 2 * width
     depth = 2 * colours * sites
     kind = solutions.dtype
-    at = lax.axis_index("space")
-    place = jnp.stack([lax.axis_index("tm"), at // 2, at % 2]).astype(jnp.int32)
     cores = [(i, i ^ 1) for i in range(members)]
 
     most = max(2, (2 * blocks + times - 1) // times)
@@ -190,15 +188,15 @@
             vectors.append(swap(own, "tm", step, times))
 
     numbers = pltpu.SMEM((blocks,), jnp.int32)
-    order, slots, spot, held = call(
+    order, slots, held = call(
         functools.partial(load, steps, first),
-        [SMEM, SMEM, HBM],
-        [(SMEM, numbers), (SMEM, numbers), (SMEM, pltpu.SMEM((3,), jnp.int32)), (VMEM, pltpu.VMEM(data.shape, kind))],
-        [sink_time[:, 0], place, far(data)],
+        [SMEM, HBM],
+        [(SMEM, numbers), (SMEM, numbers), (VMEM, pltpu.VMEM(data.shape, kind))],
+        [sink_time[:, 0], far(data)],
         scratch_shapes=[pltpu.SemaphoreType.DMA((blocks,))],
     )
     held = near(held)
-    order, slots, place = scalars(order), scalars(slots), scalars(spot)
+    order, slots = scalars(order), scalars(slots)
 
     sizes = [share * blocks // 16 for share in SHARES]
     vectors = [near(v) for v in vectors]
@@ -208,30 +206,32 @@
     terms = []
     sents = []
     for at, size in enumerate(sizes):
-        piece = (VMEM, pltpu.VMEM((chips, size, spins, rows, columns), kind))
+        pieces = [
+            (VMEM, pltpu.VMEM((count, size, spins, rows, columns), kind))
+            for count in (1, chips - 1, chips)
+        ]
         wanted = first if start + size <= half else times
         fresh = wanted - known
         after = sents[AFTER[at] : AFTER[at] + 1] if AFTER[at] is not None else []
-        operands = [place, slots, *vectors[known:wanted], held]
-        ins = [SMEM] * 2 + [VMEM] * (fresh + 1)
+        operands = [slots, *vectors[known:wanted], held]
+        ins = [SMEM] + [VMEM] * (fresh + 1)
         if left is not None:
             operands.append(near(left))
             ins.append(VMEM)
         results = call(
             functools.partial(project, chips, width, start, known, fresh),
             ins + [ANY] * len(after),
-            [piece, piece] + [lefts] * bool(fresh),
+            pieces + [lefts] * bool(fresh),
             operands + after,
-            COSTS[at],
-            input_output_aliases={len(operands) - 1: 2} if fresh and left is not None else {},
+            input_output_aliases={len(operands) - 1: 3} if fresh and left is not None else {},
         )
-        give, keep = results[:2]
+        give_near, give_far, keep = results[:3]
         if fresh:
-            left = results[2]
-        got = lax.ppermute(give, "space", cores)
-        sums = [keep, got]
+            left = results[3]
+        got = lax.ppermute(give_far, "space", cores)
+        sums = [keep, lax.ppermute(give_near, "space", cores)]
         for step in range(1, chips):
-            sent = (keep[step].astype(jnp.float32) + got[step].astype(jnp.float32)).astype(kind)
+            sent = (keep[step].astype(jnp.float32) + got[step - 1].astype(jnp.float32)).astype(kind)
             sums.append(send(sent, step, members))
         sents.append(sent)
         terms.append(sums)

time: 39.5 us -> 39.3 us (level)
  waiting for transfers between devices: 16.2 us -> 17.6 us
  Pallas kernels: 9.78 us -> 8.99 us
  starting transfers between devices: 12.2 us -> 11.6 us
    ppermute x4 -> x3, starting transfers between devices: 5.28 us -> 3.65 us  [send(): return lax.ppermute(array, 'space', route)]
    ppermute x4 -> x3, waiting for transfers between devices: 11.8 us -> 13.4 us  [send(): return lax.ppermute(array, 'space', route)]
    pallas_call x9 -> x7, Pallas kernels: 9.78 us -> 8.99 us  [call(): pl.pallas_call(kernel, in_specs=ins, out_specs=specs, out_shape=shapes, c...]
    ppermute x4 -> x6, starting transfers between devices: 0.77 us -> 1.27 us  [the longest x3 0.7 us: shards(): got = lax.ppermute(give_far, 'space', cores)]
    ppermute x3, starting transfers between devices: 6.14 us -> 6.63 us  [swap(): lax.ppermute(array, axis, [(i, peer(i, step, count)) for i in range(count)])]
  transfers between devices with their start and end apart: 11 -> 12, of which waited for: 7 -> 7; matrix products, arithmetic and copies ran while one was open for 1% -> 1% of each run, Pallas kernels for 21% -> 18%
where the time goes in v3:
time: 39.3 us; the launch traced here: 39.2 us
  waiting for transfers between devices  17.6 us (45%)
  starting transfers between devices  11.6 us (30%)
  Pallas kernels  8.99 us (23%)
  local copies, waits for them, and re-layouts  0.66 us (2%)
    ppermute x3, waiting for transfers between devices, send(): return lax.ppermute(array, 'space', route)  13.4 us
    pallas_call x7, Pallas kernels, call(): pl.pallas_call(kernel, in_specs=ins, out_specs=specs, out_shape=shapes, c...  8.99 us
    ppermute x3, starting transfers between devices, swap(): lax.ppermute(array, axis, [(i, peer(i, step, count)) for i in range(count)])  6.63 us
    ppermute x3, waiting for transfers between devices, swap(): lax.ppermute(array, axis, [(i, peer(i, step, count)) for i in range(count)])  3.89 us
    ppermute x3, starting transfers between devices, send(): return lax.ppermute(array, 'space', route)  3.65 us
  transfers between devices with their start and end apart: 12, of which 7 were waited for; matrix products, arithmetic and copies ran while one was open for 1% of the time, Pallas kernels for 18%

profile of v3, /device:TPU:0, one launch (start us, length us, event | category | flops | bytes accessed | tf_op | source)
XLA Modules:
  0.0 39.2 jit_solution(4850882143715180857)
XLA Ops:
  0.0 5.0 %collective-permute-start = (bf16[2,192,128]{2,1,0:T(8,128)(2,1)}, bf16[2,192,128]{2,1,0:T(8,128)(2,1)S(1)}, u32[]{:S(2)}, u32[]{:S(2)}) collective-permute-start(bf16[2,192,128]{2,1,0:T(8,128)(2,1)} %bitcast.9), channel_id=1, source_target_pairs={{0,12},{4,8},{8,4},{12,0},{1,13},{5,9},{9,5},{13,1},{2,14},{6,10},... | collective-permute-start | bytes 294920 | tf_op jit(solution)/shard_map/ppermute | solution.py:46
  5.1 0.0 collective-permute-start.2
  5.1 0.7 %copy-done.1 = s32[16,1]{0,1:T(1,128)S(1)} copy-done((s32[16,1]{0,1:T(1,128)S(1)}, s32[16,1]{0,1:T(1,128)}, u32[]{:S(2)}) %copy-start.1) | copy-done | bytes 88
  5.7 3.7 %shard_map.37 = (s32[16]{0:T(128)S(4)}, s32[16]{0:T(128)S(4)}, bf16[16,4,2,192,128]{4,3,2,1,0:T(8,128)(2,1)S(1)}) custom-call(s32[16]{0:T(128)S(1)} %bitcast.12, bf16[16,4,2,192,128]{4,3,2,1,0:T(8,128)(2,1)} %bitcast.13), custom_call_target="tpu_custom_call" | custom-call | flops 1 | bytes 1 | tf_op jit(solution)/shard_map/pallas_call | solution.py:51
  9.4 0.0 collective-permute-done.refs_2_
  9.4 0.9 %collective-permute-done.2.refs_1_ = bf16[2,192,128]{2,1,0:T(8,128)(2,1)S(1)} collective-permute-done((bf16[2,192,128]{2,1,0:T(8,128)(2,1)}, bf16[2,192,128]{2,1,0:T(8,128)(2,1)S(1)}, u32[]{:S(2)}, u32[]{:S(2)}) %collective-permute-start.2) | collective-permute-done | bytes 98336 | tf_op jit(solution)/shard_map/ppermute | solution.py:46
  10.3 0.9 %shard_map.38 = (bf16[1,4,4,64,128]{4,3,2,1,0:T(8,128)(2,1)S(1)}, bf16[1,4,4,64,128]{4,3,2,1,0:T(8,128)(2,1)S(1)}, bf16[2,4,4,64,128]{4,3,2,1,0:T(8,128)(2,1)S(1)}, bf16[4,256,384]{2,1,0:T(8,128)(2,1)S(1)}) custom-call(s32[16]{0:T(128)S(4)} %get-tuple-element.19.slot_ref, bf16[2,192,128]{2,1,0:T(8,128)(2,1)S(1)} %bitcast.11, ...), custom_call_target="tpu_custom_call" | custom-call | flops 1 | bytes 1 | tf_op jit(solution)/shard_map/pallas_call | solution.py:51
  11.2 0.1 collective-permute-start.10
  11.3 0.7 %shard_map.39 = (bf16[1,4,4,64,128]{4,3,2,1,0:T(8,128)(2,1)S(1)}, bf16[1,4,4,64,128]{4,3,2,1,0:T(8,128)(2,1)S(1)}, bf16[2,4,4,64,128]{4,3,2,1,0:T(8,128)(2,1)S(1)}) custom-call(s32[16]{0:T(128)S(4)} %get-tuple-element.19.slot_ref, bf16[16,4,2,192,128]{4,3,2,1,0:T(8,128)(2,1)S(1)} %get-tuple-element.20.refs_3_.refs_0_.refs_1_, ...), custom_call_target="tpu_custom_call" | custom-call | flops 1 | bytes 1 | tf_op jit(solution)/shard_map/pallas_call | solution.py:51
  12.0 0.6 %collective-permute-start.3 = (bf16[1,4,4,64,128]{4,3,2,1,0:T(8,128)(2,1)S(1)}, bf16[1,4,4,64,128]{4,3,2,1,0:T(8,128)(2,1)S(1)}, u32[]{:S(2)}, u32[]{:S(2)}) collective-permute-start(bf16[1,4,4,64,128]{4,3,2,1,0:T(8,128)(2,1)S(1)} %get-tuple-element.23), channel_id=1, source_target_pairs={{0,1},{1,0},{2,3},{3,2},{4,5},{5,4},{6,7},{7,6},{8,9},{9,8},{10,11... | collective-permute-start | bytes 786440 | tf_op jit(solution)/shard_map/ppermute | solution.py:231
  12.6 0.1 collective-permute-start.9
  12.7 0.2 collective-permute-done.10
  12.8 0.1 fusion.2
  12.9 1.6 %collective-permute-start.11 = (bf16[4,4,64,128]{3,2,1,0:T(8,128)(2,1)S(1)}, bf16[4,4,64,128]{3,2,1,0:T(8,128)(2,1)S(1)}, u32[]{:S(2)}, u32[]{:S(2)}) collective-permute-start(bf16[4,4,64,128]{3,2,1,0:T(8,128)(2,1)S(1)} %fusion.2), channel_id=1, source_target_pairs={{0,2},{1,3},{2,0},{3,1},{4,6},{5,7},{6,4},{7,5},{8,10},{9,11},{10,... | collective-permute-start | bytes 786440 | tf_op jit(solution)/shard_map/ppermute | solution.py:269
  14.5 1.6 %collective-permute-start.1 = (bf16[2,192,128]{2,1,0:T(8,128)(2,1)S(1)}, bf16[2,192,128]{2,1,0:T(8,128)(2,1)S(1)}, u32[]{:S(2)}, u32[]{:S(2)}) collective-permute-start(bf16[2,192,128]{2,1,0:T(8,128)(2,1)S(1)} %collective-permute-done.refs_2_), channel_id=1, source_target_pairs={{0,4},{4,0},{8,12},{12,8},{1,5},{5,1},{9,13},{13,9},{2,6},{6,2},{1... | collective-permute-start | bytes 294920 | tf_op jit(solution)/shard_map/ppermute | solution.py:46
  16.1 0.1 fusion.1.refs_3_
  16.2 0.6 %collective-permute-start.8 = (bf16[4,4,64,128]{3,2,1,0:T(8,128)(2,1)S(1)}, bf16[4,4,64,128]{3,2,1,0:T(8,128)(2,1)S(1)}, u32[]{:S(2)}, u32[]{:S(2)}) collective-permute-start(bf16[4,4,64,128]{3,2,1,0:T(8,128)(2,1)S(1)} %fusion.1.refs_3_), channel_id=1, source_target_pairs={{0,2},{1,3},{2,0},{3,1},{4,6},{5,7},{6,4},{7,5},{8,10},{9,11},{10,... | collective-permute-start | bytes 786440 | tf_op jit(solution)/shard_map/ppermute | solution.py:269
  16.8 3.0 %collective-permute-done.1.refs_0_ = bf16[2,192,128]{2,1,0:T(8,128)(2,1)S(1)} collective-permute-done((bf16[2,192,128]{2,1,0:T(8,128)(2,1)S(1)}, bf16[2,192,128]{2,1,0:T(8,128)(2,1)S(1)}, u32[]{:S(2)}, u32[]{:S(2)}) %collective-permute-start.1) | collective-permute-done | bytes 98336 | tf_op jit(solution)/shard_map/ppermute | solution.py:46
  19.7 1.3 %shard_map.40 = (bf16[1,8,4,64,128]{4,3,2,1,0:T(8,128)(2,1)S(1)}, bf16[1,8,4,64,128]{4,3,2,1,0:T(8,128)(2,1)S(1)}, bf16[2,8,4,64,128]{4,3,2,1,0:T(8,128)(2,1)S(1)}, bf16[4,256,384]{2,1,0:T(8,128)(2,1)S(1)}) custom-call(s32[16]{0:T(128)S(4)} %get-tuple-element.19.slot_ref, ...), custom_call_target="tpu_custom_call", output_to_operand_aliasing={{3}: (3, {})} | custom-call | flops 1 | bytes 1 | tf_op jit(solution)/shard_map/pallas_call | solution.py:51
  21.0 0.1 collective-permute-start.5
  21.1 0.5 %collective-permute-start.4 = (bf16[1,8,4,64,128]{4,3,2,1,0:T(8,128)(2,1)S(1)}, bf16[1,8,4,64,128]{4,3,2,1,0:T(8,128)(2,1)S(1)}, u32[]{:S(2)}, u32[]{:S(2)}) collective-permute-start(bf16[1,8,4,64,128]{4,3,2,1,0:T(8,128)(2,1)S(1)} %get-tuple-element.25), channel_id=1, source_target_pairs={{0,1},{1,0},{2,3},{3,2},{4,5},{5,4},{6,7},{7,6},{8,9},{9,8},{10,11... | collective-permute-start | bytes 1572872 | tf_op jit(solution)/shard_map/ppermute | solution.py:232
  21.6 0.5 %collective-permute-done.11.refs_2_ = bf16[4,4,64,128]{3,2,1,0:T(8,128)(2,1)S(1)} collective-permute-done((bf16[4,4,64,128]{3,2,1,0:T(8,128)(2,1)S(1)}, bf16[4,4,64,128]{3,2,1,0:T(8,128)(2,1)S(1)}, u32[]{:S(2)}, u32[]{:S(2)}) %collective-permute-start.11) | collective-permute-done | bytes 262176 | tf_op jit(solution)/shard_map/ppermute | solution.py:269
  22.1 0.8 %shard_map.41.refs_3_ = bf16[16,4,2,32,128]{4,3,2,1,0:T(8,128)(2,1)} custom-call(s32[16]{0:T(128)S(4)} %get-tuple-element.18.order_ref, bf16[2,4,4,64,128]{4,3,2,1,0:T(8,128)(2,1)S(1)} %get-tuple-element.28.refs_0_, bf16[1,4,4,64,128]{4,3,2,1,0:T(8,128)(2,1)S(1)} %collective-permute-done.9.refs_1_, bf16[4,4,64,128]{3,2,1,0:T(8,128)(2,1)S(1)} %collective-permute-done.11.refs_2_), custom_call_target="tpu_custom_call" | custom-call | flops 20000000000 | bytes 1 | tf_op jit(solution)/shard_map/pallas_call | solution.py:51
  22.9 0.1 collective-permute-done.5
  23.0 0.2 fusion
  23.2 1.5 %collective-permute-start.6 = (bf16[8,4,64,128]{3,2,1,0:T(8,128)(2,1)S(1)}, bf16[8,4,64,128]{3,2,1,0:T(8,128)(2,1)S(1)}, u32[]{:S(2)}, u32[]{:S(2)}) collective-permute-start(bf16[8,4,64,128]{3,2,1,0:T(8,128)(2,1)S(1)} %fusion), channel_id=1, source_target_pairs={{0,2},{1,3},{2,0},{3,1},{4,6},{5,7},{6,4},{7,5},{8,10},{9,11},{10,... | collective-permute-start | bytes 1572872 | tf_op jit(solution)/shard_map/ppermute | solution.py:269
  24.7 0.0 collective-permute-done.7.refs_1_
  24.7 3.1 %collective-permute-done.8.refs_2_ = bf16[4,4,64,128]{3,2,1,0:T(8,128)(2,1)S(1)} collective-permute-done((bf16[4,4,64,128]{3,2,1,0:T(8,128)(2,1)S(1)}, bf16[4,4,64,128]{3,2,1,0:T(8,128)(2,1)S(1)}, u32[]{:S(2)}, u32[]{:S(2)}) %collective-permute-start.8) | collective-permute-done | bytes 262176 | tf_op jit(solution)/shard_map/ppermute | solution.py:269
  27.7 0.8 %shard_map.42.refs_3_ = bf16[16,4,2,32,128]{4,3,2,1,0:T(8,128)(2,1)} custom-call(s32[16]{0:T(128)S(4)} %get-tuple-element.18.order_ref, bf16[2,4,4,64,128]{4,3,2,1,0:T(8,128)(2,1)S(1)} %get-tuple-element.22.refs_0_, bf16[1,4,4,64,128]{4,3,2,1,0:T(8,128)(2,1)S(1)} %collective-permute-done.7.refs_1_, ...), custom_call_target="tpu_custom_call", output_to_operand_aliasing={{}: (4, {})} | custom-call | flops 20000000000 | bytes 1 | tf_op jit(solution)/shard_map/pallas_call | solution.py:51
  28.5 0.0 collective-permute-done.4.refs_1_
  28.5 9.8 %collective-permute-done.6.refs_2_ = bf16[8,4,64,128]{3,2,1,0:T(8,128)(2,1)S(1)} collective-permute-done((bf16[8,4,64,128]{3,2,1,0:T(8,128)(2,1)S(1)}, bf16[8,4,64,128]{3,2,1,0:T(8,128)(2,1)S(1)}, u32[]{:S(2)}, u32[]{:S(2)}) %collective-permute-start.6) | collective-permute-done | bytes 524320 | tf_op jit(solution)/shard_map/ppermute | solution.py:269
  38.3 0.9 %shard_map.43 = bf16[16,4,2,32,128]{4,3,2,1,0:T(8,128)(2,1)} custom-call(s32[16]{0:T(128)S(4)} %get-tuple-element.18.order_ref, bf16[2,8,4,64,128]{4,3,2,1,0:T(8,128)(2,1)S(1)} %get-tuple-element.24.refs_0_, bf16[1,8,4,64,128]{4,3,2,1,0:T(8,128)(2,1)S(1)} %collective-permute-done.4.refs_1_, ...), custom_call_target="tpu_custom_call", output_to_operand_aliasing={{}: (4, {})} | custom-call | flops 20000000000 | bytes 1 | tf_op jit(solution)/shard_map/pallas_call | solution.py:51
  (6 shorter events, 0.0 us)
Async XLA Ops:
  0.0 10.3 %copy-start = (bf16[1,2,3,64,128]{4,3,2,1,0:T(8,128)(2,1)S(1)}, bf16[1,2,3,64,128]{4,3,2,1,0:T(8,128)(2,1)}, u32[]{:S(2)}) copy-start(bf16[1,2,3,64,128]{4,3,2,1,0:T(8,128)(2,1)} %param.4) | copy-start | bytes 294916
  0.0 9.4 %collective-permute-start = (bf16[2,192,128]{2,1,0:T(8,128)(2,1)}, bf16[2,192,128]{2,1,0:T(8,128)(2,1)S(1)}, u32[]{:S(2)}, u32[]{:S(2)}) collective-permute-start(bf16[2,192,128]{2,1,0:T(8,128)(2,1)} %bitcast.9), channel_id=1, source_target_pairs={{0,12},{4,8},{8,4},{12,0},{1,13},{5,9},{9,5},{13,1},{2,14},{6,10},... | collective-permute-start | bytes 294920 | tf_op jit(solution)/shard_map/ppermute | solution.py:46
  5.1 5.3 %collective-permute-start.2 = (bf16[2,192,128]{2,1,0:T(8,128)(2,1)}, bf16[2,192,128]{2,1,0:T(8,128)(2,1)S(1)}, u32[]{:S(2)}, u32[]{:S(2)}) collective-permute-start(bf16[2,192,128]{2,1,0:T(8,128)(2,1)} %bitcast.10), channel_id=1, source_target_pairs={{0,4},{4,0},{8,12},{12,8},{1,5},{5,1},{9,13},{13,9},{2,6},{6,2},{1... | collective-permute-start | bytes 294920 | tf_op jit(solution)/shard_map/ppermute | solution.py:46
  5.1 0.7 %copy-start.1 = (s32[16,1]{0,1:T(1,128)S(1)}, s32[16,1]{0,1:T(1,128)}, u32[]{:S(2)}) copy-start(s32[16,1]{0,1:T(1,128)} %param.5) | copy-start | bytes 196
  11.2 1.6 %collective-permute-start.10 = (bf16[1,4,4,64,128]{4,3,2,1,0:T(8,128)(2,1)S(1)}, bf16[1,4,4,64,128]{4,3,2,1,0:T(8,128)(2,1)S(1)}, u32[]{:S(2)}, u32[]{:S(2)}) collective-permute-start(bf16[1,4,4,64,128]{4,3,2,1,0:T(8,128)(2,1)S(1)} %get-tuple-element.30), channel_id=1, source_target_pairs={{0,1},{1,0},{2,3},{3,2},{4,5},{5,4},{6,7},{7,6},{8,9},{9,8},{10,11... | collective-permute-start | bytes 786440 | tf_op jit(solution)/shard_map/ppermute | solution.py:231
  12.0 4.1 %collective-permute-start.3 = (bf16[1,4,4,64,128]{4,3,2,1,0:T(8,128)(2,1)S(1)}, bf16[1,4,4,64,128]{4,3,2,1,0:T(8,128)(2,1)S(1)}, u32[]{:S(2)}, u32[]{:S(2)}) collective-permute-start(bf16[1,4,4,64,128]{4,3,2,1,0:T(8,128)(2,1)S(1)} %get-tuple-element.23), channel_id=1, source_target_pairs={{0,1},{1,0},{2,3},{3,2},{4,5},{5,4},{6,7},{7,6},{8,9},{9,8},{10,11... | collective-permute-start | bytes 786440 | tf_op jit(solution)/shard_map/ppermute | solution.py:231
  12.6 8.5 %collective-permute-start.9 = (bf16[1,4,4,64,128]{4,3,2,1,0:T(8,128)(2,1)S(1)}, bf16[1,4,4,64,128]{4,3,2,1,0:T(8,128)(2,1)S(1)}, u32[]{:S(2)}, u32[]{:S(2)}) collective-permute-start(bf16[1,4,4,64,128]{4,3,2,1,0:T(8,128)(2,1)S(1)} %get-tuple-element.29), channel_id=1, source_target_pairs={{0,1},{1,0},{2,3},{3,2},{4,5},{5,4},{6,7},{7,6},{8,9},{9,8},{10,11... | collective-permute-start | bytes 786440 | tf_op jit(solution)/shard_map/ppermute | solution.py:232
  12.9 9.2 %collective-permute-start.11 = (bf16[4,4,64,128]{3,2,1,0:T(8,128)(2,1)S(1)}, bf16[4,4,64,128]{3,2,1,0:T(8,128)(2,1)S(1)}, u32[]{:S(2)}, u32[]{:S(2)}) collective-permute-start(bf16[4,4,64,128]{3,2,1,0:T(8,128)(2,1)S(1)} %fusion.2), channel_id=1, source_target_pairs={{0,2},{1,3},{2,0},{3,1},{4,6},{5,7},{6,4},{7,5},{8,10},{9,11},{10,... | collective-permute-start | bytes 786440 | tf_op jit(solution)/shard_map/ppermute | solution.py:269
  14.5 10.2 %collective-permute-start.7 = (bf16[1,4,4,64,128]{4,3,2,1,0:T(8,128)(2,1)S(1)}, bf16[1,4,4,64,128]{4,3,2,1,0:T(8,128)(2,1)S(1)}, u32[]{:S(2)}, u32[]{:S(2)}) collective-permute-start(bf16[1,4,4,64,128]{4,3,2,1,0:T(8,128)(2,1)S(1)} %get-tuple-element.27), channel_id=1, source_target_pairs={{0,1},{1,0},{2,3},{3,2},{4,5},{5,4},{6,7},{7,6},{8,9},{9,8},{10,11... | collective-permute-start | bytes 786440 | tf_op jit(solution)/shard_map/ppermute | solution.py:232
  14.5 5.2 %collective-permute-start.1 = (bf16[2,192,128]{2,1,0:T(8,128)(2,1)S(1)}, bf16[2,192,128]{2,1,0:T(8,128)(2,1)S(1)}, u32[]{:S(2)}, u32[]{:S(2)}) collective-permute-start(bf16[2,192,128]{2,1,0:T(8,128)(2,1)S(1)} %collective-permute-done.refs_2_), channel_id=1, source_target_pairs={{0,4},{4,0},{8,12},{12,8},{1,5},{5,1},{9,13},{13,9},{2,6},{6,2},{1... | collective-permute-start | bytes 294920 | tf_op jit(solution)/shard_map/ppermute | solution.py:46
  16.2 11.6 %collective-permute-start.8 = (bf16[4,4,64,128]{3,2,1,0:T(8,128)(2,1)S(1)}, bf16[4,4,64,128]{3,2,1,0:T(8,128)(2,1)S(1)}, u32[]{:S(2)}, u32[]{:S(2)}) collective-permute-start(bf16[4,4,64,128]{3,2,1,0:T(8,128)(2,1)S(1)} %fusion.1.refs_3_), channel_id=1, source_target_pairs={{0,2},{1,3},{2,0},{3,1},{4,6},{5,7},{6,4},{7,5},{8,10},{9,11},{10,... | collective-permute-start | bytes 786440 | tf_op jit(solution)/shard_map/ppermute | solution.py:269
  21.0 2.0 %collective-permute-start.5 = (bf16[1,8,4,64,128]{4,3,2,1,0:T(8,128)(2,1)S(1)}, bf16[1,8,4,64,128]{4,3,2,1,0:T(8,128)(2,1)S(1)}, u32[]{:S(2)}, u32[]{:S(2)}) collective-permute-start(bf16[1,8,4,64,128]{4,3,2,1,0:T(8,128)(2,1)S(1)} %get-tuple-element.26), channel_id=1, source_target_pairs={{0,1},{1,0},{2,3},{3,2},{4,5},{5,4},{6,7},{7,6},{8,9},{9,8},{10,11... | collective-permute-start | bytes 1572872 | tf_op jit(solution)/shard_map/ppermute | solution.py:231
  21.1 7.4 %collective-permute-start.4 = (bf16[1,8,4,64,128]{4,3,2,1,0:T(8,128)(2,1)S(1)}, bf16[1,8,4,64,128]{4,3,2,1,0:T(8,128)(2,1)S(1)}, u32[]{:S(2)}, u32[]{:S(2)}) collective-permute-start(bf16[1,8,4,64,128]{4,3,2,1,0:T(8,128)(2,1)S(1)} %get-tuple-element.25), channel_id=1, source_target_pairs={{0,1},{1,0},{2,3},{3,2},{4,5},{5,4},{6,7},{7,6},{8,9},{9,8},{10,11... | collective-permute-start | bytes 1572872 | tf_op jit(solution)/shard_map/ppermute | solution.py:232
  23.2 15.1 %collective-permute-start.6 = (bf16[8,4,64,128]{3,2,1,0:T(8,128)(2,1)S(1)}, bf16[8,4,64,128]{3,2,1,0:T(8,128)(2,1)S(1)}, u32[]{:S(2)}, u32[]{:S(2)}) collective-permute-start(bf16[8,4,64,128]{3,2,1,0:T(8,128)(2,1)S(1)} %fusion), channel_id=1, source_target_pairs={{0,2},{1,3},{2,0},{3,1},{4,6},{5,7},{6,4},{7,5},{8,10},{9,11},{10,... | collective-permute-start | bytes 1572872 | tf_op jit(solution)/shard_map/ppermute | solution.py:269

commit v4 on v3

v4 whole, which is shorter than its diff:
```python
import functools

import jax
import jax.numpy as jnp
from jax import lax
from jax.experimental import pallas as pl
from jax.experimental.pallas import tpu as pltpu
from jax.sharding import PartitionSpec as P

SHARES = (4, 4, 8)
AFTER = (None, None, 1)
HOME_AFTER = 2
HOMES_BEFORE = 2
RELAY_AFTER = 0
SMEM = pl.BlockSpec(memory_space=pltpu.SMEM)
VMEM = pl.BlockSpec(memory_space=pltpu.VMEM)
HBM = pl.BlockSpec(memory_space=pltpu.HBM)
ANY = pl.BlockSpec(memory_space=pl.ANY)
LITTLE = pl.CostEstimate(flops=1, bytes_accessed=1, transcendentals=0)
MUCH = pl.CostEstimate(flops=20_000_000_000, bytes_accessed=1, transcendentals=0)
PARAMS = pltpu.CompilerParams(vmem_limit_bytes=16 * 1024 * 1024)


def near(array):
    return pltpu.with_memory_space_constraint(array, pltpu.VMEM)


def far(array):
    return pltpu.with_memory_space_constraint(array, pltpu.HBM)


def scalars(array):
    return pltpu.with_memory_space_constraint(array, pltpu.SMEM)


def in_pairs(count):
    return count & (count - 1) == 0


def peer(index, step, count):
    return index ^ step if in_pairs(count) else (index + step) % count


def apart(here, there, count):
    return here ^ there if in_pairs(count) else lax.rem(there - here + count, count)


def swap(array, axis, step, count):
    return lax.ppermute(array, axis, [(i, peer(i, step, count)) for i in range(count)])


def send(array, step, members):
    route = [(i, peer(i // 2, step, members // 2) * 2 + i % 2) for i in range(members)]
    return lax.ppermute(array, "space", route)


def call(kernel, ins, outs, operands, cost=LITTLE, **more):
    specs, shapes = zip(*outs)
    return pl.pallas_call(
        kernel,
        in_specs=ins,
        out_specs=specs,
        out_shape=shapes,
        cost_estimate=cost,
        compiler_params=PARAMS,
        **more,
    )(*operands)


def interleave(real, imag):
    whole = real.shape[0] // 128 * 128
    pieces = [real[:whole], imag[:whole], real[whole:], imag[whole:]]
    return jnp.concatenate([p for p in pieces if p.shape[0]], axis=0)


def quarter_turn(rows):
    whole = rows.shape[1] // 256 * 128
    edge = 2 * whole + (rows.shape[1] - 2 * whole) // 2
    pieces = [-rows[:, whole : 2 * whole], rows[:, :whole], -rows[:, edge:], rows[:, 2 * whole : edge]]
    return jnp.concatenate([p for p in pieces if p.shape[1]], axis=1)


def lay(chips, rows, source_ref, away_ref, home_ref, vector_ref, sem):
    copy = pltpu.make_async_copy(source_ref, vector_ref, sem)
    copy.start()
    copy.wait()
    turned = interleave(vector_ref[0], vector_ref[1]).T
    chip = lax.axis_index("space") // 2
    for to_chip in range(chips):
        part = turned[to_chip * rows : (to_chip + 1) * rows]
        step = apart(chip, to_chip, chips)

        @pl.when(step == 0)
        def _():
            home_ref[...] = part

        @pl.when(step > 0)
        def _():
            away_ref[jnp.maximum(step, 1) - 1] = part


def load(steps, first, source_ref, data_ref, order_ref, slot_ref, held_ref, times_ref, times_sem, sem):
    blocks = times_ref.shape[0]
    half = held_ref.shape[0]
    count = len(steps)
    here = lax.axis_index("tm")
    times = pltpu.make_async_copy(source_ref, times_ref, times_sem)
    times.start()
    times.wait()

    def copy(block, at):
        return pltpu.make_async_copy(data_ref.at[block], held_ref.at[at], sem.at[at])

    low, high = jnp.int32(0), jnp.int32(blocks - 1)
    for i in range(blocks):
        step = apart(times_ref[i], here, count)
        slot = jnp.int32(0)
        for at, value in enumerate(steps):
            slot = jnp.where(step == value, at, slot)
        early = slot < first
        where = jnp.where(early, low, high)
        order_ref[where] = i
        slot_ref[where] = slot
        pl.when(early & (low < half))(copy(i, jnp.minimum(low, half - 1)).start)
        one = early.astype(jnp.int32)
        low, high = low + one, high - 1 + one
    for at in range(half):
        copy(order_ref[at], at).wait()


def fill(width, rows, left_ref, slot, first_step, vector):
    core = lax.axis_index("space") % 2
    steps = left_ref.shape[1] // (2 * rows)
    for part, block in enumerate((vector, quarter_turn(vector))):
        for to_core in range(2):
            stays = (core == to_core).astype(jnp.int32)
            at = ((stays * steps + first_step) * 2 + part) * width
            left_ref[slot, pl.ds(pl.multiple_of(at, width), width), :] = block[
                to_core * width : (to_core + 1) * width
            ]


def multiply(left, block_ref, give_ref, keep_ref, i):
    spins, columns = block_ref.shape[0], block_ref.shape[-1]
    for spin in range(0, spins, 2):
        right = jnp.concatenate(
            [interleave(block_ref[s, 0], block_ref[s, 1]) for s in range(spin, spin + 2)], axis=1
        )
        result = jnp.dot(left, right, preferred_element_type=jnp.float32).astype(give_ref.dtype)
        for s in range(2):
            side = result[:, s * columns : (s + 1) * columns]
            parts = side.reshape(2, give_ref.shape[0], -1, columns)
            give_ref[:, i, spin + s] = parts[0]
            keep_ref[:, i, spin + s] = parts[1]


def project_away(width, rows, start, known, fresh, fetch, whole, order_ref, slot_ref, *refs):
    vector_refs, source_ref = refs[:fresh], refs[fresh]
    refs = list(refs)
    sem = refs.pop() if fetch else None
    whole_ref = refs.pop() if whole else None
    left_ref = refs.pop() if fresh else refs[fresh + 1]
    held_ref, base = (refs.pop(), 0) if fetch else (source_ref, start)
    give_ref, keep_ref = refs[-2:]
    size = give_ref.shape[1]

    def copy(i):
        return pltpu.make_async_copy(source_ref.at[order_ref[start + i]], held_ref.at[i], sem.at[i])

    if fetch:
        for i in range(size):
            copy(i).start()
    for slot, ref in enumerate(vector_refs):
        if known + slot == whole:
            chips = whole_ref.shape[0]
            chip = lax.axis_index("space") // 2
            turned = interleave(ref[0], ref[1]).T
            for to_chip in range(chips):
                whole_ref[apart(chip, to_chip, chips)] = turned[to_chip * rows : (to_chip + 1) * rows]
            ref = whole_ref.at[pl.ds(1, chips - 1)]
        for step in range(ref.shape[0]):
            fill(width, rows, left_ref, known + slot, step, ref[step])
    for i in range(size):
        if fetch:
            copy(i).wait()
        multiply(left_ref[slot_ref[start + i]], held_ref.at[base + i], give_ref, keep_ref, i)


def project_home(width, rows, slot_ref, *refs):
    give_ref, keep_ref, left_ref = refs[-3:]
    times = left_ref.shape[0]
    for slot, ref in enumerate(refs[:times]):
        fill(width, rows, left_ref, slot, 0, ref[0] if len(ref.shape) == 3 else ref[...])
    at = 0
    for held_ref in refs[times:-4]:
        for i in range(held_ref.shape[0]):
            multiply(left_ref[slot_ref[at]], held_ref.at[i], give_ref, keep_ref, at)
            at += 1


def mark(*refs):
    refs[-1][0] = 0


def relay(from_ref, _, to_ref):
    to_ref[...] = from_ref[...]


def finish(start, size, terms, order_ref, *refs):
    out_ref, stage_ref, sem = refs[-3:]

    def copy(i):
        return pltpu.make_async_copy(stage_ref.at[i], out_ref.at[order_ref[start + i]], sem.at[i])

    for i in range(size):
        total = None
        for ref in refs[:terms]:
            term = ref[i] if len(ref.shape) == 4 else ref[0, start + i]
            term = term.astype(jnp.float32)
            total = term if total is None else total + term
        stage_ref[i] = total.reshape(stage_ref.shape[1:]).astype(stage_ref.dtype)
        copy(i).start()
    for i in range(size):
        copy(i).wait()


def shards(solutions, eigvecs, sink_time):
    blocks, spins, _, colours, sites, columns = solutions.shape
    times = lax.axis_size("tm")
    members = lax.axis_size("space")
    chips = members // 2
    width = eigvecs.shape[-1] // members
    rows = 2 * width
    depth = 2 * colours * sites
    kind = solutions.dtype
    cores = [(i, i ^ 1) for i in range(members)]

    most = max(2, (2 * blocks + times - 1) // times)
    half = blocks // 2
    late = half // most
    first = times - late
    steps = [0] + list(range(1, times, 2)) + list(range(2, times, 2))

    own = eigvecs[0].reshape(2, colours * sites, -1)
    data = far(solutions.reshape(blocks, spins, 2, colours * sites, columns))
    away_kind = (VMEM, pltpu.VMEM((chips - 1, rows, depth), kind))
    all_kind = (VMEM, pltpu.VMEM((chips, rows, depth), kind))
    home_kind = (VMEM, pltpu.VMEM((rows, depth), kind))
    away, home = call(
        functools.partial(lay, chips, rows),
        [HBM],
        [away_kind, home_kind],
        [far(own)],
        scratch_shapes=[pltpu.VMEM(own.shape, kind), pltpu.SemaphoreType.DMA],
    )
    aways = [away] + [
        swap(own if step == steps[1] else away, "tm", step, times) for step in steps[1:first]
    ]

    sizes = [share * blocks // 16 for share in SHARES]
    numbers = (SMEM, pltpu.SMEM((blocks,), jnp.int32))

    def holding(size):
        return (VMEM, pltpu.VMEM((size, *data.shape[1:]), kind))

    def sums(count, size):
        return (VMEM, pltpu.VMEM((count, size, spins, rows, columns), kind))

    order, slots, held = call(
        functools.partial(load, steps, first),
        [HBM, HBM],
        [numbers, numbers, holding(half)],
        [far(sink_time[:, 0]), data],
        scratch_shapes=[
            pltpu.SMEM((blocks,), jnp.int32),
            pltpu.SemaphoreType.DMA,
            pltpu.SemaphoreType.DMA((half,)),
        ],
    )
    order, slots = scalars(order), scalars(slots)
    for step in steps[first:]:
        through = in_pairs(times) and steps.index(step ^ 1) < first
        aways.append(swap(aways[steps.index(step ^ 1)], "tm", 1, times) if through else swap(away, "tm", step, times))

    lefts = (VMEM, pltpu.VMEM((times, 2 * (chips - 1) * rows, depth), kind))
    left = None
    helds, sents, terms = [near(held)], [], []
    known = start = 0
    for at, size in enumerate(sizes):
        wanted = first if start + size <= half else times
        fresh = [near(a) for a in aways[known:wanted]]
        after = [] if AFTER[at] is None else [sents[AFTER[at]]]
        if at == HOMES_BEFORE:
            (home,) = call(relay, [VMEM, ANY], [home_kind], [near(home), sents[RELAY_AFTER]])
            homes = [home, nearest] + [swap(home, "tm", step, times) for step in steps[2:]]
        fetch = start >= half
        operands = [*fresh, data if fetch else helds[0]]
        ins = [VMEM] * len(fresh) + [HBM if fetch else VMEM]
        if left is not None:
            operands.append(near(left))
            ins.append(VMEM)
        outs = [sums(chips - 1, size)] * 2
        if fetch:
            outs.append(holding(size))
        if fresh:
            outs.append(lefts)
        whole = not start
        if whole:
            outs.append(all_kind)
        results = call(
            functools.partial(project_away, width, rows, start, known, len(fresh), fetch, int(whole)),
            [SMEM] * 2 + ins + [ANY] * len(after),
            outs,
            [order, slots, *operands, *after],
            scratch_shapes=[pltpu.SemaphoreType.DMA((size,))] if fetch else [],
            input_output_aliases={len(operands) + 1: len(outs) - 1} if fresh and left is not None else {},
        )
        give, keep = results[:2]
        if fetch:
            helds.append(near(results[2]))
        if fresh:
            left = results[2 + fetch]
        if whole:
            nearest = near(results[-1])
        got = lax.ppermute(give, "space", cores)
        arrived = []
        for step in range(1, chips):
            sent = keep[step - 1].astype(jnp.float32) + got[step - 1].astype(jnp.float32)
            sent = sent.astype(kind)
            arrived.append(send(sent, step, members))
        sents.append(sent)
        terms.append((start, size, arrived))
        known = wanted
        start += size

    give, keep = call(
        functools.partial(project_home, width, rows),
        [SMEM] + [VMEM] * (times + len(helds)) + [ANY],
        [sums(1, blocks)] * 2,
        [slots, *[near(h) for h in homes], *helds, sents[HOME_AFTER]],
        scratch_shapes=[pltpu.VMEM((times, 2 * rows, depth), kind)],
    )
    got = lax.ppermute(give, "space", cores)

    token = []
    for _, _, arrived in terms[:-1]:
        token = call(
            mark, [ANY] * (1 + len(token)), [(SMEM, pltpu.SMEM((1,), jnp.int32))], [arrived[-1], *token], MUCH
        )
    result = None
    for start, size, arrived in terms:
        arrays = [keep, got, *arrived]
        operands = [order, *[near(a) for a in arrays]]
        ins = [SMEM] + [VMEM] * len(arrays)
        aliases = {}
        if result is not None:
            aliases = {len(operands): 0}
            operands.append(result)
            ins.append(HBM)
        else:
            operands += token
            ins += [ANY] * len(token)
        (result,) = call(
            functools.partial(finish, start, size, len(arrays)),
            ins,
            [(HBM, jax.ShapeDtypeStruct((blocks, spins, 2, width, columns), kind))],
            operands,
            LITTLE,
            scratch_shapes=[
                pltpu.VMEM((size, spins, 2, width, columns), kind),
                pltpu.SemaphoreType.DMA((size,)),
            ],
            input_output_aliases=aliases,
        )
    return result


def solution(mesh):
    in_specs = (
        P(("grp", "tm"), None, None, None, "space", None),
        P("tm", None, None, "space", None),
        P(("grp", "tm"), None),
    )
    out_specs = P(("grp", "tm"), None, None, "space", None)
    return jax.shard_map(shards, mesh=mesh, in_specs=in_specs, out_specs=out_specs, check_vma=False)
```

time: 39.3 us -> 38.6 us (0.982)
  waiting for transfers between devices: 17.6 us -> 13.1 us
  Pallas kernels: 8.99 us -> 11.3 us
  starting transfers between devices: 11.6 us -> 13.5 us
  local copies, waits for them, and re-layouts: 0.66 us -> 0 us
    ppermute x3, waiting for transfers between devices: 13.4 us -> 8.15 us  [send(): return lax.ppermute(array, 'space', route)]
    ppermute x6 -> x4, waiting for transfers between devices: 0.31 us -> 4.14 us  [shards(): got = lax.ppermute(give, 'space', cores)]
    ppermute x3 -> x5, waiting for transfers between devices: 3.89 us -> 0.82 us  [swap(): lax.ppermute(array, axis, [(i, peer(i, step, count)) for i in range(count)])]
    ppermute x3 -> x5, starting transfers between devices: 6.63 us -> 9.05 us  [swap(): lax.ppermute(array, axis, [(i, peer(i, step, count)) for i in range(count)])]
    pallas_call x7 -> x12, Pallas kernels: 8.99 us -> 11.3 us  [call(): pl.pallas_call(kernel, in_specs=ins, out_specs=specs, out_shape=shapes, c...]
    unnamed x4 -> x0, local copies, waits for them, and re-layouts: 0.66 us -> none
    ppermute x6 -> x4, starting transfers between devices: 1.27 us -> 0.77 us  [shards(): got = lax.ppermute(give, 'space', cores)]
  transfers between devices with their start and end apart: 12 -> 12, of which waited for: 7 -> 7; matrix products, arithmetic and copies ran while one was open for 1% -> 1% of each run, Pallas kernels for 18% -> 26%
where the time goes in v4:
time: 38.6 us; the launch traced here: 38.4 us
  starting transfers between devices  13.5 us (35%)
  waiting for transfers between devices  13.1 us (34%)
  Pallas kernels  11.3 us (29%)
    pallas_call x12, Pallas kernels, call(): pl.pallas_call(kernel, in_specs=ins, out_specs=specs, out_shape=shapes, c...  11.3 us
    ppermute x5, starting transfers between devices, swap(): lax.ppermute(array, axis, [(i, peer(i, step, count)) for i in range(count)])  9.05 us
    ppermute x3, waiting for transfers between devices, send(): return lax.ppermute(array, 'space', route)  8.15 us
    ppermute x4, waiting for transfers between devices, shards(): got = lax.ppermute(give, 'space', cores)  4.14 us
    ppermute x3, starting transfers between devices, send(): return lax.ppermute(array, 'space', route)  3.72 us
    ppermute x5, waiting for transfers between devices, swap(): lax.ppermute(array, axis, [(i, peer(i, step, count)) for i in range(count)])  0.82 us
    ppermute x4, starting transfers between devices, shards(): got = lax.ppermute(give, 'space', cores)  0.77 us
  transfers between devices with their start and end apart: 12, of which 7 were waited for; matrix products, arithmetic and copies ran while one was open for 1% of the time, Pallas kernels for 26%

profile of v4, /device:TPU:0, one launch (start us, length us, event | category | flops | bytes accessed | tf_op | source)
XLA Modules:
  0.0 38.4 jit_solution(14536068747251481500)
XLA Ops:
  0.0 3.0 %collective-permute-start = (bf16[2,192,128]{2,1,0:T(8,128)(2,1)}, bf16[2,192,128]{2,1,0:T(8,128)(2,1)S(1)}, u32[]{:S(2)}, u32[]{:S(2)}) collective-permute-start(bf16[2,192,128]{2,1,0:T(8,128)(2,1)} %bitcast.11), channel_id=1, source_target_pairs={{0,4},{4,0},{8,12},{12,8},{1,5},{5,1},{9,13},{13,9},{2,6},{6,2},{1... | collective-permute-start | bytes 294920 | tf_op jit(solution)/shard_map/ppermute | solution.py:49
  3.0 1.0 %shard_map.38 = (bf16[1,64,384]{2,1,0:T(8,128)(2,1)S(1)}, bf16[64,384]{1,0:T(8,128)(2,1)S(1)}) custom-call(bf16[2,192,128]{2,1,0:T(8,128)(2,1)} %bitcast.12), custom_call_target="tpu_custom_call" | custom-call | flops 1 | bytes 1 | tf_op jit(solution)/shard_map/pallas_call | solution.py:59
  4.1 2.5 %collective-permute-start.1 = (bf16[1,64,384]{2,1,0:T(8,128)(2,1)S(1)}, bf16[1,64,384]{2,1,0:T(8,128)(2,1)S(1)}, u32[]{:S(2)}, u32[]{:S(2)}) collective-permute-start(bf16[1,64,384]{2,1,0:T(8,128)(2,1)S(1)} %get-tuple-element.24.refs_0_), channel_id=1, source_target_pairs={{0,12},{4,8},{8,4},{12,0},{1,13},{5,9},{9,5},{13,1},{2,14},{6,10},... | collective-permute-start | bytes 147464 | tf_op jit(solution)/shard_map/ppermute | solution.py:49
  6.6 2.6 %shard_map.37 = (s32[16]{0:T(128)S(4)}, s32[16]{0:T(128)S(4)}, bf16[8,4,2,192,128]{4,3,2,1,0:T(8,128)(2,1)S(1)}) custom-call(s32[16]{0:T(128)} %bitcast.13, bf16[16,4,2,192,128]{4,3,2,1,0:T(8,128)(2,1)} %bitcast.9), custom_call_target="tpu_custom_call" | custom-call | flops 1 | bytes 1 | tf_op jit(solution)/shard_map/pallas_call | solution.py:59
  9.2 0.8 %collective-permute-done.1.refs_2_ = bf16[1,64,384]{2,1,0:T(8,128)(2,1)S(1)} collective-permute-done((bf16[1,64,384]{2,1,0:T(8,128)(2,1)S(1)}, bf16[1,64,384]{2,1,0:T(8,128)(2,1)S(1)}, u32[]{:S(2)}, u32[]{:S(2)}) %collective-permute-start.1) | collective-permute-done | bytes 49184 | tf_op jit(solution)/shard_map/ppermute | solution.py:49
  10.0 0.0 collective-permute-done.refs_1_
  10.0 0.6 %shard_map.39 = (bf16[1,4,4,64,128]{4,3,2,1,0:T(8,128)(2,1)S(1)}, bf16[1,4,4,64,128]{4,3,2,1,0:T(8,128)(2,1)S(1)}, bf16[4,128,384]{2,1,0:T(8,128)(2,1)S(1)}, bf16[2,64,384]{2,1,0:T(8,128)(2,1)S(1)}) custom-call(s32[16]{0:T(128)S(4)} %get-tuple-element.21.order_ref, s32[16]{0:T(128)S(4)} %get-tuple-element.22.slot_ref, ...), custom_call_target="tpu_custom_call" | custom-call | flops 1 | bytes 1 | tf_op jit(solution)/shard_map/pallas_call | solution.py:59
  10.6 0.1 collective-permute-start.2
  10.7 0.4 %shard_map.41 = (bf16[1,4,4,64,128]{4,3,2,1,0:T(8,128)(2,1)S(1)}, bf16[1,4,4,64,128]{4,3,2,1,0:T(8,128)(2,1)S(1)}) custom-call(s32[16]{0:T(128)S(4)} %get-tuple-element.21.order_ref, s32[16]{0:T(128)S(4)} %get-tuple-element.22.slot_ref, bf16[8,4,2,192,128]{4,3,2,1,0:T(8,128)(2,1)S(1)} %get-tuple-element.25.refs_3_.refs_0_.refs_4_, ...), custom_call_target="tpu_custom_call" | custom-call | flops 1 | bytes 1 | tf_op jit(solution)/shard_map/pallas_call | solution.py:59
  11.1 0.6 %collective-permute-start.6 = (bf16[1,4,4,64,128]{4,3,2,1,0:T(8,128)(2,1)S(1)}, bf16[1,4,4,64,128]{4,3,2,1,0:T(8,128)(2,1)S(1)}, u32[]{:S(2)}, u32[]{:S(2)}) collective-permute-start(bf16[1,4,4,64,128]{4,3,2,1,0:T(8,128)(2,1)S(1)} %get-tuple-element.31), channel_id=1, source_target_pairs={{0,1},{1,0},{2,3},{3,2},{4,5},{5,4},{6,7},{7,6},{8,9},{9,8},{10,11... | collective-permute-start | bytes 786440 | tf_op jit(solution)/shard_map/ppermute | solution.py:325
  11.7 0.5 %collective-permute-done.2 = bf16[1,4,4,64,128]{4,3,2,1,0:T(8,128)(2,1)S(1)} collective-permute-done((bf16[1,4,4,64,128]{4,3,2,1,0:T(8,128)(2,1)S(1)}, bf16[1,4,4,64,128]{4,3,2,1,0:T(8,128)(2,1)S(1)}, u32[]{:S(2)}, u32[]{:S(2)}) %collective-permute-start.2) | collective-permute-done | bytes 262176 | tf_op jit(solution)/shard_map/ppermute | solution.py:325
  12.2 0.1 fusion.1._
  12.3 1.6 %collective-permute-start.11 = (bf16[4,4,64,128]{3,2,1,0:T(8,128)(2,1)S(1)}, bf16[4,4,64,128]{3,2,1,0:T(8,128)(2,1)S(1)}, u32[]{:S(2)}, u32[]{:S(2)}) collective-permute-start(bf16[4,4,64,128]{3,2,1,0:T(8,128)(2,1)S(1)} %fusion.1._), channel_id=1, source_target_pairs={{0,2},{1,3},{2,0},{3,1},{4,6},{5,7},{6,4},{7,5},{8,10},{9,11},{10,... | collective-permute-start | bytes 786440 | tf_op jit(solution)/shard_map/ppermute | solution.py:54
  13.8 0.0 collective-permute-start.5
  13.9 2.5 %collective-permute-start.3 = (bf16[64,384]{1,0:T(8,128)(2,1)S(1)}, bf16[64,384]{1,0:T(8,128)(2,1)S(1)}, u32[]{:S(2)}, u32[]{:S(2)}) collective-permute-start(bf16[64,384]{1,0:T(8,128)(2,1)S(1)} %shard_map.40.refs_0_), channel_id=1, source_target_pairs={{0,12},{4,8},{8,4},{12,0},{1,13},{5,9},{9,5},{13,1},{2,14},{6,10},... | collective-permute-start | bytes 147464 | tf_op jit(solution)/shard_map/ppermute | solution.py:49
  16.4 0.9 %collective-permute-start.4 = (bf16[64,384]{1,0:T(8,128)(2,1)S(1)}, bf16[64,384]{1,0:T(8,128)(2,1)S(1)}, u32[]{:S(2)}, u32[]{:S(2)}) collective-permute-start(bf16[64,384]{1,0:T(8,128)(2,1)S(1)} %shard_map.40.refs_0_), channel_id=1, source_target_pairs={{0,8},{4,12},{8,0},{12,4},{1,9},{5,13},{9,1},{13,5},{2,10},{6,14},... | collective-permute-start | bytes 147464 | tf_op jit(solution)/shard_map/ppermute | solution.py:49
  17.3 0.1 fusion.2.refs_3_
  17.4 0.6 %collective-permute-start.10 = (bf16[4,4,64,128]{3,2,1,0:T(8,128)(2,1)S(1)}, bf16[4,4,64,128]{3,2,1,0:T(8,128)(2,1)S(1)}, u32[]{:S(2)}, u32[]{:S(2)}) collective-permute-start(bf16[4,4,64,128]{3,2,1,0:T(8,128)(2,1)S(1)} %fusion.2.refs_3_), channel_id=1, source_target_pairs={{0,2},{1,3},{2,0},{3,1},{4,6},{5,7},{6,4},{7,5},{8,10},{9,11},{10,... | collective-permute-start | bytes 786440 | tf_op jit(solution)/shard_map/ppermute | solution.py:54
  18.0 3.0 %shard_map.42 = (bf16[1,8,4,64,128]{4,3,2,1,0:T(8,128)(2,1)S(1)}, bf16[1,8,4,64,128]{4,3,2,1,0:T(8,128)(2,1)S(1)}, bf16[8,4,2,192,128]{4,3,2,1,0:T(8,128)(2,1)S(1)}, bf16[4,128,384]{2,1,0:T(8,128)(2,1)S(1)}) custom-call(s32[16]{0:T(128)S(4)} %get-tuple-element.21.order_ref, s32[16]{0:T(128)S(4)} %get-tuple-element.22.slot_ref, ...), custom_call_target="tpu_custom_call", output_to_operand_aliasing={{3}: (4, {})} | custom-call | flops 1 | bytes 1 | tf_op jit(solution)/shard_map/pallas_call | solution.py:59
  21.0 0.1 collective-permute-start.7
  21.1 0.4 %collective-permute-done.11.refs_0_.refs_2_ = bf16[4,4,64,128]{3,2,1,0:T(8,128)(2,1)S(1)} collective-permute-done((bf16[4,4,64,128]{3,2,1,0:T(8,128)(2,1)S(1)}, bf16[4,4,64,128]{3,2,1,0:T(8,128)(2,1)S(1)}, u32[]{:S(2)}, u32[]{:S(2)}) %collective-permute-start.11) | collective-permute-done | bytes 262176 | tf_op jit(solution)/shard_map/ppermute | solution.py:54
  21.5 1.5 %collective-permute-done.7 = bf16[1,8,4,64,128]{4,3,2,1,0:T(8,128)(2,1)S(1)} collective-permute-done((bf16[1,8,4,64,128]{4,3,2,1,0:T(8,128)(2,1)S(1)}, bf16[1,8,4,64,128]{4,3,2,1,0:T(8,128)(2,1)S(1)}, u32[]{:S(2)}, u32[]{:S(2)}) %collective-permute-start.7) | collective-permute-done | bytes 524320 | tf_op jit(solution)/shard_map/ppermute | solution.py:325
  23.0 0.2 fusion.refs_6_
  23.2 1.6 %collective-permute-start.9 = (bf16[8,4,64,128]{3,2,1,0:T(8,128)(2,1)S(1)}, bf16[8,4,64,128]{3,2,1,0:T(8,128)(2,1)S(1)}, u32[]{:S(2)}, u32[]{:S(2)}) collective-permute-start(bf16[8,4,64,128]{3,2,1,0:T(8,128)(2,1)S(1)} %fusion.refs_6_), channel_id=1, source_target_pairs={{0,2},{1,3},{2,0},{3,1},{4,6},{5,7},{6,4},{7,5},{8,10},{9,11},{10,... | collective-permute-start | bytes 1572872 | tf_op jit(solution)/shard_map/ppermute | solution.py:54
  24.7 1.3 %shard_map.43 = (bf16[1,16,4,64,128]{4,3,2,1,0:T(8,128)(2,1)S(1)}, bf16[1,16,4,64,128]{4,3,2,1,0:T(8,128)(2,1)S(1)}) custom-call(s32[16]{0:T(128)S(4)} %get-tuple-element.22.slot_ref, bf16[64,384]{1,0:T(8,128)(2,1)S(1)} %shard_map.40.refs_0_, bf16[2,64,384]{2,1,0:T(8,128)(2,1)S(1)} %get-tuple-element.28.refs_1_, ...), custom_call_target="tpu_custom_call" | custom-call | flops 1 | bytes 1 | tf_op jit(solution)/shard_map/pallas_call | solution.py:59
  26.1 0.1 collective-permute-start.8
  26.1 0.5 %collective-permute-done.10.refs_0_.refs_2_ = bf16[4,4,64,128]{3,2,1,0:T(8,128)(2,1)S(1)} collective-permute-done((bf16[4,4,64,128]{3,2,1,0:T(8,128)(2,1)S(1)}, bf16[4,4,64,128]{3,2,1,0:T(8,128)(2,1)S(1)}, u32[]{:S(2)}, u32[]{:S(2)}) %collective-permute-start.10) | collective-permute-done | bytes 262176 | tf_op jit(solution)/shard_map/ppermute | solution.py:54
  26.6 2.2 %collective-permute-done.8.refs_1_ = bf16[1,16,4,64,128]{4,3,2,1,0:T(8,128)(2,1)S(1)} collective-permute-done((bf16[1,16,4,64,128]{4,3,2,1,0:T(8,128)(2,1)S(1)}, bf16[1,16,4,64,128]{4,3,2,1,0:T(8,128)(2,1)S(1)}, u32[]{:S(2)}, u32[]{:S(2)}) %collective-permute-start.8) | collective-permute-done | bytes 1048608 | tf_op jit(solution)/shard_map/ppermute | solution.py:343
  28.8 0.8 %shard_map.46.refs_3_ = bf16[16,4,2,32,128]{4,3,2,1,0:T(8,128)(2,1)} custom-call(s32[16]{0:T(128)S(4)} %get-tuple-element.21.order_ref, bf16[1,16,4,64,128]{4,3,2,1,0:T(8,128)(2,1)S(1)} %get-tuple-element.35.refs_0_, bf16[1,16,4,64,128]{4,3,2,1,0:T(8,128)(2,1)S(1)} %collective-permute-done.8.refs_1_, ...), custom_call_target="tpu_custom_call" | custom-call | flops 1 | bytes 1 | tf_op jit(solution)/shard_map/pallas_call | solution.py:59
  29.6 0.8 %shard_map.47.refs_3_ = bf16[16,4,2,32,128]{4,3,2,1,0:T(8,128)(2,1)} custom-call(s32[16]{0:T(128)S(4)} %get-tuple-element.21.order_ref, bf16[1,16,4,64,128]{4,3,2,1,0:T(8,128)(2,1)S(1)} %get-tuple-element.35.refs_0_, bf16[1,16,4,64,128]{4,3,2,1,0:T(8,128)(2,1)S(1)} %collective-permute-done.8.refs_1_, ...), custom_call_target="tpu_custom_call", output_to_operand_aliasing={{}: (4, {})} | custom-call | flops 1 | bytes 1 | tf_op jit(solution)/shard_map/pallas_call | solution.py:59
  30.3 7.2 %collective-permute-done.9.refs_2_ = bf16[8,4,64,128]{3,2,1,0:T(8,128)(2,1)S(1)} collective-permute-done((bf16[8,4,64,128]{3,2,1,0:T(8,128)(2,1)S(1)}, bf16[8,4,64,128]{3,2,1,0:T(8,128)(2,1)S(1)}, u32[]{:S(2)}, u32[]{:S(2)}) %collective-permute-start.9) | collective-permute-done | bytes 524320 | tf_op jit(solution)/shard_map/ppermute | solution.py:54
  37.6 0.9 %shard_map.48 = bf16[16,4,2,32,128]{4,3,2,1,0:T(8,128)(2,1)} custom-call(s32[16]{0:T(128)S(4)} %get-tuple-element.21.order_ref, bf16[1,16,4,64,128]{4,3,2,1,0:T(8,128)(2,1)S(1)} %get-tuple-element.35.refs_0_, bf16[1,16,4,64,128]{4,3,2,1,0:T(8,128)(2,1)S(1)} %collective-permute-done.8.refs_1_, ...), custom_call_target="tpu_custom_call", output_to_operand_aliasing={{}: (4, {})} | custom-call | flops 1 | bytes 1 | tf_op jit(solution)/shard_map/pallas_call | solution.py:59
  (7 shorter events, 0.0 us)
Async XLA Ops:
  0.0 10.0 %collective-permute-start = (bf16[2,192,128]{2,1,0:T(8,128)(2,1)}, bf16[2,192,128]{2,1,0:T(8,128)(2,1)S(1)}, u32[]{:S(2)}, u32[]{:S(2)}) collective-permute-start(bf16[2,192,128]{2,1,0:T(8,128)(2,1)} %bitcast.11), channel_id=1, source_target_pairs={{0,4},{4,0},{8,12},{12,8},{1,5},{5,1},{9,13},{13,9},{2,6},{6,2},{1... | collective-permute-start | bytes 294920 | tf_op jit(solution)/shard_map/ppermute | solution.py:49
  4.1 6.0 %collective-permute-start.1 = (bf16[1,64,384]{2,1,0:T(8,128)(2,1)S(1)}, bf16[1,64,384]{2,1,0:T(8,128)(2,1)S(1)}, u32[]{:S(2)}, u32[]{:S(2)}) collective-permute-start(bf16[1,64,384]{2,1,0:T(8,128)(2,1)S(1)} %get-tuple-element.24.refs_0_), channel_id=1, source_target_pairs={{0,12},{4,8},{8,4},{12,0},{1,13},{5,9},{9,5},{13,1},{2,14},{6,10},... | collective-permute-start | bytes 147464 | tf_op jit(solution)/shard_map/ppermute | solution.py:49
  10.6 1.6 %collective-permute-start.2 = (bf16[1,4,4,64,128]{4,3,2,1,0:T(8,128)(2,1)S(1)}, bf16[1,4,4,64,128]{4,3,2,1,0:T(8,128)(2,1)S(1)}, u32[]{:S(2)}, u32[]{:S(2)}) collective-permute-start(bf16[1,4,4,64,128]{4,3,2,1,0:T(8,128)(2,1)S(1)} %get-tuple-element.27), channel_id=1, source_target_pairs={{0,1},{1,0},{2,3},{3,2},{4,5},{5,4},{6,7},{7,6},{8,9},{9,8},{10,11... | collective-permute-start | bytes 786440 | tf_op jit(solution)/shard_map/ppermute | solution.py:325
  11.1 6.2 %collective-permute-start.6 = (bf16[1,4,4,64,128]{4,3,2,1,0:T(8,128)(2,1)S(1)}, bf16[1,4,4,64,128]{4,3,2,1,0:T(8,128)(2,1)S(1)}, u32[]{:S(2)}, u32[]{:S(2)}) collective-permute-start(bf16[1,4,4,64,128]{4,3,2,1,0:T(8,128)(2,1)S(1)} %get-tuple-element.31), channel_id=1, source_target_pairs={{0,1},{1,0},{2,3},{3,2},{4,5},{5,4},{6,7},{7,6},{8,9},{9,8},{10,11... | collective-permute-start | bytes 786440 | tf_op jit(solution)/shard_map/ppermute | solution.py:325
  12.3 9.2 %collective-permute-start.11 = (bf16[4,4,64,128]{3,2,1,0:T(8,128)(2,1)S(1)}, bf16[4,4,64,128]{3,2,1,0:T(8,128)(2,1)S(1)}, u32[]{:S(2)}, u32[]{:S(2)}) collective-permute-start(bf16[4,4,64,128]{3,2,1,0:T(8,128)(2,1)S(1)} %fusion.1._), channel_id=1, source_target_pairs={{0,2},{1,3},{2,0},{3,1},{4,6},{5,7},{6,4},{7,5},{8,10},{9,11},{10,... | collective-permute-start | bytes 786440 | tf_op jit(solution)/shard_map/ppermute | solution.py:54
  13.8 4.2 %collective-permute-start.5 = (bf16[1,64,384]{2,1,0:T(8,128)(2,1)S(1)}, bf16[1,64,384]{2,1,0:T(8,128)(2,1)S(1)}, u32[]{:S(2)}, u32[]{:S(2)}) collective-permute-start(bf16[1,64,384]{2,1,0:T(8,128)(2,1)S(1)} %collective-permute-done.1.refs_2_), channel_id=1, source_target_pairs={{0,4},{4,0},{8,12},{12,8},{1,5},{5,1},{9,13},{13,9},{2,6},{6,2},{1... | collective-permute-start | bytes 147464 | tf_op jit(solution)/shard_map/ppermute | solution.py:49
  13.9 10.9 %collective-permute-start.3 = (bf16[64,384]{1,0:T(8,128)(2,1)S(1)}, bf16[64,384]{1,0:T(8,128)(2,1)S(1)}, u32[]{:S(2)}, u32[]{:S(2)}) collective-permute-start(bf16[64,384]{1,0:T(8,128)(2,1)S(1)} %shard_map.40.refs_0_), channel_id=1, source_target_pairs={{0,12},{4,8},{8,4},{12,0},{1,13},{5,9},{9,5},{13,1},{2,14},{6,10},... | collective-permute-start | bytes 147464 | tf_op jit(solution)/shard_map/ppermute | solution.py:49
  16.4 8.3 %collective-permute-start.4 = (bf16[64,384]{1,0:T(8,128)(2,1)S(1)}, bf16[64,384]{1,0:T(8,128)(2,1)S(1)}, u32[]{:S(2)}, u32[]{:S(2)}) collective-permute-start(bf16[64,384]{1,0:T(8,128)(2,1)S(1)} %shard_map.40.refs_0_), channel_id=1, source_target_pairs={{0,8},{4,12},{8,0},{12,4},{1,9},{5,13},{9,1},{13,5},{2,10},{6,14},... | collective-permute-start | bytes 147464 | tf_op jit(solution)/shard_map/ppermute | solution.py:49
  17.4 9.2 %collective-permute-start.10 = (bf16[4,4,64,128]{3,2,1,0:T(8,128)(2,1)S(1)}, bf16[4,4,64,128]{3,2,1,0:T(8,128)(2,1)S(1)}, u32[]{:S(2)}, u32[]{:S(2)}) collective-permute-start(bf16[4,4,64,128]{3,2,1,0:T(8,128)(2,1)S(1)} %fusion.2.refs_3_), channel_id=1, source_target_pairs={{0,2},{1,3},{2,0},{3,1},{4,6},{5,7},{6,4},{7,5},{8,10},{9,11},{10,... | collective-permute-start | bytes 786440 | tf_op jit(solution)/shard_map/ppermute | solution.py:54
  21.0 2.0 %collective-permute-start.7 = (bf16[1,8,4,64,128]{4,3,2,1,0:T(8,128)(2,1)S(1)}, bf16[1,8,4,64,128]{4,3,2,1,0:T(8,128)(2,1)S(1)}, u32[]{:S(2)}, u32[]{:S(2)}) collective-permute-start(bf16[1,8,4,64,128]{4,3,2,1,0:T(8,128)(2,1)S(1)} %get-tuple-element.34), channel_id=1, source_target_pairs={{0,1},{1,0},{2,3},{3,2},{4,5},{5,4},{6,7},{7,6},{8,9},{9,8},{10,11... | collective-permute-start | bytes 1572872 | tf_op jit(solution)/shard_map/ppermute | solution.py:325
  23.2 14.4 %collective-permute-start.9 = (bf16[8,4,64,128]{3,2,1,0:T(8,128)(2,1)S(1)}, bf16[8,4,64,128]{3,2,1,0:T(8,128)(2,1)S(1)}, u32[]{:S(2)}, u32[]{:S(2)}) collective-permute-start(bf16[8,4,64,128]{3,2,1,0:T(8,128)(2,1)S(1)} %fusion.refs_6_), channel_id=1, source_target_pairs={{0,2},{1,3},{2,0},{3,1},{4,6},{5,7},{6,4},{7,5},{8,10},{9,11},{10,... | collective-permute-start | bytes 1572872 | tf_op jit(solution)/shard_map/ppermute | solution.py:54
  26.1 2.7 %collective-permute-start.8 = (bf16[1,16,4,64,128]{4,3,2,1,0:T(8,128)(2,1)S(1)}, bf16[1,16,4,64,128]{4,3,2,1,0:T(8,128)(2,1)S(1)}, u32[]{:S(2)}, u32[]{:S(2)}) collective-permute-start(bf16[1,16,4,64,128]{4,3,2,1,0:T(8,128)(2,1)S(1)} %get-tuple-element.36), channel_id=1, source_target_pairs={{0,1},{1,0},{2,3},{3,2},{4,5},{5,4},{6,7},{7,6},{8,9},{9,8},{10,11... | collective-permute-start | bytes 3145736 | tf_op jit(solution)/shard_map/ppermute | solution.py:343

commit v5 on v4

--- a/solution.py
+++ b/solution.py
@@ -7,11 +7,11 @@
 from jax.experimental.pallas import tpu as pltpu
 from jax.sharding import PartitionSpec as P
 
-SHARES = (4, 4, 8)
+SHARES = (3, 5, 8)
 AFTER = (None, None, 1)
 HOME_AFTER = 2
 HOMES_BEFORE = 2
-RELAY_AFTER = 0
+RELAY_AFTER = 1
 SMEM = pl.BlockSpec(memory_space=pltpu.SMEM)
 VMEM = pl.BlockSpec(memory_space=pltpu.VMEM)
 HBM = pl.BlockSpec(memory_space=pltpu.HBM)
@@ -81,9 +81,20 @@
 
 
 def lay(chips, rows, source_ref, away_ref, home_ref, vector_ref, sem):
-    copy = pltpu.make_async_copy(source_ref, vector_ref, sem)
-    copy.start()
-    copy.wait()
+    cut = vector_ref.shape[1] // 2
+    copies = [
+        pltpu.make_async_copy(
+            source_ref.at[part, pl.ds(at * cut, cut)],
+            vector_ref.at[part, pl.ds(at * cut, cut)],
+            sem.at[part, at],
+        )
+        for part in range(2)
+        for at in range(2)
+    ]
+    for copy in copies:
+        copy.start()
+    for copy in copies:
+        copy.wait()
     turned = interleave(vector_ref[0], vector_ref[1]).T
     chip = lax.axis_index("space") // 2
     for to_chip in range(chips):
@@ -239,7 +250,7 @@
     half = blocks // 2
     late = half // most
     first = times - late
-    steps = [0] + list(range(1, times, 2)) + list(range(2, times, 2))
+    steps = list(range(times))
 
     own = eigvecs[0].reshape(2, colours * sites, -1)
     data = far(solutions.reshape(blocks, spins, 2, colours * sites, columns))
@@ -251,7 +262,7 @@
         [HBM],
         [away_kind, home_kind],
         [far(own)],
-        scratch_shapes=[pltpu.VMEM(own.shape, kind), pltpu.SemaphoreType.DMA],
+        scratch_shapes=[pltpu.VMEM(own.shape, kind), pltpu.SemaphoreType.DMA((2, 2))],
     )
     aways = [away] + [
         swap(own if step == steps[1] else away, "tm", step, times) for step in steps[1:first]

time: 38.6 us -> 38 us (0.984)
  waiting for transfers between devices: 13.1 us -> 12.4 us
    ppermute x4, waiting for transfers between devices: 4.14 us -> 3.53 us  [shards(): got = lax.ppermute(give, 'space', cores)]
    ppermute x5, waiting for transfers between devices: 0.82 us -> 0.34 us  [swap(): lax.ppermute(array, axis, [(i, peer(i, step, count)) for i in range(count)])]
  transfers between devices with their start and end apart: 12 -> 12, of which waited for: 7 -> 5; matrix products, arithmetic and copies ran while one was open for 1% -> 1% of each run, Pallas kernels for 26% -> 26%
where the time goes in v5:
time: 38 us; the launch traced here: 37.8 us
  starting transfers between devices  13.7 us (36%)
  waiting for transfers between devices  12.4 us (33%)
  Pallas kernels  11.2 us (29%)
    pallas_call x12, Pallas kernels, call(): pl.pallas_call(kernel, in_specs=ins, out_specs=specs, out_shape=shapes, c...  11.2 us
    ppermute x5, starting transfers between devices, swap(): lax.ppermute(array, axis, [(i, peer(i, step, count)) for i in range(count)])  9.26 us
    ppermute x3, waiting for transfers between devices, send(): return lax.ppermute(array, 'space', route)  8.48 us
    ppermute x3, starting transfers between devices, send(): return lax.ppermute(array, 'space', route)  3.66 us
    ppermute x4, waiting for transfers between devices, shards(): got = lax.ppermute(give, 'space', cores)  3.53 us
    ppermute x4, starting transfers between devices, shards(): got = lax.ppermute(give, 'space', cores)  0.77 us
  transfers between devices with their start and end apart: 12, of which 5 were waited for; matrix products, arithmetic and copies ran while one was open for 1% of the time, Pallas kernels for 26%

profile of v5, /device:TPU:0, one launch (start us, length us, event | category | flops | bytes accessed | tf_op | source)
XLA Modules:
  0.0 37.8 jit_solution(14790683929174028576)
XLA Ops:
  0.0 3.0 %collective-permute-start = (bf16[2,192,128]{2,1,0:T(8,128)(2,1)}, bf16[2,192,128]{2,1,0:T(8,128)(2,1)S(1)}, u32[]{:S(2)}, u32[]{:S(2)}) collective-permute-start(bf16[2,192,128]{2,1,0:T(8,128)(2,1)} %bitcast.11), channel_id=1, source_target_pairs={{0,4},{4,0},{8,12},{12,8},{1,5},{5,1},{9,13},{13,9},{2,6},{6,2},{1... | collective-permute-start | bytes 294920 | tf_op jit(solution)/shard_map/ppermute | solution.py:49
  3.0 0.9 %shard_map.38 = (bf16[1,64,384]{2,1,0:T(8,128)(2,1)S(1)}, bf16[64,384]{1,0:T(8,128)(2,1)S(1)}) custom-call(bf16[2,192,128]{2,1,0:T(8,128)(2,1)} %bitcast.12), custom_call_target="tpu_custom_call" | custom-call | flops 1 | bytes 1 | tf_op jit(solution)/shard_map/pallas_call | solution.py:59
  4.0 2.7 %collective-permute-start.1 = (bf16[1,64,384]{2,1,0:T(8,128)(2,1)S(1)}, bf16[1,64,384]{2,1,0:T(8,128)(2,1)S(1)}, u32[]{:S(2)}, u32[]{:S(2)}) collective-permute-start(bf16[1,64,384]{2,1,0:T(8,128)(2,1)S(1)} %get-tuple-element.25.refs_0_), channel_id=1, source_target_pairs={{0,8},{4,12},{8,0},{12,4},{1,9},{5,13},{9,1},{13,5},{2,10},{6,14},... | collective-permute-start | bytes 147464 | tf_op jit(solution)/shard_map/ppermute | solution.py:49
  6.6 2.6 %shard_map.37 = (s32[16]{0:T(128)S(4)}, s32[16]{0:T(128)S(4)}, bf16[8,4,2,192,128]{4,3,2,1,0:T(8,128)(2,1)S(1)}) custom-call(s32[16]{0:T(128)} %bitcast.13, bf16[16,4,2,192,128]{4,3,2,1,0:T(8,128)(2,1)} %bitcast.9), custom_call_target="tpu_custom_call" | custom-call | flops 1 | bytes 1 | tf_op jit(solution)/shard_map/pallas_call | solution.py:59
  9.2 0.3 collective-permute-done.1.refs_2_
  9.6 0.0 collective-permute-done.refs_1_
  9.6 0.5 %shard_map.39 = (bf16[1,3,4,64,128]{4,3,2,1,0:T(8,128)(2,1)S(1)}, bf16[1,3,4,64,128]{4,3,2,1,0:T(8,128)(2,1)S(1)}, bf16[4,128,384]{2,1,0:T(8,128)(2,1)S(1)}, bf16[2,64,384]{2,1,0:T(8,128)(2,1)S(1)}) custom-call(s32[16]{0:T(128)S(4)} %get-tuple-element.21.order_ref, s32[16]{0:T(128)S(4)} %get-tuple-element.22.slot_ref, ...), custom_call_target="tpu_custom_call" | custom-call | flops 1 | bytes 1 | tf_op jit(solution)/shard_map/pallas_call | solution.py:59
  10.1 0.1 collective-permute-start.10
  10.2 0.5 %shard_map.40 = (bf16[1,5,4,64,128]{4,3,2,1,0:T(8,128)(2,1)S(1)}, bf16[1,5,4,64,128]{4,3,2,1,0:T(8,128)(2,1)S(1)}) custom-call(s32[16]{0:T(128)S(4)} %get-tuple-element.21.order_ref, s32[16]{0:T(128)S(4)} %get-tuple-element.22.slot_ref, bf16[8,4,2,192,128]{4,3,2,1,0:T(8,128)(2,1)S(1)} %get-tuple-element.24.refs_3_.refs_0_.refs_4_, ...), custom_call_target="tpu_custom_call" | custom-call | flops 1 | bytes 1 | tf_op jit(solution)/shard_map/pallas_call | solution.py:59
  10.7 0.6 %collective-permute-start.2 = (bf16[1,5,4,64,128]{4,3,2,1,0:T(8,128)(2,1)S(1)}, bf16[1,5,4,64,128]{4,3,2,1,0:T(8,128)(2,1)S(1)}, u32[]{:S(2)}, u32[]{:S(2)}) collective-permute-start(bf16[1,5,4,64,128]{4,3,2,1,0:T(8,128)(2,1)S(1)} %get-tuple-element.28), channel_id=1, source_target_pairs={{0,1},{1,0},{2,3},{3,2},{4,5},{5,4},{6,7},{7,6},{8,9},{9,8},{10,11... | collective-permute-start | bytes 983048 | tf_op jit(solution)/shard_map/ppermute | solution.py:336
  11.2 0.4 %collective-permute-start.5 = (bf16[1,64,384]{2,1,0:T(8,128)(2,1)S(1)}, bf16[1,64,384]{2,1,0:T(8,128)(2,1)S(1)}, u32[]{:S(2)}, u32[]{:S(2)}) collective-permute-start(bf16[1,64,384]{2,1,0:T(8,128)(2,1)S(1)} %collective-permute-done.1.refs_2_), channel_id=1, source_target_pairs={{0,4},{4,0},{8,12},{12,8},{1,5},{5,1},{9,13},{13,9},{2,6},{6,2},{1... | collective-permute-start | bytes 147464 | tf_op jit(solution)/shard_map/ppermute | solution.py:49
  11.6 0.0 collective-permute-done.10
  11.6 0.1 fusion.2
  11.7 1.6 %collective-permute-start.11 = (bf16[3,4,64,128]{3,2,1,0:T(8,128)(2,1)S(1)}, bf16[3,4,64,128]{3,2,1,0:T(8,128)(2,1)S(1)}, u32[]{:S(2)}, u32[]{:S(2)}) collective-permute-start(bf16[3,4,64,128]{3,2,1,0:T(8,128)(2,1)S(1)} %fusion.2), channel_id=1, source_target_pairs={{0,2},{1,3},{2,0},{3,1},{4,6},{5,7},{6,4},{7,5},{8,10},{9,11},{10,... | collective-permute-start | bytes 589832 | tf_op jit(solution)/shard_map/ppermute | solution.py:54
  13.2 0.0 collective-permute-done.2
  13.3 0.1 fusion.1._.refs_3_
  13.4 3.2 %collective-permute-start.4 = (bf16[64,384]{1,0:T(8,128)(2,1)S(1)}, bf16[64,384]{1,0:T(8,128)(2,1)S(1)}, u32[]{:S(2)}, u32[]{:S(2)}) collective-permute-start(bf16[64,384]{1,0:T(8,128)(2,1)S(1)} %shard_map.41.refs_0_), channel_id=1, source_target_pairs={{0,12},{4,8},{8,4},{12,0},{1,13},{5,9},{9,5},{13,1},{2,14},{6,10},... | collective-permute-start | bytes 147464 | tf_op jit(solution)/shard_map/ppermute | solution.py:49
  16.6 0.5 %collective-permute-start.9 = (bf16[5,4,64,128]{3,2,1,0:T(8,128)(2,1)S(1)}, bf16[5,4,64,128]{3,2,1,0:T(8,128)(2,1)S(1)}, u32[]{:S(2)}, u32[]{:S(2)}) collective-permute-start(bf16[5,4,64,128]{3,2,1,0:T(8,128)(2,1)S(1)} %fusion.1._.refs_3_), channel_id=1, source_target_pairs={{0,2},{1,3},{2,0},{3,1},{4,6},{5,7},{6,4},{7,5},{8,10},{9,11},{10,... | collective-permute-start | bytes 983048 | tf_op jit(solution)/shard_map/ppermute | solution.py:54
  17.1 0.0 collective-permute-done.5.refs_0_
  17.1 3.0 %shard_map.42 = (bf16[1,8,4,64,128]{4,3,2,1,0:T(8,128)(2,1)S(1)}, bf16[1,8,4,64,128]{4,3,2,1,0:T(8,128)(2,1)S(1)}, bf16[8,4,2,192,128]{4,3,2,1,0:T(8,128)(2,1)S(1)}, bf16[4,128,384]{2,1,0:T(8,128)(2,1)S(1)}) custom-call(s32[16]{0:T(128)S(4)} %get-tuple-element.21.order_ref, s32[16]{0:T(128)S(4)} %get-tuple-element.22.slot_ref, ...), custom_call_target="tpu_custom_call", output_to_operand_aliasing={{3}: (4, {})} | custom-call | flops 1 | bytes 1 | tf_op jit(solution)/shard_map/pallas_call | solution.py:59
  20.1 0.1 collective-permute-start.6
  20.2 1.9 %collective-permute-done.6 = bf16[1,8,4,64,128]{4,3,2,1,0:T(8,128)(2,1)S(1)} collective-permute-done((bf16[1,8,4,64,128]{4,3,2,1,0:T(8,128)(2,1)S(1)}, bf16[1,8,4,64,128]{4,3,2,1,0:T(8,128)(2,1)S(1)}, u32[]{:S(2)}, u32[]{:S(2)}) %collective-permute-start.6) | collective-permute-done | bytes 524320 | tf_op jit(solution)/shard_map/ppermute | solution.py:336
  22.0 0.2 fusion.refs_6_
  22.3 1.6 %collective-permute-start.8 = (bf16[8,4,64,128]{3,2,1,0:T(8,128)(2,1)S(1)}, bf16[8,4,64,128]{3,2,1,0:T(8,128)(2,1)S(1)}, u32[]{:S(2)}, u32[]{:S(2)}) collective-permute-start(bf16[8,4,64,128]{3,2,1,0:T(8,128)(2,1)S(1)} %fusion.refs_6_), channel_id=1, source_target_pairs={{0,2},{1,3},{2,0},{3,1},{4,6},{5,7},{6,4},{7,5},{8,10},{9,11},{10,... | collective-permute-start | bytes 1572872 | tf_op jit(solution)/shard_map/ppermute | solution.py:54
  23.8 1.3 %shard_map.43 = (bf16[1,16,4,64,128]{4,3,2,1,0:T(8,128)(2,1)S(1)}, bf16[1,16,4,64,128]{4,3,2,1,0:T(8,128)(2,1)S(1)}) custom-call(s32[16]{0:T(128)S(4)} %get-tuple-element.22.slot_ref, bf16[64,384]{1,0:T(8,128)(2,1)S(1)} %shard_map.41.refs_0_, bf16[2,64,384]{2,1,0:T(8,128)(2,1)S(1)} %get-tuple-element.29.refs_1_, ...), custom_call_target="tpu_custom_call" | custom-call | flops 1 | bytes 1 | tf_op jit(solution)/shard_map/pallas_call | solution.py:59
  25.2 0.1 collective-permute-start.7
  25.2 1.0 %collective-permute-done.9.refs_0_.refs_2_ = bf16[5,4,64,128]{3,2,1,0:T(8,128)(2,1)S(1)} collective-permute-done((bf16[5,4,64,128]{3,2,1,0:T(8,128)(2,1)S(1)}, bf16[5,4,64,128]{3,2,1,0:T(8,128)(2,1)S(1)}, u32[]{:S(2)}, u32[]{:S(2)}) %collective-permute-start.9) | collective-permute-done | bytes 327712 | tf_op jit(solution)/shard_map/ppermute | solution.py:54
  26.2 1.7 %collective-permute-done.7.refs_1_ = bf16[1,16,4,64,128]{4,3,2,1,0:T(8,128)(2,1)S(1)} collective-permute-done((bf16[1,16,4,64,128]{4,3,2,1,0:T(8,128)(2,1)S(1)}, bf16[1,16,4,64,128]{4,3,2,1,0:T(8,128)(2,1)S(1)}, u32[]{:S(2)}, u32[]{:S(2)}) %collective-permute-start.7) | collective-permute-done | bytes 1048608 | tf_op jit(solution)/shard_map/ppermute | solution.py:354
  27.9 0.7 %shard_map.46.refs_3_ = bf16[16,4,2,32,128]{4,3,2,1,0:T(8,128)(2,1)} custom-call(s32[16]{0:T(128)S(4)} %get-tuple-element.21.order_ref, bf16[1,16,4,64,128]{4,3,2,1,0:T(8,128)(2,1)S(1)} %get-tuple-element.33.refs_0_, bf16[1,16,4,64,128]{4,3,2,1,0:T(8,128)(2,1)S(1)} %collective-permute-done.7.refs_1_, ...), custom_call_target="tpu_custom_call" | custom-call | flops 1 | bytes 1 | tf_op jit(solution)/shard_map/pallas_call | solution.py:59
  28.6 0.8 %shard_map.47.refs_3_ = bf16[16,4,2,32,128]{4,3,2,1,0:T(8,128)(2,1)} custom-call(s32[16]{0:T(128)S(4)} %get-tuple-element.21.order_ref, bf16[1,16,4,64,128]{4,3,2,1,0:T(8,128)(2,1)S(1)} %get-tuple-element.33.refs_0_, bf16[1,16,4,64,128]{4,3,2,1,0:T(8,128)(2,1)S(1)} %collective-permute-done.7.refs_1_, ...), custom_call_target="tpu_custom_call", output_to_operand_aliasing={{}: (4, {})} | custom-call | flops 1 | bytes 1 | tf_op jit(solution)/shard_map/pallas_call | solution.py:59
  29.4 7.5 %collective-permute-done.8.refs_2_ = bf16[8,4,64,128]{3,2,1,0:T(8,128)(2,1)S(1)} collective-permute-done((bf16[8,4,64,128]{3,2,1,0:T(8,128)(2,1)S(1)}, bf16[8,4,64,128]{3,2,1,0:T(8,128)(2,1)S(1)}, u32[]{:S(2)}, u32[]{:S(2)}) %collective-permute-start.8) | collective-permute-done | bytes 524320 | tf_op jit(solution)/shard_map/ppermute | solution.py:54
  36.9 0.9 %shard_map.48 = bf16[16,4,2,32,128]{4,3,2,1,0:T(8,128)(2,1)} custom-call(s32[16]{0:T(128)S(4)} %get-tuple-element.21.order_ref, bf16[1,16,4,64,128]{4,3,2,1,0:T(8,128)(2,1)S(1)} %get-tuple-element.33.refs_0_, bf16[1,16,4,64,128]{4,3,2,1,0:T(8,128)(2,1)S(1)} %collective-permute-done.7.refs_1_, ...), custom_call_target="tpu_custom_call", output_to_operand_aliasing={{}: (4, {})} | custom-call | flops 1 | bytes 1 | tf_op jit(solution)/shard_map/pallas_call | solution.py:59
  (7 shorter events, 0.0 us)
Async XLA Ops:
  0.0 9.6 %collective-permute-start = (bf16[2,192,128]{2,1,0:T(8,128)(2,1)}, bf16[2,192,128]{2,1,0:T(8,128)(2,1)S(1)}, u32[]{:S(2)}, u32[]{:S(2)}) collective-permute-start(bf16[2,192,128]{2,1,0:T(8,128)(2,1)} %bitcast.11), channel_id=1, source_target_pairs={{0,4},{4,0},{8,12},{12,8},{1,5},{5,1},{9,13},{13,9},{2,6},{6,2},{1... | collective-permute-start | bytes 294920 | tf_op jit(solution)/shard_map/ppermute | solution.py:49
  4.0 5.6 %collective-permute-start.1 = (bf16[1,64,384]{2,1,0:T(8,128)(2,1)S(1)}, bf16[1,64,384]{2,1,0:T(8,128)(2,1)S(1)}, u32[]{:S(2)}, u32[]{:S(2)}) collective-permute-start(bf16[1,64,384]{2,1,0:T(8,128)(2,1)S(1)} %get-tuple-element.25.refs_0_), channel_id=1, source_target_pairs={{0,8},{4,12},{8,0},{12,4},{1,9},{5,13},{9,1},{13,5},{2,10},{6,14},... | collective-permute-start | bytes 147464 | tf_op jit(solution)/shard_map/ppermute | solution.py:49
  10.1 1.5 %collective-permute-start.10 = (bf16[1,3,4,64,128]{4,3,2,1,0:T(8,128)(2,1)S(1)}, bf16[1,3,4,64,128]{4,3,2,1,0:T(8,128)(2,1)S(1)}, u32[]{:S(2)}, u32[]{:S(2)}) collective-permute-start(bf16[1,3,4,64,128]{4,3,2,1,0:T(8,128)(2,1)S(1)} %get-tuple-element.36), channel_id=1, source_target_pairs={{0,1},{1,0},{2,3},{3,2},{4,5},{5,4},{6,7},{7,6},{8,9},{9,8},{10,11... | collective-permute-start | bytes 589832 | tf_op jit(solution)/shard_map/ppermute | solution.py:336
  10.7 2.6 %collective-permute-start.2 = (bf16[1,5,4,64,128]{4,3,2,1,0:T(8,128)(2,1)S(1)}, bf16[1,5,4,64,128]{4,3,2,1,0:T(8,128)(2,1)S(1)}, u32[]{:S(2)}, u32[]{:S(2)}) collective-permute-start(bf16[1,5,4,64,128]{4,3,2,1,0:T(8,128)(2,1)S(1)} %get-tuple-element.28), channel_id=1, source_target_pairs={{0,1},{1,0},{2,3},{3,2},{4,5},{5,4},{6,7},{7,6},{8,9},{9,8},{10,11... | collective-permute-start | bytes 983048 | tf_op jit(solution)/shard_map/ppermute | solution.py:336
  11.2 5.9 %collective-permute-start.5 = (bf16[1,64,384]{2,1,0:T(8,128)(2,1)S(1)}, bf16[1,64,384]{2,1,0:T(8,128)(2,1)S(1)}, u32[]{:S(2)}, u32[]{:S(2)}) collective-permute-start(bf16[1,64,384]{2,1,0:T(8,128)(2,1)S(1)} %collective-permute-done.1.refs_2_), channel_id=1, source_target_pairs={{0,4},{4,0},{8,12},{12,8},{1,5},{5,1},{9,13},{13,9},{2,6},{6,2},{1... | collective-permute-start | bytes 147464 | tf_op jit(solution)/shard_map/ppermute | solution.py:49
  11.7 8.5 %collective-permute-start.11 = (bf16[3,4,64,128]{3,2,1,0:T(8,128)(2,1)S(1)}, bf16[3,4,64,128]{3,2,1,0:T(8,128)(2,1)S(1)}, u32[]{:S(2)}, u32[]{:S(2)}) collective-permute-start(bf16[3,4,64,128]{3,2,1,0:T(8,128)(2,1)S(1)} %fusion.2), channel_id=1, source_target_pairs={{0,2},{1,3},{2,0},{3,1},{4,6},{5,7},{6,4},{7,5},{8,10},{9,11},{10,... | collective-permute-start | bytes 589832 | tf_op jit(solution)/shard_map/ppermute | solution.py:54
  13.4 10.5 %collective-permute-start.4 = (bf16[64,384]{1,0:T(8,128)(2,1)S(1)}, bf16[64,384]{1,0:T(8,128)(2,1)S(1)}, u32[]{:S(2)}, u32[]{:S(2)}) collective-permute-start(bf16[64,384]{1,0:T(8,128)(2,1)S(1)} %shard_map.41.refs_0_), channel_id=1, source_target_pairs={{0,12},{4,8},{8,4},{12,0},{1,13},{5,9},{9,5},{13,1},{2,14},{6,10},... | collective-permute-start | bytes 147464 | tf_op jit(solution)/shard_map/ppermute | solution.py:49
  16.6 7.3 %collective-permute-start.3 = (bf16[64,384]{1,0:T(8,128)(2,1)S(1)}, bf16[64,384]{1,0:T(8,128)(2,1)S(1)}, u32[]{:S(2)}, u32[]{:S(2)}) collective-permute-start(bf16[64,384]{1,0:T(8,128)(2,1)S(1)} %shard_map.41.refs_0_), channel_id=1, source_target_pairs={{0,8},{4,12},{8,0},{12,4},{1,9},{5,13},{9,1},{13,5},{2,10},{6,14},... | collective-permute-start | bytes 147464 | tf_op jit(solution)/shard_map/ppermute | solution.py:49
  16.6 9.7 %collective-permute-start.9 = (bf16[5,4,64,128]{3,2,1,0:T(8,128)(2,1)S(1)}, bf16[5,4,64,128]{3,2,1,0:T(8,128)(2,1)S(1)}, u32[]{:S(2)}, u32[]{:S(2)}) collective-permute-start(bf16[5,4,64,128]{3,2,1,0:T(8,128)(2,1)S(1)} %fusion.1._.refs_3_), channel_id=1, source_target_pairs={{0,2},{1,3},{2,0},{3,1},{4,6},{5,7},{6,4},{7,5},{8,10},{9,11},{10,... | collective-permute-start | bytes 983048 | tf_op jit(solution)/shard_map/ppermute | solution.py:54
  20.1 2.0 %collective-permute-start.6 = (bf16[1,8,4,64,128]{4,3,2,1,0:T(8,128)(2,1)S(1)}, bf16[1,8,4,64,128]{4,3,2,1,0:T(8,128)(2,1)S(1)}, u32[]{:S(2)}, u32[]{:S(2)}) collective-permute-start(bf16[1,8,4,64,128]{4,3,2,1,0:T(8,128)(2,1)S(1)} %get-tuple-element.32), channel_id=1, source_target_pairs={{0,1},{1,0},{2,3},{3,2},{4,5},{5,4},{6,7},{7,6},{8,9},{9,8},{10,11... | collective-permute-start | bytes 1572872 | tf_op jit(solution)/shard_map/ppermute | solution.py:336
  22.3 14.7 %collective-permute-start.8 = (bf16[8,4,64,128]{3,2,1,0:T(8,128)(2,1)S(1)}, bf16[8,4,64,128]{3,2,1,0:T(8,128)(2,1)S(1)}, u32[]{:S(2)}, u32[]{:S(2)}) collective-permute-start(bf16[8,4,64,128]{3,2,1,0:T(8,128)(2,1)S(1)} %fusion.refs_6_), channel_id=1, source_target_pairs={{0,2},{1,3},{2,0},{3,1},{4,6},{5,7},{6,4},{7,5},{8,10},{9,11},{10,... | collective-permute-start | bytes 1572872 | tf_op jit(solution)/shard_map/ppermute | solution.py:54
  25.2 2.7 %collective-permute-start.7 = (bf16[1,16,4,64,128]{4,3,2,1,0:T(8,128)(2,1)S(1)}, bf16[1,16,4,64,128]{4,3,2,1,0:T(8,128)(2,1)S(1)}, u32[]{:S(2)}, u32[]{:S(2)}) collective-permute-start(bf16[1,16,4,64,128]{4,3,2,1,0:T(8,128)(2,1)S(1)} %get-tuple-element.34), channel_id=1, source_target_pairs={{0,1},{1,0},{2,3},{3,2},{4,5},{5,4},{6,7},{7,6},{8,9},{9,8},{10,11... | collective-permute-start | bytes 3145736 | tf_op jit(solution)/shard_map/ppermute | solution.py:354

commit v6 on v5

--- a/solution.py
+++ b/solution.py
@@ -7,7 +7,7 @@
 from jax.experimental.pallas import tpu as pltpu
 from jax.sharding import PartitionSpec as P
 
-SHARES = (3, 5, 8)
+SHARES = (2, 6, 8)
 AFTER = (None, None, 1)
 HOME_AFTER = 2
 HOMES_BEFORE = 2

time: 38 us -> 39 us (1.026)
  waiting for transfers between devices: 12.4 us -> 14.4 us
  starting transfers between devices: 13.7 us -> 12.6 us
    ppermute x5, waiting for transfers between devices: 0.34 us -> 4.53 us  [swap(): lax.ppermute(array, axis, [(i, peer(i, step, count)) for i in range(count)])]
    ppermute x3, waiting for transfers between devices: 8.48 us -> 6.2 us  [send(): return lax.ppermute(array, 'space', route)]
    ppermute x5, starting transfers between devices: 9.26 us -> 8.2 us  [swap(): lax.ppermute(array, axis, [(i, peer(i, step, count)) for i in range(count)])]
  transfers between devices with their start and end apart: 12 -> 12, of which waited for: 5 -> 8; matrix products, arithmetic and copies ran while one was open for 1% -> 1% of each run, Pallas kernels for 26% -> 24%
where the time goes in v6:
time: 39 us; the launch traced here: 38.8 us
  waiting for transfers between devices  14.4 us (37%)
  starting transfers between devices  12.6 us (32%)
  Pallas kernels  11.3 us (29%)
    pallas_call x12, Pallas kernels, call(): pl.pallas_call(kernel, in_specs=ins, out_specs=specs, out_shape=shapes, c...  11.3 us
    ppermute x5, starting transfers between devices, swap(): lax.ppermute(array, axis, [(i, peer(i, step, count)) for i in range(count)])  8.2 us
    ppermute x3, waiting for transfers between devices, send(): return lax.ppermute(array, 'space', route)  6.2 us
    ppermute x5, waiting for transfers between devices, swap(): lax.ppermute(array, axis, [(i, peer(i, step, count)) for i in range(count)])  4.53 us
    ppermute x3, starting transfers between devices, send(): return lax.ppermute(array, 'space', route)  3.71 us
    ppermute x4, waiting for transfers between devices, shards(): got = lax.ppermute(give, 'space', cores)  3.65 us
  transfers between devices with their start and end apart: 12, of which 8 were waited for; matrix products, arithmetic and copies ran while one was open for 1% of the time, Pallas kernels for 24%

profile of v6, /device:TPU:0, one launch (start us, length us, event | category | flops | bytes accessed | tf_op | source)
XLA Modules:
  0.0 38.8 jit_solution(12087312030812137217)
XLA Ops:
  0.0 3.0 %collective-permute-start = (bf16[2,192,128]{2,1,0:T(8,128)(2,1)}, bf16[2,192,128]{2,1,0:T(8,128)(2,1)S(1)}, u32[]{:S(2)}, u32[]{:S(2)}) collective-permute-start(bf16[2,192,128]{2,1,0:T(8,128)(2,1)} %bitcast.11), channel_id=1, source_target_pairs={{0,4},{4,0},{8,12},{12,8},{1,5},{5,1},{9,13},{13,9},{2,6},{6,2},{1... | collective-permute-start | bytes 294920 | tf_op jit(solution)/shard_map/ppermute | solution.py:49
  3.0 0.9 %shard_map.38 = (bf16[1,64,384]{2,1,0:T(8,128)(2,1)S(1)}, bf16[64,384]{1,0:T(8,128)(2,1)S(1)}) custom-call(bf16[2,192,128]{2,1,0:T(8,128)(2,1)} %bitcast.12), custom_call_target="tpu_custom_call" | custom-call | flops 1 | bytes 1 | tf_op jit(solution)/shard_map/pallas_call | solution.py:59
  4.0 2.7 %collective-permute-start.1 = (bf16[1,64,384]{2,1,0:T(8,128)(2,1)S(1)}, bf16[1,64,384]{2,1,0:T(8,128)(2,1)S(1)}, u32[]{:S(2)}, u32[]{:S(2)}) collective-permute-start(bf16[1,64,384]{2,1,0:T(8,128)(2,1)S(1)} %get-tuple-element.25.refs_0_), channel_id=1, source_target_pairs={{0,8},{4,12},{8,0},{12,4},{1,9},{5,13},{9,1},{13,5},{2,10},{6,14},... | collective-permute-start | bytes 147464 | tf_op jit(solution)/shard_map/ppermute | solution.py:49
  6.6 2.6 %shard_map.37 = (s32[16]{0:T(128)S(4)}, s32[16]{0:T(128)S(4)}, bf16[8,4,2,192,128]{4,3,2,1,0:T(8,128)(2,1)S(1)}) custom-call(s32[16]{0:T(128)} %bitcast.13, bf16[16,4,2,192,128]{4,3,2,1,0:T(8,128)(2,1)} %bitcast.9), custom_call_target="tpu_custom_call" | custom-call | flops 1 | bytes 1 | tf_op jit(solution)/shard_map/pallas_call | solution.py:59
  9.2 0.3 collective-permute-done.1.refs_2_
  9.6 0.4 %shard_map.39 = (bf16[1,2,4,64,128]{4,3,2,1,0:T(8,128)(2,1)S(1)}, bf16[1,2,4,64,128]{4,3,2,1,0:T(8,128)(2,1)S(1)}, bf16[4,128,384]{2,1,0:T(8,128)(2,1)S(1)}, bf16[2,64,384]{2,1,0:T(8,128)(2,1)S(1)}) custom-call(s32[16]{0:T(128)S(4)} %get-tuple-element.21.order_ref, s32[16]{0:T(128)S(4)} %get-tuple-element.22.slot_ref, ...), custom_call_target="tpu_custom_call" | custom-call | flops 1 | bytes 1 | tf_op jit(solution)/shard_map/pallas_call | solution.py:59
  10.0 0.6 %shard_map.40 = (bf16[1,6,4,64,128]{4,3,2,1,0:T(8,128)(2,1)S(1)}, bf16[1,6,4,64,128]{4,3,2,1,0:T(8,128)(2,1)S(1)}) custom-call(s32[16]{0:T(128)S(4)} %get-tuple-element.21.order_ref, s32[16]{0:T(128)S(4)} %get-tuple-element.22.slot_ref, bf16[8,4,2,192,128]{4,3,2,1,0:T(8,128)(2,1)S(1)} %get-tuple-element.24.refs_3_.refs_0_.refs_4_, ...), custom_call_target="tpu_custom_call" | custom-call | flops 1 | bytes 1 | tf_op jit(solution)/shard_map/pallas_call | solution.py:59
  10.6 0.1 collective-permute-start.2
  10.7 0.5 %collective-permute-start.10 = (bf16[1,2,4,64,128]{4,3,2,1,0:T(8,128)(2,1)S(1)}, bf16[1,2,4,64,128]{4,3,2,1,0:T(8,128)(2,1)S(1)}, u32[]{:S(2)}, u32[]{:S(2)}) collective-permute-start(bf16[1,2,4,64,128]{4,3,2,1,0:T(8,128)(2,1)S(1)} %get-tuple-element.36), channel_id=1, source_target_pairs={{0,1},{1,0},{2,3},{3,2},{4,5},{5,4},{6,7},{7,6},{8,9},{9,8},{10,11... | collective-permute-start | bytes 393224 | tf_op jit(solution)/shard_map/ppermute | solution.py:336
  11.2 0.4 collective-permute-start.5
  11.5 1.0 %collective-permute-done.10 = bf16[1,2,4,64,128]{4,3,2,1,0:T(8,128)(2,1)S(1)} collective-permute-done((bf16[1,2,4,64,128]{4,3,2,1,0:T(8,128)(2,1)S(1)}, bf16[1,2,4,64,128]{4,3,2,1,0:T(8,128)(2,1)S(1)}, u32[]{:S(2)}, u32[]{:S(2)}) %collective-permute-start.10) | collective-permute-done | bytes 131104 | tf_op jit(solution)/shard_map/ppermute | solution.py:336
  12.6 1.6 %collective-permute-start.11 = (bf16[2,4,64,128]{3,2,1,0:T(8,128)(2,1)S(1)}, bf16[2,4,64,128]{3,2,1,0:T(8,128)(2,1)S(1)}, u32[]{:S(2)}, u32[]{:S(2)}) collective-permute-start(bf16[2,4,64,128]{3,2,1,0:T(8,128)(2,1)S(1)} %fusion.2), channel_id=1, source_target_pairs={{0,2},{1,3},{2,0},{3,1},{4,6},{5,7},{6,4},{7,5},{8,10},{9,11},{10,... | collective-permute-start | bytes 393224 | tf_op jit(solution)/shard_map/ppermute | solution.py:54
  14.2 0.0 collective-permute-done.2
  14.2 0.1 fusion.1._.refs_3_
  14.3 0.6 %collective-permute-start.9 = (bf16[6,4,64,128]{3,2,1,0:T(8,128)(2,1)S(1)}, bf16[6,4,64,128]{3,2,1,0:T(8,128)(2,1)S(1)}, u32[]{:S(2)}, u32[]{:S(2)}) collective-permute-start(bf16[6,4,64,128]{3,2,1,0:T(8,128)(2,1)S(1)} %fusion.1._.refs_3_), channel_id=1, source_target_pairs={{0,2},{1,3},{2,0},{3,1},{4,6},{5,7},{6,4},{7,5},{8,10},{9,11},{10,... | collective-permute-start | bytes 1179656 | tf_op jit(solution)/shard_map/ppermute | solution.py:54
  14.9 0.4 collective-permute-done.5.refs_0_
  15.3 3.0 %shard_map.42 = (bf16[1,8,4,64,128]{4,3,2,1,0:T(8,128)(2,1)S(1)}, bf16[1,8,4,64,128]{4,3,2,1,0:T(8,128)(2,1)S(1)}, bf16[8,4,2,192,128]{4,3,2,1,0:T(8,128)(2,1)S(1)}, bf16[4,128,384]{2,1,0:T(8,128)(2,1)S(1)}) custom-call(s32[16]{0:T(128)S(4)} %get-tuple-element.21.order_ref, s32[16]{0:T(128)S(4)} %get-tuple-element.22.slot_ref, ...), custom_call_target="tpu_custom_call", output_to_operand_aliasing={{3}: (4, {})} | custom-call | flops 1 | bytes 1 | tf_op jit(solution)/shard_map/pallas_call | solution.py:59
  18.2 0.1 collective-permute-start.6
  18.3 0.7 %collective-permute-done.11.refs_0_.refs_2_ = bf16[2,4,64,128]{3,2,1,0:T(8,128)(2,1)S(1)} collective-permute-done((bf16[2,4,64,128]{3,2,1,0:T(8,128)(2,1)S(1)}, bf16[2,4,64,128]{3,2,1,0:T(8,128)(2,1)S(1)}, u32[]{:S(2)}, u32[]{:S(2)}) %collective-permute-start.11) | collective-permute-done | bytes 131104 | tf_op jit(solution)/shard_map/ppermute | solution.py:54
  19.0 2.1 %collective-permute-start.4 = (bf16[64,384]{1,0:T(8,128)(2,1)S(1)}, bf16[64,384]{1,0:T(8,128)(2,1)S(1)}, u32[]{:S(2)}, u32[]{:S(2)}) collective-permute-start(bf16[64,384]{1,0:T(8,128)(2,1)S(1)} %shard_map.41.refs_0_), channel_id=1, source_target_pairs={{0,12},{4,8},{8,4},{12,0},{1,13},{5,9},{9,5},{13,1},{2,14},{6,10},... | collective-permute-start | bytes 147464 | tf_op jit(solution)/shard_map/ppermute | solution.py:49
  21.2 0.0 collective-permute-start.3
  21.2 0.2 fusion.refs_6_
  21.4 1.6 %collective-permute-start.8 = (bf16[8,4,64,128]{3,2,1,0:T(8,128)(2,1)S(1)}, bf16[8,4,64,128]{3,2,1,0:T(8,128)(2,1)S(1)}, u32[]{:S(2)}, u32[]{:S(2)}) collective-permute-start(bf16[8,4,64,128]{3,2,1,0:T(8,128)(2,1)S(1)} %fusion.refs_6_), channel_id=1, source_target_pairs={{0,2},{1,3},{2,0},{3,1},{4,6},{5,7},{6,4},{7,5},{8,10},{9,11},{10,... | collective-permute-start | bytes 1572872 | tf_op jit(solution)/shard_map/ppermute | solution.py:54
  22.9 2.4 %collective-permute-done.4.refs_3_ = bf16[64,384]{1,0:T(8,128)(2,1)S(1)} collective-permute-done((bf16[64,384]{1,0:T(8,128)(2,1)S(1)}, bf16[64,384]{1,0:T(8,128)(2,1)S(1)}, u32[]{:S(2)}, u32[]{:S(2)}) %collective-permute-start.4) | collective-permute-done | bytes 49184 | tf_op jit(solution)/shard_map/ppermute | solution.py:49
  25.3 1.5 %collective-permute-done.3.refs_2_ = bf16[64,384]{1,0:T(8,128)(2,1)S(1)} collective-permute-done((bf16[64,384]{1,0:T(8,128)(2,1)S(1)}, bf16[64,384]{1,0:T(8,128)(2,1)S(1)}, u32[]{:S(2)}, u32[]{:S(2)}) %collective-permute-start.3) | collective-permute-done | bytes 49184 | tf_op jit(solution)/shard_map/ppermute | solution.py:49
  26.8 1.3 %shard_map.43 = (bf16[1,16,4,64,128]{4,3,2,1,0:T(8,128)(2,1)S(1)}, bf16[1,16,4,64,128]{4,3,2,1,0:T(8,128)(2,1)S(1)}) custom-call(s32[16]{0:T(128)S(4)} %get-tuple-element.22.slot_ref, bf16[64,384]{1,0:T(8,128)(2,1)S(1)} %shard_map.41.refs_0_, bf16[2,64,384]{2,1,0:T(8,128)(2,1)S(1)} %get-tuple-element.29.refs_1_, ...), custom_call_target="tpu_custom_call" | custom-call | flops 1 | bytes 1 | tf_op jit(solution)/shard_map/pallas_call | solution.py:59
  28.1 0.1 collective-permute-start.7
  28.2 2.6 %collective-permute-done.7.refs_1_ = bf16[1,16,4,64,128]{4,3,2,1,0:T(8,128)(2,1)S(1)} collective-permute-done((bf16[1,16,4,64,128]{4,3,2,1,0:T(8,128)(2,1)S(1)}, bf16[1,16,4,64,128]{4,3,2,1,0:T(8,128)(2,1)S(1)}, u32[]{:S(2)}, u32[]{:S(2)}) %collective-permute-start.7) | collective-permute-done | bytes 1048608 | tf_op jit(solution)/shard_map/ppermute | solution.py:354
  30.8 0.7 %shard_map.46.refs_3_ = bf16[16,4,2,32,128]{4,3,2,1,0:T(8,128)(2,1)} custom-call(s32[16]{0:T(128)S(4)} %get-tuple-element.21.order_ref, bf16[1,16,4,64,128]{4,3,2,1,0:T(8,128)(2,1)S(1)} %get-tuple-element.33.refs_0_, bf16[1,16,4,64,128]{4,3,2,1,0:T(8,128)(2,1)S(1)} %collective-permute-done.7.refs_1_, ...), custom_call_target="tpu_custom_call" | custom-call | flops 1 | bytes 1 | tf_op jit(solution)/shard_map/pallas_call | solution.py:59
  31.5 0.8 %shard_map.47.refs_3_ = bf16[16,4,2,32,128]{4,3,2,1,0:T(8,128)(2,1)} custom-call(s32[16]{0:T(128)S(4)} %get-tuple-element.21.order_ref, bf16[1,16,4,64,128]{4,3,2,1,0:T(8,128)(2,1)S(1)} %get-tuple-element.33.refs_0_, bf16[1,16,4,64,128]{4,3,2,1,0:T(8,128)(2,1)S(1)} %collective-permute-done.7.refs_1_, ...), custom_call_target="tpu_custom_call", output_to_operand_aliasing={{}: (4, {})} | custom-call | flops 1 | bytes 1 | tf_op jit(solution)/shard_map/pallas_call | solution.py:59
  32.4 5.5 %collective-permute-done.8.refs_2_ = bf16[8,4,64,128]{3,2,1,0:T(8,128)(2,1)S(1)} collective-permute-done((bf16[8,4,64,128]{3,2,1,0:T(8,128)(2,1)S(1)}, bf16[8,4,64,128]{3,2,1,0:T(8,128)(2,1)S(1)}, u32[]{:S(2)}, u32[]{:S(2)}) %collective-permute-start.8) | collective-permute-done | bytes 524320 | tf_op jit(solution)/shard_map/ppermute | solution.py:54
  37.9 0.9 %shard_map.48 = bf16[16,4,2,32,128]{4,3,2,1,0:T(8,128)(2,1)} custom-call(s32[16]{0:T(128)S(4)} %get-tuple-element.21.order_ref, bf16[1,16,4,64,128]{4,3,2,1,0:T(8,128)(2,1)S(1)} %get-tuple-element.33.refs_0_, bf16[1,16,4,64,128]{4,3,2,1,0:T(8,128)(2,1)S(1)} %collective-permute-done.7.refs_1_, ...), custom_call_target="tpu_custom_call", output_to_operand_aliasing={{}: (4, {})} | custom-call | flops 1 | bytes 1 | tf_op jit(solution)/shard_map/pallas_call | solution.py:59
  (7 shorter events, 0.1 us)
Async XLA Ops:
  0.0 9.6 %collective-permute-start = (bf16[2,192,128]{2,1,0:T(8,128)(2,1)}, bf16[2,192,128]{2,1,0:T(8,128)(2,1)S(1)}, u32[]{:S(2)}, u32[]{:S(2)}) collective-permute-start(bf16[2,192,128]{2,1,0:T(8,128)(2,1)} %bitcast.11), channel_id=1, source_target_pairs={{0,4},{4,0},{8,12},{12,8},{1,5},{5,1},{9,13},{13,9},{2,6},{6,2},{1... | collective-permute-start | bytes 294920 | tf_op jit(solution)/shard_map/ppermute | solution.py:49
  4.0 5.6 %collective-permute-start.1 = (bf16[1,64,384]{2,1,0:T(8,128)(2,1)S(1)}, bf16[1,64,384]{2,1,0:T(8,128)(2,1)S(1)}, u32[]{:S(2)}, u32[]{:S(2)}) collective-permute-start(bf16[1,64,384]{2,1,0:T(8,128)(2,1)S(1)} %get-tuple-element.25.refs_0_), channel_id=1, source_target_pairs={{0,8},{4,12},{8,0},{12,4},{1,9},{5,13},{9,1},{13,5},{2,10},{6,14},... | collective-permute-start | bytes 147464 | tf_op jit(solution)/shard_map/ppermute | solution.py:49
  10.6 3.6 %collective-permute-start.2 = (bf16[1,6,4,64,128]{4,3,2,1,0:T(8,128)(2,1)S(1)}, bf16[1,6,4,64,128]{4,3,2,1,0:T(8,128)(2,1)S(1)}, u32[]{:S(2)}, u32[]{:S(2)}) collective-permute-start(bf16[1,6,4,64,128]{4,3,2,1,0:T(8,128)(2,1)S(1)} %get-tuple-element.28), channel_id=1, source_target_pairs={{0,1},{1,0},{2,3},{3,2},{4,5},{5,4},{6,7},{7,6},{8,9},{9,8},{10,11... | collective-permute-start | bytes 1179656 | tf_op jit(solution)/shard_map/ppermute | solution.py:336
  10.7 1.9 %collective-permute-start.10 = (bf16[1,2,4,64,128]{4,3,2,1,0:T(8,128)(2,1)S(1)}, bf16[1,2,4,64,128]{4,3,2,1,0:T(8,128)(2,1)S(1)}, u32[]{:S(2)}, u32[]{:S(2)}) collective-permute-start(bf16[1,2,4,64,128]{4,3,2,1,0:T(8,128)(2,1)S(1)} %get-tuple-element.36), channel_id=1, source_target_pairs={{0,1},{1,0},{2,3},{3,2},{4,5},{5,4},{6,7},{7,6},{8,9},{9,8},{10,11... | collective-permute-start | bytes 393224 | tf_op jit(solution)/shard_map/ppermute | solution.py:336
  11.2 4.1 %collective-permute-start.5 = (bf16[1,64,384]{2,1,0:T(8,128)(2,1)S(1)}, bf16[1,64,384]{2,1,0:T(8,128)(2,1)S(1)}, u32[]{:S(2)}, u32[]{:S(2)}) collective-permute-start(bf16[1,64,384]{2,1,0:T(8,128)(2,1)S(1)} %collective-permute-done.1.refs_2_), channel_id=1, source_target_pairs={{0,4},{4,0},{8,12},{12,8},{1,5},{5,1},{9,13},{13,9},{2,6},{6,2},{1... | collective-permute-start | bytes 147464 | tf_op jit(solution)/shard_map/ppermute | solution.py:49
  12.6 6.4 %collective-permute-start.11 = (bf16[2,4,64,128]{3,2,1,0:T(8,128)(2,1)S(1)}, bf16[2,4,64,128]{3,2,1,0:T(8,128)(2,1)S(1)}, u32[]{:S(2)}, u32[]{:S(2)}) collective-permute-start(bf16[2,4,64,128]{3,2,1,0:T(8,128)(2,1)S(1)} %fusion.2), channel_id=1, source_target_pairs={{0,2},{1,3},{2,0},{3,1},{4,6},{5,7},{6,4},{7,5},{8,10},{9,11},{10,... | collective-permute-start | bytes 393224 | tf_op jit(solution)/shard_map/ppermute | solution.py:54
  14.3 13.9 %collective-permute-start.9 = (bf16[6,4,64,128]{3,2,1,0:T(8,128)(2,1)S(1)}, bf16[6,4,64,128]{3,2,1,0:T(8,128)(2,1)S(1)}, u32[]{:S(2)}, u32[]{:S(2)}) collective-permute-start(bf16[6,4,64,128]{3,2,1,0:T(8,128)(2,1)S(1)} %fusion.1._.refs_3_), channel_id=1, source_target_pairs={{0,2},{1,3},{2,0},{3,1},{4,6},{5,7},{6,4},{7,5},{8,10},{9,11},{10,... | collective-permute-start | bytes 1179656 | tf_op jit(solution)/shard_map/ppermute | solution.py:54
  18.2 2.9 %collective-permute-start.6 = (bf16[1,8,4,64,128]{4,3,2,1,0:T(8,128)(2,1)S(1)}, bf16[1,8,4,64,128]{4,3,2,1,0:T(8,128)(2,1)S(1)}, u32[]{:S(2)}, u32[]{:S(2)}) collective-permute-start(bf16[1,8,4,64,128]{4,3,2,1,0:T(8,128)(2,1)S(1)} %get-tuple-element.32), channel_id=1, source_target_pairs={{0,1},{1,0},{2,3},{3,2},{4,5},{5,4},{6,7},{7,6},{8,9},{9,8},{10,11... | collective-permute-start | bytes 1572872 | tf_op jit(solution)/shard_map/ppermute | solution.py:336
  19.0 6.3 %collective-permute-start.4 = (bf16[64,384]{1,0:T(8,128)(2,1)S(1)}, bf16[64,384]{1,0:T(8,128)(2,1)S(1)}, u32[]{:S(2)}, u32[]{:S(2)}) collective-permute-start(bf16[64,384]{1,0:T(8,128)(2,1)S(1)} %shard_map.41.refs_0_), channel_id=1, source_target_pairs={{0,12},{4,8},{8,4},{12,0},{1,13},{5,9},{9,5},{13,1},{2,14},{6,10},... | collective-permute-start | bytes 147464 | tf_op jit(solution)/shard_map/ppermute | solution.py:49
  21.2 5.6 %collective-permute-start.3 = (bf16[64,384]{1,0:T(8,128)(2,1)S(1)}, bf16[64,384]{1,0:T(8,128)(2,1)S(1)}, u32[]{:S(2)}, u32[]{:S(2)}) collective-permute-start(bf16[64,384]{1,0:T(8,128)(2,1)S(1)} %shard_map.41.refs_0_), channel_id=1, source_target_pairs={{0,8},{4,12},{8,0},{12,4},{1,9},{5,13},{9,1},{13,5},{2,10},{6,14},... | collective-permute-start | bytes 147464 | tf_op jit(solution)/shard_map/ppermute | solution.py:49
  21.4 16.5 %collective-permute-start.8 = (bf16[8,4,64,128]{3,2,1,0:T(8,128)(2,1)S(1)}, bf16[8,4,64,128]{3,2,1,0:T(8,128)(2,1)S(1)}, u32[]{:S(2)}, u32[]{:S(2)}) collective-permute-start(bf16[8,4,64,128]{3,2,1,0:T(8,128)(2,1)S(1)} %fusion.refs_6_), channel_id=1, source_target_pairs={{0,2},{1,3},{2,0},{3,1},{4,6},{5,7},{6,4},{7,5},{8,10},{9,11},{10,... | collective-permute-start | bytes 1572872 | tf_op jit(solution)/shard_map/ppermute | solution.py:54
  28.1 2.7 %collective-permute-start.7 = (bf16[1,16,4,64,128]{4,3,2,1,0:T(8,128)(2,1)S(1)}, bf16[1,16,4,64,128]{4,3,2,1,0:T(8,128)(2,1)S(1)}, u32[]{:S(2)}, u32[]{:S(2)}) collective-permute-start(bf16[1,16,4,64,128]{4,3,2,1,0:T(8,128)(2,1)S(1)} %get-tuple-element.34), channel_id=1, source_target_pairs={{0,1},{1,0},{2,3},{3,2},{4,5},{5,4},{6,7},{7,6},{8,9},{9,8},{10,11... | collective-permute-start | bytes 3145736 | tf_op jit(solution)/shard_map/ppermute | solution.py:354
